TPU v7x, 512 devices: a whole 4x4x16 slice. The times are simulated.
512 devices in a mesh: seg: 64 (over x_hi, z, core), op: 8 (over y, x_lo).
Axes of the slice: x: 4 (x_hi: 2, x_lo: 2; x = x_hi * 2 + x_lo), y: 4, z: 16, core: 2. Of those that a mesh axis runs over, the one named last changes fastest.
Arguments:
- left_in: bfloat16 [64, 8, 24, 128, 128], P('seg', 'op'), may hold values from -6 to 6
- right_in: bfloat16 [64, 8, 24, 128, 128], P('seg', 'op'), may hold values from -6 to 6
- site_blocks: bfloat16 [128, 96, 128, 128], P('seg', 'op'), may hold values from -0.5 to 0.5
- sectors: int32 [128, 96, 2], P('seg'), may hold values from 0 to 23, as said below
- site_operator: float32 [128, 8, 96], P('seg', 'op'), may hold values from 0.4 to 1.2
- sector_sizes: int32 [24], replicated, may hold values from 32 to 128, as said below
Outputs:
- left_env: bfloat16 [64, 8, 24, 128, 128], P('seg', 'op')
- right_env: bfloat16 [64, 8, 24, 128, 128], P('seg', 'op')
- left_sum: float32 [64, 24, 128, 128], P('seg', 'op')
- right_sum: float32 [64, 24, 128, 128], P('seg', 'op')
Inputs may be any that keep to these rules, and one draw needn't show every extreme that they name: `sectors`: in every site each sector is the left sector of exactly four blocks and the right sector of exactly four blocks. `sector_sizes`: some sector has all 128 rows live.
All inputs are finite; a program needn't handle non-finite values.
Results may differ from a plain program's by a relative error of at most 0.015.
Values may be sent and summed in bfloat16 or wider, within the bound.
No kernel may reach another device: no remote copies, remote signals or barrier semaphores. Data moves between devices by JAX's collectives and lax.ppermute only.
A program may use at most 64 MiB of HBM per device.

v0:
```python
import jax
import jax.numpy as jnp
from jax import lax
from jax.sharding import PartitionSpec as P


def passed_along(block, axis, distance):
    devices = range(lax.axis_size(axis))
    route = [(i - distance, i) for i in devices if i - distance in devices]
    return lax.ppermute(block, axis, route)


def sector_mask(sector_sizes, block_width):
    live = (
        lax.broadcasted_iota(jnp.int32, (sector_sizes.shape[0], block_width), 1)
        < sector_sizes[:, None]
    )
    return live[:, :, None] & live[:, None, :]


def finish(total, live_mask):
    return jnp.where(live_mask, total, 0.0).astype(jnp.bfloat16)


def left_grouped(environ, blocks, scaled, source, num_sectors):
    chosen = jnp.take(environ, source, axis=0)
    halfway = jnp.einsum("kab,kbc->kac", chosen, blocks, preferred_element_type=jnp.float32).astype(
        jnp.bfloat16
    )
    per_sector = blocks.shape[0] // num_sectors
    width = blocks.shape[1]
    grouped_scaled = scaled.reshape(num_sectors, per_sector, width, width)
    grouped_half = halfway.reshape(num_sectors, per_sector, width, width)
    return jnp.einsum(
        "tkai,tkac->tic", grouped_scaled, grouped_half, preferred_element_type=jnp.float32
    )


def right_grouped(environ, blocks, scaled, target, num_sectors):
    chosen = jnp.take(environ, target, axis=0)
    halfway = jnp.einsum("kab,kbc->kac", blocks, chosen, preferred_element_type=jnp.float32).astype(
        jnp.bfloat16
    )
    per_sector = blocks.shape[0] // num_sectors
    width = blocks.shape[1]
    grouped_scaled = scaled.reshape(num_sectors, per_sector, width, width)
    grouped_half = halfway.reshape(num_sectors, per_sector, width, width)
    return jnp.einsum(
        "skac,skdc->sad", grouped_half, grouped_scaled, preferred_element_type=jnp.float32
    )


def scale_rows(blocks, weights):
    return (blocks.astype(jnp.float32) * weights[:, None, None]).astype(jnp.bfloat16)


def prepare(gathered, source, target, weights):
    prepared = []
    for site in range(2):
        by_target = jnp.argsort(target[site], stable=True)
        by_source = jnp.argsort(source[site], stable=True)
        target_blocks = jnp.take(gathered[site], by_target, axis=0)
        source_blocks = jnp.take(gathered[site], by_source, axis=0)
        prepared.append(
            (
                target_blocks,
                jnp.take(source[site], by_target),
                scale_rows(target_blocks, jnp.take(weights[site], by_target)),
                source_blocks,
                jnp.take(target[site], by_source),
                scale_rows(source_blocks, jnp.take(weights[site], by_source)),
            )
        )
    return prepared


def extend_left(environ, prepared_site, num_sectors, live_mask):
    return finish(
        left_grouped(environ, prepared_site[0], prepared_site[2], prepared_site[1], num_sectors),
        live_mask,
    )


def extend_right(environ, prepared_site, num_sectors, live_mask):
    return finish(
        right_grouped(environ, prepared_site[3], prepared_site[5], prepared_site[4], num_sectors),
        live_mask,
    )


def local(left_in, right_in, site_blocks, sectors, site_operator, sector_sizes):
    num_sectors = left_in.shape[2]
    block_width = left_in.shape[3]
    live_mask = sector_mask(sector_sizes, block_width)
    left_edge = finish(left_in[0, 0].astype(jnp.float32), live_mask)
    right_edge = finish(right_in[0, 0].astype(jnp.float32), live_mask)
    position = lax.axis_index("seg")
    last_index = lax.axis_size("seg") - 1
    source = sectors[:, :, 0]
    target = sectors[:, :, 1]
    weights = site_operator[:, 0, :]
    gathered = lax.all_gather(site_blocks, "op", axis=1, tiled=True)
    prepared = prepare(gathered, source, target, weights)
    state_left = left_edge
    state_right = right_edge
    arrived_left = passed_along(state_left, "seg", 1)
    arrived_right = passed_along(state_right, "seg", -1)
    incoming_left = jnp.where(position == 0, left_edge, arrived_left)
    incoming_right = jnp.where(position == last_index, right_edge, arrived_right)
    inner_left = extend_left(incoming_left, prepared[0], num_sectors, live_mask)
    inner_right = extend_right(incoming_right, prepared[1], num_sectors, live_mask)
    state_left = extend_left(inner_left, prepared[1], num_sectors, live_mask)
    state_right = extend_right(inner_right, prepared[0], num_sectors, live_mask)
    left_summed, right_summed = (
        lax.psum_scatter(
            state_left.astype(jnp.float32).astype(jnp.bfloat16),
            "op",
            scatter_dimension=0,
            tiled=True,
        ).astype(jnp.float32),
        lax.psum_scatter(
            state_right.astype(jnp.float32).astype(jnp.bfloat16),
            "op",
            scatter_dimension=0,
            tiled=True,
        ).astype(jnp.float32),
    )
    return (state_left[None, None], state_right[None, None], left_summed[None], right_summed[None])


def solution(mesh):
    placed = (
        P("seg", "op", None, None, None),
        P("seg", "op", None, None, None),
        P("seg", "op", None, None),
        P("seg", None, None),
        P("seg", "op", None),
        P(),
    )
    return jax.shard_map(
        local,
        mesh=mesh,
        in_specs=placed,
        out_specs=(
            P("seg", "op", None, None, None),
            P("seg", "op", None, None, None),
            P("seg", "op", None, None),
            P("seg", "op", None, None),
        ),
        check_vma=False,
    )
```

profile of v0, /device:TPU:32, one launch (start us, length us, event | category | flops | bytes accessed | tf_op | source)
XLA Modules:
  0.0 294.1 jit_solution(18172648013989718393)
XLA Ops:
  7.2 0.7 all-gather.2.cloned.1.call-update
  8.0 0.7 iota_compare_fusion
  8.7 1.8 fusion.27
  10.5 1.9 collective-permute-start.1
  12.5 2.4 collective-permute-start
  14.9 2.5 sort.62
  17.5 1.2 gather_fusion.12
  18.7 1.2 gather_fusion.10
  20.0 2.5 sort.61
  22.5 1.2 gather_fusion.15
  23.7 1.2 gather_fusion.13
  25.0 2.5 sort.60
  27.5 1.2 gather_fusion.4
  28.8 2.5 sort.59
  31.4 1.2 gather_fusion.6
  32.7 1.2 gather_fusion.3
  34.0 1.2 gather_fusion.1
  35.2 1.2 broadcast_select_fusion.8
  36.5 2.7 gather_fusion.11
  39.2 2.8 gather_fusion.5
  42.0 110.1 %all-gather.2.cloned.1.call-done = bf16[2,96,128,128]{3,2,1,0:T(8,128)(2,1)} async-done(((bf16[2,12,128,128]{3,2,1,0:T(8,128)(2,1)}), bf16[2,96,128,128]{3,2,1,0:T(8,128)(2,1)}) %all-gather.2.cloned.1.call-update) | async-done | bytes 6291472 | tf_op jit(solution)/shard_map/all_gather | solution.py:102
  152.1 6.5 %slice_bitcast_fusion = (bf16[96,128,128]{2,1,0:T(8,128)(2,1)}, bf16[96,128,128]{2,1,0:T(8,128)(2,1)S(1)}) fusion(bf16[2,96,128,128]{3,2,1,0:T(8,128)(2,1)} %all-gather.2.cloned.1.call-done), kind=kLoop, calls=%fused_computation.26 | loop fusion | bytes 12582912 | tf_op jit(solution)/shard_map/squeeze | solution.py:62
  158.7 4.6 %gather_fusion.8 = bf16[96,128,128]{2,1,0:T(8,128)(2,1)} fusion(bf16[96,128,128]{2,1,0:T(8,128)(2,1)} %get-tuple-element.30, s32[1024]{0:T(1024)S(1)} %pad_clamp_fusion.3), kind=kCustom, calls=%fused_computation.5.clone | custom fusion | bytes 6291840 | tf_op jit(solution)/shard_map/jit(_take)/gather | solution.py:63
  163.3 4.6 %gather_fusion.2 = bf16[96,128,128]{2,1,0:T(8,128)(2,1)} fusion(bf16[96,128,128]{2,1,0:T(8,128)(2,1)} %get-tuple-element.30, s32[1024]{0:T(1024)S(1)} %pad_clamp_fusion.6), kind=kCustom, calls=%fused_computation.4.clone | custom fusion | bytes 6291840 | tf_op jit(solution)/shard_map/jit(_take)/gather | solution.py:62
  167.9 2.7 gather_fusion.9
  170.6 2.9 %multiply_convert_fusion.1 = bf16[96,128,128]{2,1,0:T(8,128)(2,1)S(1)} fusion(f32[96]{0:T(128)S(1)} %get-tuple-element.20, bf16[96,128,128]{2,1,0:T(8,128)(2,1)} %gather_fusion.9, pred[96]{0:T(512)(128)(4,1)S(1)} %get-tuple-element.21), kind=kLoop, calls=%fused_computation.17 | loop fusion | flops 6291456 | bytes 6291936 | tf_op jit(solution)/shard_map/convert_element_type | solution.py:54
  173.6 0.8 copy-done.5
  174.4 1.3 fusion.18
  175.8 1.9 fusion.28
  177.7 3.8 %gather_fusion.14 = bf16[96,128,128]{2,1,0:T(8,128)(2,1)} fusion(bf16[24,128,128]{2,1,0:T(8,128)(2,1)} %fusion.28, s32[1024]{0:T(1024)S(1)} %pad_clamp_fusion), kind=kCustom, calls=%fused_computation.15.clone | custom fusion | bytes 6291840 | tf_op jit(solution)/shard_map/jit(_take)/gather | solution.py:40
  181.5 2.9 %multiply_convert_fusion = bf16[96,128,128]{2,1,0:T(8,128)(2,1)S(1)} fusion(f32[96]{0:T(128)S(1)} %get-tuple-element.16, bf16[96,128,128]{2,1,0:T(8,128)(2,1)} %gather_fusion.8, pred[96]{0:T(512)(128)(4,1)S(1)} %get-tuple-element.17), kind=kLoop, calls=%fused_computation.16 | loop fusion | flops 6291456 | bytes 6291936 | tf_op jit(solution)/shard_map/convert_element_type | solution.py:54
  184.5 0.8 copy-done.6
  185.3 1.3 fusion.21
  186.6 2.0 fusion.29
  188.7 2.9 %multiply_convert_fusion.2 = bf16[96,128,128]{2,1,0:T(8,128)(2,1)S(1)} fusion(f32[96]{0:T(128)S(1)} %broadcast_select_fusion.12, bf16[96,128,128]{2,1,0:T(8,128)(2,1)} %gather_fusion.2, pred[96]{0:T(512)(128)(4,1)S(1)} %get-tuple-element.29), kind=kLoop, calls=%fused_computation.18 | loop fusion | flops 6291456 | bytes 6291936 | tf_op jit(solution)/shard_map/convert_element_type | solution.py:54
  191.7 0.8 copy-done.4
  192.5 1.3 fusion.12
  193.8 2.3 fusion.25
  196.1 2.7 gather_fusion
  198.8 4.0 %gather_fusion.7 = bf16[96,128,128]{2,1,0:T(8,128)(2,1)} fusion(bf16[24,128,128]{2,1,0:T(8,128)(2,1)} %fusion.25, s32[1024]{0:T(1024)S(1)} %pad_clamp_fusion.4), kind=kCustom, calls=%fused_computation.13.clone | custom fusion | bytes 6291840 | tf_op jit(solution)/shard_map/jit(_take)/gather | solution.py:26
  202.8 0.9 multiply_convert_fusion.3
  203.8 1.0 copy-done.7
  204.7 1.4 fusion.15
  206.1 2.2 fusion.26
  208.4 27.9 %reduce-scatter.5.cloned.1.call-done = bf16[3,128,128]{2,1,0:T(8,128)(2,1)} async-done(((bf16[24,128,128]{2,1,0:T(8,128)(2,1)}), bf16[3,128,128]{2,1,0:T(8,128)(2,1)}) %reduce-scatter.5.cloned.1.call-update) | async-done | bytes 98320 | tf_op jit(solution)/shard_map/reduce_scatter | solution.py:121
  236.3 1.6 bitcast_convert_fusion
  237.8 48.1 %reduce-scatter.3.cloned.1.call-done = bf16[3,128,128]{2,1,0:T(8,128)(2,1)} async-done(((bf16[24,128,128]{2,1,0:T(8,128)(2,1)}), bf16[3,128,128]{2,1,0:T(8,128)(2,1)}) %reduce-scatter.3.cloned.1.call-update) | async-done | bytes 98320 | tf_op jit(solution)/shard_map/reduce_scatter | solution.py:115
  286.0 1.6 bitcast_convert_fusion.1
  (50 shorter events, 0.4 us)
Async XLA Ops:
  7.2 7.7 %copy-start.8 = (s32[2,96,2]{1,2,0:T(2,128)S(1)}, s32[2,96,2]{1,2,0:T(2,128)}, u32[]{:S(2)}) copy-start(s32[2,96,2]{1,2,0:T(2,128)} %param.17) | copy-start | bytes 4612
  7.2 10.3 %copy-start.9 = (f32[2,1,96]{2,1,0:T(1,128)S(1)}, f32[2,1,96]{2,1,0:T(1,128)}, u32[]{:S(2)}) copy-start(f32[2,1,96]{2,1,0:T(1,128)} %param.18) | copy-start | bytes 2308
  7.2 144.9 %all-gather.2.cloned.1.call-start = ((), (), s32[]{:S(2)}) async-start(), calls=%async_computation.2 | async-start | bytes 7077888 | tf_op jit(solution)/shard_map/all_gather | solution.py:102
  7.9 228.3 %reduce-scatter.5.cloned.1.call-start = ((), (), s32[]{:S(2)}) async-start(), calls=%async_computation.4 | async-start | bytes 884736 | tf_op jit(solution)/shard_map/reduce_scatter | solution.py:121
  10.5 24.7 %collective-permute-start.1 = (bf16[24,128,128]{2,1,0:T(8,128)(2,1)S(1)}, bf16[24,128,128]{2,1,0:T(8,128)(2,1)}, u32[]{:S(2)}, u32[]{:S(2)}) collective-permute-start(bf16[24,128,128]{2,1,0:T(8,128)(2,1)S(1)} %get-tuple-element.32), channel_id=1, source_target_pairs={{8,0},{16,8},{24,16},{32,24},{40,32},{48,40},{56,48},{64,56},{72,6... | collective-permute-start | bytes 2359304 | tf_op jit(solution)/shard_map/ppermute | solution.py:10
  12.5 26.7 %collective-permute-start = (bf16[24,128,128]{2,1,0:T(8,128)(2,1)S(1)}, bf16[24,128,128]{2,1,0:T(8,128)(2,1)S(1)}, u32[]{:S(2)}, u32[]{:S(2)}) collective-permute-start(bf16[24,128,128]{2,1,0:T(8,128)(2,1)S(1)} %get-tuple-element.33), channel_id=1, source_target_pairs={{0,8},{8,16},{16,24},{24,32},{32,40},{40,48},{48,56},{56,64},{64,7... | collective-permute-start | bytes 2359304 | tf_op jit(solution)/shard_map/ppermute | solution.py:10
  170.6 3.0 %copy-start.3 = (bf16[96,128,128]{2,1,0:T(8,128)(2,1)S(1)}, bf16[96,128,128]{2,1,0:T(8,128)(2,1)}, u32[]{:S(2)}) copy-start(bf16[96,128,128]{2,1,0:T(8,128)(2,1)} %gather_fusion.9) | copy-start | bytes 9437188
  170.6 3.8 %copy-start.5 = (bf16[96,128,128]{2,1,0:T(8,128)(2,1)S(1)}, bf16[96,128,128]{2,1,0:T(8,128)(2,1)}, u32[]{:S(2)}) copy-start(bf16[96,128,128]{2,1,0:T(8,128)(2,1)} %gather_fusion.11) | copy-start | bytes 9437188
  181.5 3.0 %copy-start.1 = (bf16[96,128,128]{2,1,0:T(8,128)(2,1)S(1)}, bf16[96,128,128]{2,1,0:T(8,128)(2,1)}, u32[]{:S(2)}) copy-start(bf16[96,128,128]{2,1,0:T(8,128)(2,1)} %gather_fusion.8) | copy-start | bytes 9437188
  181.5 3.8 %copy-start.6 = (bf16[96,128,128]{2,1,0:T(8,128)(2,1)S(1)}, bf16[96,128,128]{2,1,0:T(8,128)(2,1)}, u32[]{:S(2)}) copy-start(bf16[96,128,128]{2,1,0:T(8,128)(2,1)} %gather_fusion.14) | copy-start | bytes 9437188
  188.6 97.3 %reduce-scatter.3.cloned.1.call-start = ((), (), s32[]{:S(2)}) async-start(), calls=%async_computation.3 | async-start | bytes 884736 | tf_op jit(solution)/shard_map/reduce_scatter | solution.py:115
  188.7 3.0 %copy-start = (bf16[96,128,128]{2,1,0:T(8,128)(2,1)S(1)}, bf16[96,128,128]{2,1,0:T(8,128)(2,1)}, u32[]{:S(2)}) copy-start(bf16[96,128,128]{2,1,0:T(8,128)(2,1)} %gather_fusion.2) | copy-start | bytes 9437188
  188.7 3.8 %copy-start.4 = (bf16[96,128,128]{2,1,0:T(8,128)(2,1)S(1)}, bf16[96,128,128]{2,1,0:T(8,128)(2,1)}, u32[]{:S(2)}) copy-start(bf16[96,128,128]{2,1,0:T(8,128)(2,1)} %gather_fusion.5) | copy-start | bytes 9437188
  198.8 4.0 %copy-start.2 = (bf16[96,128,128]{2,1,0:T(8,128)(2,1)S(1)}, bf16[96,128,128]{2,1,0:T(8,128)(2,1)}, u32[]{:S(2)}) copy-start(bf16[96,128,128]{2,1,0:T(8,128)(2,1)} %gather_fusion) | copy-start | bytes 9437188
  202.8 1.9 copy-start.7
Sparse Core Ops, SparseCore 0:
  10.1 141.9 all-gather.1
  188.7 47.4 reduce-scatter.4
  239.9 46.0 reduce-scatter.2
where the time goes:
time: 295 us; the launch traced here: 294 us
  waiting for transfers between devices  187 us (63%)
  local copies, waits for them, and re-layouts  47.8 us (16%)
  other arithmetic  27.1 us (9%)
  between operations  14.1 us (5%)
  matrix products  13.8 us (5%)
  starting transfers between devices  4.45 us (2%)
    all_gather x1, waiting for transfers between devices, local(): gathered = lax.all_gather(site_blocks, 'op', axis=1, tiled=True)  110 us
    reduce_scatter x1, waiting for transfers between devices, local(): lax.psum_scatter(state_left.astype(jnp.float32).astype(jnp.bfloat16), 'op...  48.1 us
    reduce_scatter x1, waiting for transfers between devices, local(): lax.psum_scatter(state_right.astype(jnp.float32).astype(jnp.bfloat16), 'o...  27.9 us
    convert_element_type x4, other arithmetic, scale_rows(): (blocks.astype(jnp.float32) * weights[:, None, None]).astype(jnp.bfloat16)  9.75 us
    gather x2, local copies, waits for them, and re-layouts, prepare(): source_blocks = jnp.take(gathered[site], by_source, axis=0)  7.36 us
    gather x2, local copies, waits for them, and re-layouts, prepare(): target_blocks = jnp.take(gathered[site], by_target, axis=0)  7.32 us
    gather x2, local copies, waits for them, and re-layouts, left_grouped(): chosen = jnp.take(environ, source, axis=0)  6.79 us
    squeeze x1, local copies, waits for them, and re-layouts, prepare(): target_blocks = jnp.take(gathered[site], by_target, axis=0)  6.53 us
  transfers between devices with their start and end apart: 5, of which 3 were waited for; matrix products, arithmetic and copies ran while one was open for 17% of the time, Pallas kernels for 0%

commit v1 on v0

v1 whole, which is shorter than its diff:
```python
import jax
import jax.numpy as jnp
from jax import lax
from jax.experimental import pallas as pl
from jax.experimental.pallas import tpu as pltpu
from jax.sharding import PartitionSpec as P

F32 = jnp.float32
BF16 = jnp.bfloat16
VMEM = pl.BlockSpec(memory_space=pltpu.VMEM)
SMEM = pl.BlockSpec(memory_space=pltpu.SMEM)
ANY = pl.BlockSpec(memory_space=pl.ANY)
NY, NX = 4, 2
TERMS = NY * NX
PER_SECTOR = 4
NN = (((1,), (0,)), ((), ()))
TN = (((0,), (0,)), ((), ()))
NT = (((1,), (1,)), ((), ()))
OWN, DOWN, UP, OPP, X_OWN, X_DOWN, X_UP, X_OPP, FIRST_SEG, LAST_SEG = range(10)


def dot(a, b, dims):
    return lax.dot_general(a, b, dims, preferred_element_type=F32)


def op_route(dy, dx):
    return [(o, ((o // NX + dy) % NY) * NX + ((o % NX) ^ dx)) for o in range(TERMS)]


def hop(block, dy, dx):
    return lax.ppermute(block, "op", op_route(dy, dx))


def along_segments(block, distance):
    devices = range(lax.axis_size("seg"))
    route = [(i - distance, i) for i in devices if i - distance in devices]
    return lax.ppermute(block, "seg", route)


def live(sizes, sector, width):
    rows = lax.broadcasted_iota(jnp.int32, (width, width), 0)
    cols = lax.broadcasted_iota(jnp.int32, (width, width), 1)
    return jnp.maximum(rows, cols) < sizes[sector]


def finish(total, sizes, out, extra=None):
    num, width, _ = total.shape

    @pl.loop(0, num, step=4)
    def _(start):
        for t in range(4):
            kept = jnp.where(live(sizes, start + t, width), total[start + t], 0.0).astype(BF16)
            out[start + t] = kept
            if extra is not None:
                extra(start + t, kept)


def group(order, at, sector):
    return [order[at + PER_SECTOR * sector + j] for j in range(PER_SECTOR)]


def stage(count, unroll):
    def run(body):
        @pl.loop(0, count, step=unroll)
        def _(start):
            for u in range(unroll):
                body(start + u)

    return run


def sorted_left(env, blocks, half, total, order, weights, site, unroll):
    num, width, _ = total.shape
    n = num * PER_SECTOR

    @stage(num, unroll)
    def _(s):
        members = group(order, 2 * site * n, s)
        wide = jnp.concatenate([blocks[k] for k in members], axis=1)
        found = dot(env[s], wide, NN)
        for j, k in enumerate(members):
            piece = found[:, j * width : (j + 1) * width]
            half[k] = (piece * weights[site * n + k]).astype(BF16)

    @stage(num, unroll)
    def _(t):
        members = group(order, (2 * site + 1) * n, t)
        a = jnp.concatenate([blocks[k] for k in members], axis=0)
        y = jnp.concatenate([half[k] for k in members], axis=0)
        total[t] = dot(a, y, TN)


def sorted_right(env, blocks, half, total, order, weights, site, unroll):
    num, width, _ = total.shape
    n = num * PER_SECTOR

    @stage(num, unroll)
    def _(t):
        members = group(order, (2 * site + 1) * n, t)
        tall = jnp.concatenate([blocks[k] for k in members], axis=0)
        found = dot(tall, env[t], NN)
        for j, k in enumerate(members):
            piece = found[j * width : (j + 1) * width]
            half[k] = (piece * weights[site * n + k]).astype(BF16)

    @stage(num, unroll)
    def _(s):
        members = group(order, 2 * site * n, s)
        a = jnp.concatenate([blocks[k] for k in members], axis=1)
        z = jnp.concatenate([half[k] for k in members], axis=1)
        total[s] = dot(z, a, NT)


def add_left(env, total, blocks, sectors, weights, site, first, count, n):
    found = []
    for j in range(count):
        k = site * n + first + j
        block = blocks[j]
        half = (dot(env[sectors[2 * k]], block, NN) * weights[k]).astype(BF16)
        found.append((sectors[2 * k + 1], dot(block, half, TN)))
    for place, value in found:
        total[place] += value


def add_right(env, total, blocks, sectors, weights, site, first, count, n):
    found = []
    for j in range(count):
        k = site * n + first + j
        block = blocks[j]
        half = (dot(block, env[sectors[2 * k + 1]], NN) * weights[k]).astype(BF16)
        found.append((sectors[2 * k], dot(half, block, NT)))
    for place, value in found:
        total[place] += value


def call(body, outs, ins, scratch=(), flops=0):
    return pl.pallas_call(
        body,
        out_shape=[shape for _, shape in outs],
        in_specs=[spec for spec, _ in ins],
        out_specs=[spec for spec, _ in outs],
        scratch_shapes=list(scratch),
        compiler_params=pltpu.CompilerParams(vmem_limit_bytes=24 * 1024 * 1024),
        cost_estimate=pl.CostEstimate(flops=flops, bytes_accessed=6000000, transcendentals=0),
    )(*[array for _, array in ins])


def local(left_in, right_in, site_blocks, sectors, site_operator, sector_sizes):
    num, width = left_in.shape[2], left_in.shape[3]
    n = sectors.shape[1]
    share = n // TERMS
    per = num // TERMS
    env = jax.ShapeDtypeStruct((num, width, width), BF16)
    total = jax.ShapeDtypeStruct((num, width, width), F32)
    site_shape = jax.ShapeDtypeStruct((share, width, width), BF16)
    site_scratch = pltpu.VMEM((n, width, width), BF16)
    left_own, right_own = left_in[0, 0], right_in[0, 0]
    me = lax.axis_index("op")
    my_y, my_x = me // NX, me % NX
    seg = lax.axis_index("seg")
    shards = [((my_y + dy) % NY) * NX + (my_x ^ dx) for dx in (0, 1) for dy in (0, 3, 1, 2)]
    meta = jnp.stack(
        shards + [(seg == 0).astype(jnp.int32), (seg == lax.axis_size("seg") - 1).astype(jnp.int32)]
    )
    sec = sectors.reshape(-1)
    wts = site_operator.reshape(-1)

    own = site_blocks
    b_x = hop(own, 0, 1)
    down = hop(own, 1, 0)
    up = hop(own, -1, 0)
    left_arrived = along_segments(left_own, 1)
    right_arrived = along_segments(right_own, -1)
    x_down = hop(down, 0, 1)
    x_up = hop(b_x, -1, 0)
    opp = hop(down, 1, 0)

    def prepare(sec, sizes, meta, lo, la, ro, ra, le, re, order, count):
        @pl.loop(0, num)
        def _(t):
            alive = live(sizes, t, width)
            from_left = jnp.where(meta[FIRST_SEG] == 1, lo[t], la[t])
            from_right = jnp.where(meta[LAST_SEG] == 1, ro[t], ra[t])
            le[t] = jnp.where(alive, from_left.astype(F32), 0.0).astype(BF16)
            re[t] = jnp.where(alive, from_right.astype(F32), 0.0).astype(BF16)
            for table in range(4):
                count[table * num + t] = 0

        @pl.loop(0, n)
        def _(k):
            for table in range(4):
                site, side = table // 2, table % 2
                sector = sec[2 * (site * n + k) + side]
                seen = count[table * num + sector]
                order[table * n + PER_SECTOR * sector + seen] = k
                count[table * num + sector] = seen + 1

    le, re, order = call(
        prepare,
        [(VMEM, env), (VMEM, env), (SMEM, jax.ShapeDtypeStruct((4 * n,), jnp.int32))],
        [(SMEM, sec), (SMEM, sector_sizes), (SMEM, meta)]
        + [(VMEM, a) for a in (left_own, left_arrived, right_own, right_arrived)],
        scratch=[pltpu.SMEM((4 * num,), jnp.int32)],
    )

    def near(sec, wts, meta, le, re, own, down, up, b_x, lt, rt, token):
        @pl.loop(0, num, step=4)
        def _(t):
            for u in range(4):
                lt[t + u] = jnp.zeros((width, width), F32)
                rt[t + u] = jnp.zeros((width, width), F32)

        for ref, slot in ((own, OWN), (down, DOWN), (up, UP), (b_x, X_OWN)):
            first = meta[slot] * share
            add_left(le, lt, ref.at[0], sec, wts, 0, first, share, n)
            add_right(re, rt, ref.at[1], sec, wts, 1, first, share, n)
        token[0] = 0

    lt, rt, token = call(
        near,
        [(VMEM, total), (VMEM, total), (SMEM, jax.ShapeDtypeStruct((1,), jnp.int32))],
        [(SMEM, sec), (SMEM, wts), (SMEM, meta)]
        + [(VMEM, a) for a in (le, re, own, down, up, b_x)],
        flops=2 * 48 * 4 * 128**3,
    )

    def pick(token, x_down, x_up, out0, out1, sems):
        copies = [
            pltpu.make_async_copy(x_down.at[0], out0, sems.at[0]),
            pltpu.make_async_copy(x_up.at[1], out1, sems.at[1]),
        ]
        for copy in copies:
            copy.start()
        for copy in copies:
            copy.wait()

    send0, send1 = call(
        pick,
        [(ANY, site_shape), (ANY, site_shape)],
        [(SMEM, token), (ANY, x_down), (ANY, x_up)],
        scratch=[pltpu.SemaphoreType.DMA((2,))],
    )
    x_opp0 = hop(send0, 1, 0)
    x_opp1 = hop(send1, -1, 0)

    def further(sec, wts, meta, le, re, lt_in, rt_in, opp, x_down, x_up, lt, rt):
        @pl.loop(0, num, step=4)
        def _(t):
            for u in range(4):
                lt[t + u] = lt_in[t + u]
                rt[t + u] = rt_in[t + u]

        for ref, slot in ((x_down, X_DOWN), (x_up, X_UP), (opp, OPP)):
            first = meta[slot] * share
            add_left(le, lt, ref.at[0], sec, wts, 0, first, share, n)
            add_right(re, rt, ref.at[1], sec, wts, 1, first, share, n)

    lt, rt = call(
        further,
        [(VMEM, total), (VMEM, total)],
        [(SMEM, sec), (SMEM, wts), (SMEM, meta)]
        + [(VMEM, a) for a in (le, re, lt, rt, opp, x_down, x_up)],
        flops=2 * 36 * 4 * 128**3,
    )

    slots = (OWN, DOWN, UP, X_OWN, X_DOWN, X_UP, OPP)
    known = (own, down, up, b_x, x_down, x_up, opp)

    def last(sec, order, wts, sizes, meta, le, re, lt_in, rt_in, late0, late1, *rest):
        known, rest = rest[:7], rest[7:]
        left_out, right_out, both, lt, rt, le2, re2, done_left, done_right = rest[:9]
        blocks0, blocks1, half, sems, out_sems = rest[9:]
        copies = []
        for site, late, blocks in ((1, late1, blocks1), (0, late0, blocks0)):
            for i, slot in enumerate(slots + (X_OPP,)):
                source = late if slot == X_OPP else known[i].at[site]
                first = pl.multiple_of(meta[slot] * share, share)
                copies.append(
                    pltpu.make_async_copy(
                        source, blocks.at[pl.ds(first, share)], sems.at[site * TERMS + i]
                    )
                )
        for copy in copies:
            copy.start()

        @pl.loop(0, num, step=4)
        def _(t):
            for u in range(4):
                lt[t + u] = lt_in[t + u]
                rt[t + u] = rt_in[t + u]

        first = meta[X_OPP] * share
        add_left(le, lt, late0, sec, wts, 0, first, share, n)
        finish(lt, sizes, le2)
        add_right(re, rt, late1, sec, wts, 1, first, share, n)
        finish(rt, sizes, re2)
        for copy in copies[:TERMS]:
            copy.wait()
        sorted_left(le2, blocks1, half, lt, order, wts, 1, 12)

        def send_out(done, out, at):
            parts = [
                pltpu.make_async_copy(done, out, out_sems.at[2 * at]),
                pltpu.make_async_copy(
                    done.reshape(TERMS, per, width, width),
                    both.at[:, pl.ds(at * per, per)],
                    out_sems.at[2 * at + 1],
                ),
            ]
            for part in parts:
                part.start()
            return parts

        finish(lt, sizes, done_left)
        sent = send_out(done_left, left_out, 0)
        for copy in copies[TERMS:]:
            copy.wait()
        sorted_right(re2, blocks0, half, rt, order, wts, 0, 12)
        finish(rt, sizes, done_right)
        sent += send_out(done_right, right_out, 1)
        for part in sent:
            part.wait()

    packed = jax.ShapeDtypeStruct((TERMS, 2 * per, width, width), BF16)
    left_state, right_state, both = call(
        last,
        [(ANY, env), (ANY, env), (ANY, packed)],
        [(SMEM, sec), (SMEM, order), (SMEM, wts), (SMEM, sector_sizes), (SMEM, meta)]
        + [(VMEM, a) for a in (le, re, lt, rt, x_opp0, x_opp1)]
        + [(ANY, a) for a in known],
        scratch=[pltpu.VMEM(total.shape, F32)] * 2
        + [pltpu.VMEM(env.shape, BF16)] * 4
        + [site_scratch] * 3
        + [pltpu.SemaphoreType.DMA((2 * TERMS,)), pltpu.SemaphoreType.DMA((4,))],
        flops=2 * 204 * 2 * 128**3,
    )
    parts = lax.all_to_all(both, "op", 0, 0, tiled=True)

    def sum_terms(parts, left_sum, right_sum):
        for t in range(per):
            for out, at in ((left_sum, t), (right_sum, per + t)):
                value = parts[0, at].astype(F32)
                for term in range(1, TERMS):
                    value += parts[term, at].astype(F32)
                out[t] = value

    part = jax.ShapeDtypeStruct((per, width, width), F32)
    left_sum, right_sum = call(sum_terms, [(VMEM, part), (VMEM, part)], [(VMEM, parts)])
    return left_state[None, None], right_state[None, None], left_sum[None], right_sum[None]


def solution(mesh):
    placed = (
        P("seg", "op", None, None, None),
        P("seg", "op", None, None, None),
        P("seg", "op", None, None),
        P("seg", None, None),
        P("seg", "op", None),
        P(),
    )
    return jax.shard_map(
        local,
        mesh=mesh,
        in_specs=placed,
        out_specs=(
            P("seg", "op", None, None, None),
            P("seg", "op", None, None, None),
            P("seg", "op", None, None),
            P("seg", "op", None, None),
        ),
        check_vma=False,
    )
```

time: 295 us -> 111 us (0.38)
  the two profiles are of different devices: /device:TPU:32 before, /device:TPU:484 now
where the time goes in v1:
time: 111 us; the launch traced here: 110 us
  starting transfers between devices  32.7 us (29%)
  Pallas kernels  28.8 us (26%)
  blocking collectives  23.9 us (22%)
  waiting for transfers between devices  16 us (14%)
  local copies, waits for them, and re-layouts  6.66 us (6%)
  other arithmetic  1.33 us (1%)
    pallas_call x6, Pallas kernels, call(): pl.pallas_call(body, out_shape=[shape for _, shape in outs], in_specs=[sp...  28.8 us
    ppermute x8, starting transfers between devices, hop(): return lax.ppermute(block, 'op', op_route(dy, dx))  27.1 us
    all_to_all x1, blocking collectives, local(): parts = lax.all_to_all(both, 'op', 0, 0, tiled=True)  23.9 us
    ppermute x8, waiting for transfers between devices, hop(): return lax.ppermute(block, 'op', op_route(dy, dx))  16 us
    unnamed x16, local copies, waits for them, and re-layouts  6.34 us
    ppermute x2, starting transfers between devices, along_segments(): return lax.ppermute(block, 'seg', route)  5.57 us
  transfers between devices with their start and end apart: 10, of which 3 were waited for; matrix products, arithmetic and copies ran while one was open for 3% of the time, Pallas kernels for 15%

profile of v1, /device:TPU:484, one launch (start us, length us, event | category | flops | bytes accessed | tf_op | source)
XLA Modules:
  0.0 110.5 jit_solution(756093240567997327)
XLA Ops:
  0.6 3.1 %collective-permute-start.4 = (bf16[2,12,128,128]{3,2,1,0:T(8,128)(2,1)}, bf16[2,12,128,128]{3,2,1,0:T(8,128)(2,1)S(1)}, u32[]{:S(2)}, u32[]{:S(2)}) collective-permute-start(bf16[2,12,128,128]{3,2,1,0:T(8,128)(2,1)} %rest_0_.1), channel_id=1, source_target_pairs={{0,1},{1,0},{2,3},{3,2},{4,5},{5,4},{6,7},{7,6},{8,9},{9,8},{10,11... | collective-permute-start | bytes 2359304 | tf_op jit(solution)/shard_map/ppermute | solution.py:31
  3.7 3.5 %collective-permute-start.2 = (bf16[2,12,128,128]{3,2,1,0:T(8,128)(2,1)}, bf16[2,12,128,128]{3,2,1,0:T(8,128)(2,1)S(1)}, u32[]{:S(2)}, u32[]{:S(2)}) collective-permute-start(bf16[2,12,128,128]{3,2,1,0:T(8,128)(2,1)} %rest_0_.1), channel_id=1, source_target_pairs={{0,2},{1,3},{2,4},{3,5},{4,6},{5,7},{6,0},{7,1},{8,10},{9,11},{10,... | collective-permute-start | bytes 2359304 | tf_op jit(solution)/shard_map/ppermute | solution.py:31
  7.2 1.9 %collective-permute-start = (bf16[24,128,128]{2,1,0:T(8,128)(2,1)}, bf16[24,128,128]{2,1,0:T(8,128)(2,1)S(1)}, u32[]{:S(2)}, u32[]{:S(2)}) collective-permute-start(bf16[24,128,128]{2,1,0:T(8,128)(2,1)} %bitcast.16), channel_id=1, source_target_pairs={{0,8},{8,16},{16,24},{24,32},{32,40},{40,48},{48,56},{56,64},{64,7... | collective-permute-start | bytes 2359304 | tf_op jit(solution)/shard_map/ppermute | solution.py:37
  9.2 3.6 %collective-permute-start.1 = (bf16[24,128,128]{2,1,0:T(8,128)(2,1)}, bf16[24,128,128]{2,1,0:T(8,128)(2,1)}, u32[]{:S(2)}, u32[]{:S(2)}) collective-permute-start(bf16[24,128,128]{2,1,0:T(8,128)(2,1)} %bitcast.18), channel_id=1, source_target_pairs={{8,0},{16,8},{24,16},{32,24},{40,32},{48,40},{56,48},{64,56},{72,6... | collective-permute-start | bytes 2359304 | tf_op jit(solution)/shard_map/ppermute | solution.py:37
  12.8 3.6 %collective-permute-start.3 = (bf16[2,12,128,128]{3,2,1,0:T(8,128)(2,1)}, bf16[2,12,128,128]{3,2,1,0:T(8,128)(2,1)}, u32[]{:S(2)}, u32[]{:S(2)}) collective-permute-start(bf16[2,12,128,128]{3,2,1,0:T(8,128)(2,1)} %rest_0_.1), channel_id=1, source_target_pairs={{0,6},{1,7},{2,0},{3,1},{4,2},{5,3},{6,4},{7,5},{8,14},{9,15},{10,... | collective-permute-start | bytes 2359304 | tf_op jit(solution)/shard_map/ppermute | solution.py:31
  16.4 14.0 %collective-permute-done.4.b_x.rest_3_ = bf16[2,12,128,128]{3,2,1,0:T(8,128)(2,1)S(1)} collective-permute-done((bf16[2,12,128,128]{3,2,1,0:T(8,128)(2,1)}, bf16[2,12,128,128]{3,2,1,0:T(8,128)(2,1)S(1)}, u32[]{:S(2)}, u32[]{:S(2)}) %collective-permute-start.4) | collective-permute-done | bytes 786464 | tf_op jit(solution)/shard_map/ppermute | solution.py:31
  30.4 4.9 %collective-permute-start.7 = (bf16[2,12,128,128]{3,2,1,0:T(8,128)(2,1)S(1)}, bf16[2,12,128,128]{3,2,1,0:T(8,128)(2,1)S(1)}, u32[]{:S(2)}, u32[]{:S(2)}) collective-permute-start(bf16[2,12,128,128]{3,2,1,0:T(8,128)(2,1)S(1)} %collective-permute-done.4.b_x.rest_3_), channel_id=1, source_target_pairs={{0,6},{1,7},{2,0},{3,1},{4,2},{5,3},{6,4},{7,5},{8,14},{9,15},{10,... | collective-permute-start | bytes 2359304 | tf_op jit(solution)/shard_map/ppermute | solution.py:31
  35.4 0.0 collective-permute-done.2.down.rest_1_
  35.4 3.1 %collective-permute-start.6 = (bf16[2,12,128,128]{3,2,1,0:T(8,128)(2,1)S(1)}, bf16[2,12,128,128]{3,2,1,0:T(8,128)(2,1)S(1)}, u32[]{:S(2)}, u32[]{:S(2)}) collective-permute-start(bf16[2,12,128,128]{3,2,1,0:T(8,128)(2,1)S(1)} %collective-permute-done.2.down.rest_1_), channel_id=1, source_target_pairs={{0,1},{1,0},{2,3},{3,2},{4,5},{5,4},{6,7},{7,6},{8,9},{9,8},{10,11... | collective-permute-start | bytes 2359304 | tf_op jit(solution)/shard_map/ppermute | solution.py:31
  38.5 0.0 collective-permute-done.la
  38.5 0.0 copy-start.3
  38.5 0.9 copy-done.3
  39.4 1.9 %collective-permute-start.5 = (bf16[2,12,128,128]{3,2,1,0:T(8,128)(2,1)S(1)}, bf16[2,12,128,128]{3,2,1,0:T(8,128)(2,1)}, u32[]{:S(2)}, u32[]{:S(2)}) collective-permute-start(bf16[2,12,128,128]{3,2,1,0:T(8,128)(2,1)S(1)} %collective-permute-done.2.down.rest_1_), channel_id=1, source_target_pairs={{0,2},{1,3},{2,4},{3,5},{4,6},{5,7},{6,0},{7,1},{8,10},{9,11},{10,... | collective-permute-start | bytes 2359304 | tf_op jit(solution)/shard_map/ppermute | solution.py:31
  41.4 0.5 broadcast.9
  41.9 1.3 %reduce.3 = f32[2,96]{1,0:T(2,128)S(1)} reduce(f32[2,1,96]{2,1,0:T(1,128)} %param.10, f32[]{:T(128)} %broadcast.9), dimensions={1}, to_apply=%param.10.reduce_sub_computation.3 | reduce | bytes 1540 | tf_op args[4]
  43.3 0.1 reshape.15.wts
  43.4 0.8 copy.10
  44.2 0.1 reshape.14.sec
  44.3 0.1 stack.51.meta
  44.4 0.0 copy-start
  44.4 0.0 collective-permute-done.1.ra
  44.4 0.0 copy-start.1
  44.4 1.2 %copy-done.1 = bf16[1,1,24,128,128]{4,3,2,1,0:T(8,128)(2,1)S(1)} copy-done((bf16[1,1,24,128,128]{4,3,2,1,0:T(8,128)(2,1)S(1)}, bf16[1,1,24,128,128]{4,3,2,1,0:T(8,128)(2,1)}, u32[]{:S(2)}) %copy-start.1) | copy-done | bytes 786456
  45.6 0.0 copy-start.2
  45.6 1.1 %copy-done.2 = bf16[1,1,24,128,128]{4,3,2,1,0:T(8,128)(2,1)S(1)} copy-done((bf16[1,1,24,128,128]{4,3,2,1,0:T(8,128)(2,1)S(1)}, bf16[1,1,24,128,128]{4,3,2,1,0:T(8,128)(2,1)}, u32[]{:S(2)}) %copy-start.2) | copy-done | bytes 786456
  46.7 0.0 copy-start.4
  46.7 1.1 %copy-done.4 = bf16[24,128,128]{2,1,0:T(8,128)(2,1)S(1)} copy-done((bf16[24,128,128]{2,1,0:T(8,128)(2,1)S(1)}, bf16[24,128,128]{2,1,0:T(8,128)(2,1)}, u32[]{:S(2)}) %copy-start.4) | copy-done | bytes 786456
  47.9 0.0 copy-start.5
  47.9 0.7 copy-done.5
  48.5 5.1 %shard_map.93 = (bf16[24,128,128]{2,1,0:T(8,128)(2,1)S(1)}, bf16[24,128,128]{2,1,0:T(8,128)(2,1)S(1)}, s32[384]{0:T(512)S(1)}) custom-call(s32[384]{0:T(512)S(1)} %reshape.14.sec, s32[24]{0:T(128)S(1)} %copy-done.5, s32[10]{0:T(128)S(1)} %stack.51.meta, bf16[24,128,128]{2,1,0:T(8,128)(2,1)S(1)} %bitcast.17, bf16[24,128,128]{2,1,0:T(8,128)(2,1)S(1)} %copy-done.4, ...), custom_call_target="tpu_custom_call" | custom-call | bytes 6000000 | tf_op jit(solution)/shard_map/pallas_call | solution.py:137
  53.7 0.0 collective-permute-done.3.up.rest_2_
  53.7 0.0 copy-done
  53.7 5.9 %shard_map.94 = (f32[24,128,128]{2,1,0:T(8,128)S(1)}, f32[24,128,128]{2,1,0:T(8,128)S(1)}, s32[1]{0:T(128)}) custom-call(s32[384]{0:T(512)S(1)} %reshape.14.sec, f32[192]{0:T(256)S(1)} %reshape.15.wts, s32[10]{0:T(128)S(1)} %stack.51.meta, bf16[24,128,128]{2,1,0:T(8,128)(2,1)S(1)} %get-tuple-element.20.le, bf16[24,128,128]{2,1,0:T(8,128)(2,1)S(1)} %get-tuple-element.21.re, ...), custom_call_target="tpu_custom_call" | custom-call | flops 805306368 | bytes 6000000 | tf_op jit(solution)/shard_map/pallas_call | solution.py:137
  59.6 0.0 collective-permute-done.7.x_up.rest_5_
  59.6 0.0 collective-permute-done.6.x_down.rest_4_
  59.6 1.0 shard_map.96
  60.7 2.5 %collective-permute-start.8 = (bf16[12,128,128]{2,1,0:T(8,128)(2,1)S(1)}, bf16[12,128,128]{2,1,0:T(8,128)(2,1)S(1)}, u32[]{:S(2)}, u32[]{:S(2)}) collective-permute-start(bf16[12,128,128]{2,1,0:T(8,128)(2,1)S(1)} %get-tuple-element.27), channel_id=1, source_target_pairs={{0,2},{1,3},{2,4},{3,5},{4,6},{5,7},{6,0},{7,1},{8,10},{9,11},{10,... | collective-permute-start | bytes 1179656 | tf_op jit(solution)/shard_map/ppermute | solution.py:31
  63.2 4.6 %collective-permute-start.9 = (bf16[12,128,128]{2,1,0:T(8,128)(2,1)S(1)}, bf16[12,128,128]{2,1,0:T(8,128)(2,1)S(1)}, u32[]{:S(2)}, u32[]{:S(2)}) collective-permute-start(bf16[12,128,128]{2,1,0:T(8,128)(2,1)S(1)} %get-tuple-element.28), channel_id=1, source_target_pairs={{0,6},{1,7},{2,0},{3,1},{4,2},{5,3},{6,4},{7,5},{8,14},{9,15},{10,... | collective-permute-start | bytes 1179656 | tf_op jit(solution)/shard_map/ppermute | solution.py:31
  67.7 0.0 collective-permute-done.5.opp.rest_6_
  67.8 0.0 copy-start.6
  67.8 4.7 %shard_map.95 = (f32[24,128,128]{2,1,0:T(8,128)S(1)}, f32[24,128,128]{2,1,0:T(8,128)S(1)}) custom-call(s32[384]{0:T(512)S(1)} %reshape.14.sec, f32[192]{0:T(256)S(1)} %reshape.15.wts, s32[10]{0:T(128)S(1)} %stack.51.meta, bf16[24,128,128]{2,1,0:T(8,128)(2,1)S(1)} %get-tuple-element.20.le, bf16[24,128,128]{2,1,0:T(8,128)(2,1)S(1)} %get-tuple-element.21.re, ...), custom_call_target="tpu_custom_call" | custom-call | flops 603979776 | bytes 6000000 | tf_op jit(solution)/shard_map/pallas_call | solution.py:137
  72.5 0.8 collective-permute-done.8.late0
  73.3 1.2 %collective-permute-done.9.late1 = bf16[12,128,128]{2,1,0:T(8,128)(2,1)S(1)} collective-permute-done((bf16[12,128,128]{2,1,0:T(8,128)(2,1)S(1)}, bf16[12,128,128]{2,1,0:T(8,128)(2,1)S(1)}, u32[]{:S(2)}, u32[]{:S(2)}) %collective-permute-start.9) | collective-permute-done | bytes 393248 | tf_op jit(solution)/shard_map/ppermute | solution.py:31
  74.5 0.0 copy-done.6
  74.5 11.1 %shard_map.97 = (bf16[24,128,128]{2,1,0:T(8,128)(2,1)}, bf16[24,128,128]{2,1,0:T(8,128)(2,1)}, bf16[8,6,128,128]{3,2,1,0:T(8,128)(2,1)S(1)}) custom-call(s32[384]{0:T(512)S(1)} %reshape.14.sec, s32[384]{0:T(512)S(1)} %get-tuple-element.19.order, f32[192]{0:T(256)S(1)} %reshape.15.wts, s32[24]{0:T(128)S(1)} %copy-done.6, s32[10]{0:T(128)S(1)} %stack.51.meta, ...), custom_call_target="tpu_custom_call" | custom-call | flops 1711276032 | bytes 6000000 | tf_op jit(solution)/shard_map/pallas_call | solution.py:137
  85.6 23.9 %all_to_all.5.parts = bf16[8,6,128,128]{3,2,1,0:T(8,128)(2,1)S(1)} all-to-all(bf16[8,6,128,128]{3,2,1,0:T(8,128)(2,1)S(1)} %get-tuple-element.31), channel_id=1, replica_groups=mesh['seg'=64,'op'=8] {'op'}, dimensions={0} | all-to-all | bytes 3145728 | tf_op jit(solution)/shard_map/all_to_all | solution.py:337
  109.6 0.9 shard_map.98
Async XLA Ops:
  0.6 29.8 %collective-permute-start.4 = (bf16[2,12,128,128]{3,2,1,0:T(8,128)(2,1)}, bf16[2,12,128,128]{3,2,1,0:T(8,128)(2,1)S(1)}, u32[]{:S(2)}, u32[]{:S(2)}) collective-permute-start(bf16[2,12,128,128]{3,2,1,0:T(8,128)(2,1)} %rest_0_.1), channel_id=1, source_target_pairs={{0,1},{1,0},{2,3},{3,2},{4,5},{5,4},{6,7},{7,6},{8,9},{9,8},{10,11... | collective-permute-start | bytes 2359304 | tf_op jit(solution)/shard_map/ppermute | solution.py:31
  3.7 31.6 %collective-permute-start.2 = (bf16[2,12,128,128]{3,2,1,0:T(8,128)(2,1)}, bf16[2,12,128,128]{3,2,1,0:T(8,128)(2,1)S(1)}, u32[]{:S(2)}, u32[]{:S(2)}) collective-permute-start(bf16[2,12,128,128]{3,2,1,0:T(8,128)(2,1)} %rest_0_.1), channel_id=1, source_target_pairs={{0,2},{1,3},{2,4},{3,5},{4,6},{5,7},{6,0},{7,1},{8,10},{9,11},{10,... | collective-permute-start | bytes 2359304 | tf_op jit(solution)/shard_map/ppermute | solution.py:31
  7.2 31.2 %collective-permute-start = (bf16[24,128,128]{2,1,0:T(8,128)(2,1)}, bf16[24,128,128]{2,1,0:T(8,128)(2,1)S(1)}, u32[]{:S(2)}, u32[]{:S(2)}) collective-permute-start(bf16[24,128,128]{2,1,0:T(8,128)(2,1)} %bitcast.16), channel_id=1, source_target_pairs={{0,8},{8,16},{16,24},{24,32},{32,40},{40,48},{48,56},{56,64},{64,7... | collective-permute-start | bytes 2359304 | tf_op jit(solution)/shard_map/ppermute | solution.py:37
  9.2 35.2 %collective-permute-start.1 = (bf16[24,128,128]{2,1,0:T(8,128)(2,1)}, bf16[24,128,128]{2,1,0:T(8,128)(2,1)}, u32[]{:S(2)}, u32[]{:S(2)}) collective-permute-start(bf16[24,128,128]{2,1,0:T(8,128)(2,1)} %bitcast.18), channel_id=1, source_target_pairs={{8,0},{16,8},{24,16},{32,24},{40,32},{48,40},{56,48},{64,56},{72,6... | collective-permute-start | bytes 2359304 | tf_op jit(solution)/shard_map/ppermute | solution.py:37
  12.8 40.8 %collective-permute-start.3 = (bf16[2,12,128,128]{3,2,1,0:T(8,128)(2,1)}, bf16[2,12,128,128]{3,2,1,0:T(8,128)(2,1)}, u32[]{:S(2)}, u32[]{:S(2)}) collective-permute-start(bf16[2,12,128,128]{3,2,1,0:T(8,128)(2,1)} %rest_0_.1), channel_id=1, source_target_pairs={{0,6},{1,7},{2,0},{3,1},{4,2},{5,3},{6,4},{7,5},{8,14},{9,15},{10,... | collective-permute-start | bytes 2359304 | tf_op jit(solution)/shard_map/ppermute | solution.py:31
  30.4 29.2 %collective-permute-start.7 = (bf16[2,12,128,128]{3,2,1,0:T(8,128)(2,1)S(1)}, bf16[2,12,128,128]{3,2,1,0:T(8,128)(2,1)S(1)}, u32[]{:S(2)}, u32[]{:S(2)}) collective-permute-start(bf16[2,12,128,128]{3,2,1,0:T(8,128)(2,1)S(1)} %collective-permute-done.4.b_x.rest_3_), channel_id=1, source_target_pairs={{0,6},{1,7},{2,0},{3,1},{4,2},{5,3},{6,4},{7,5},{8,14},{9,15},{10,... | collective-permute-start | bytes 2359304 | tf_op jit(solution)/shard_map/ppermute | solution.py:31
  35.4 24.2 %collective-permute-start.6 = (bf16[2,12,128,128]{3,2,1,0:T(8,128)(2,1)S(1)}, bf16[2,12,128,128]{3,2,1,0:T(8,128)(2,1)S(1)}, u32[]{:S(2)}, u32[]{:S(2)}) collective-permute-start(bf16[2,12,128,128]{3,2,1,0:T(8,128)(2,1)S(1)} %collective-permute-done.2.down.rest_1_), channel_id=1, source_target_pairs={{0,1},{1,0},{2,3},{3,2},{4,5},{5,4},{6,7},{7,6},{8,9},{9,8},{10,11... | collective-permute-start | bytes 2359304 | tf_op jit(solution)/shard_map/ppermute | solution.py:31
  38.5 0.9 copy-start.3
  39.4 28.4 %collective-permute-start.5 = (bf16[2,12,128,128]{3,2,1,0:T(8,128)(2,1)S(1)}, bf16[2,12,128,128]{3,2,1,0:T(8,128)(2,1)}, u32[]{:S(2)}, u32[]{:S(2)}) collective-permute-start(bf16[2,12,128,128]{3,2,1,0:T(8,128)(2,1)S(1)} %collective-permute-done.2.down.rest_1_), channel_id=1, source_target_pairs={{0,2},{1,3},{2,4},{3,5},{4,6},{5,7},{6,0},{7,1},{8,10},{9,11},{10,... | collective-permute-start | bytes 2359304 | tf_op jit(solution)/shard_map/ppermute | solution.py:31
  44.4 9.3 %copy-start = (bf16[2,12,128,128]{3,2,1,0:T(8,128)(2,1)S(1)}, bf16[2,12,128,128]{3,2,1,0:T(8,128)(2,1)}, u32[]{:S(2)}) copy-start(bf16[2,12,128,128]{3,2,1,0:T(8,128)(2,1)} %rest_0_.1) | copy-start | bytes 2359300
  44.4 1.2 %copy-start.1 = (bf16[1,1,24,128,128]{4,3,2,1,0:T(8,128)(2,1)S(1)}, bf16[1,1,24,128,128]{4,3,2,1,0:T(8,128)(2,1)}, u32[]{:S(2)}) copy-start(bf16[1,1,24,128,128]{4,3,2,1,0:T(8,128)(2,1)} %param.6) | copy-start | bytes 2359300
  45.6 1.1 %copy-start.2 = (bf16[1,1,24,128,128]{4,3,2,1,0:T(8,128)(2,1)S(1)}, bf16[1,1,24,128,128]{4,3,2,1,0:T(8,128)(2,1)}, u32[]{:S(2)}) copy-start(bf16[1,1,24,128,128]{4,3,2,1,0:T(8,128)(2,1)} %param.7) | copy-start | bytes 2359300
  46.7 1.1 %copy-start.4 = (bf16[24,128,128]{2,1,0:T(8,128)(2,1)S(1)}, bf16[24,128,128]{2,1,0:T(8,128)(2,1)}, u32[]{:S(2)}) copy-start(bf16[24,128,128]{2,1,0:T(8,128)(2,1)} %copy-done.3) | copy-start | bytes 2359300
  47.9 0.7 copy-start.5
  60.7 12.6 %collective-permute-start.8 = (bf16[12,128,128]{2,1,0:T(8,128)(2,1)S(1)}, bf16[12,128,128]{2,1,0:T(8,128)(2,1)S(1)}, u32[]{:S(2)}, u32[]{:S(2)}) collective-permute-start(bf16[12,128,128]{2,1,0:T(8,128)(2,1)S(1)} %get-tuple-element.27), channel_id=1, source_target_pairs={{0,2},{1,3},{2,4},{3,5},{4,6},{5,7},{6,0},{7,1},{8,10},{9,11},{10,... | collective-permute-start | bytes 1179656 | tf_op jit(solution)/shard_map/ppermute | solution.py:31
  63.2 11.3 %collective-permute-start.9 = (bf16[12,128,128]{2,1,0:T(8,128)(2,1)S(1)}, bf16[12,128,128]{2,1,0:T(8,128)(2,1)S(1)}, u32[]{:S(2)}, u32[]{:S(2)}) collective-permute-start(bf16[12,128,128]{2,1,0:T(8,128)(2,1)S(1)} %get-tuple-element.28), channel_id=1, source_target_pairs={{0,6},{1,7},{2,0},{3,1},{4,2},{5,3},{6,4},{7,5},{8,14},{9,15},{10,... | collective-permute-start | bytes 1179656 | tf_op jit(solution)/shard_map/ppermute | solution.py:31
  67.8 6.7 %copy-start.6 = (s32[24]{0:T(128)S(1)}, s32[24]{0:T(128)}, u32[]{:S(2)}) copy-start(s32[24]{0:T(128)} %sizes.3) | copy-start | bytes 292

commit v2 on v1

v2 whole, which is shorter than its diff:
```python
import jax
import jax.numpy as jnp
from jax import lax
from jax.experimental import pallas as pl
from jax.experimental.pallas import tpu as pltpu
from jax.sharding import PartitionSpec as P

F32 = jnp.float32
BF16 = jnp.bfloat16
VMEM = pl.BlockSpec(memory_space=pltpu.VMEM)
SMEM = pl.BlockSpec(memory_space=pltpu.SMEM)
HBM = pl.BlockSpec(memory_space=pltpu.HBM)
NY, NX = 4, 2
TERMS = NY * NX
PER_SECTOR = 4
UNROLL = 12
NN = (((1,), (0,)), ((), ()))
TN = (((0,), (0,)), ((), ()))
NT = (((1,), (1,)), ((), ()))
OWN, DOWN, UP, OPP, X_OWN, X_DOWN, X_UP, X_OPP = range(8)
STEPS_OF = ((0, 0), (-1, 0), (1, 0), (2, 0), (0, 1), (-1, 1), (1, 1), (2, 1))


def dot(a, b, dims):
    return lax.dot_general(a, b, dims, preferred_element_type=F32)


def op_route(dy, dx):
    return [(o, ((o // NX + dy) % NY) * NX + ((o % NX) ^ dx)) for o in range(TERMS)]


def hop(block, dy, dx):
    return lax.ppermute(block, "op", op_route(dy, dx))


def along_segments(block, distance, across):
    size = lax.axis_size("seg")
    route = [(i - distance, i) for i in range(size) if i - distance in range(size)]
    middle = {size // 2 - 1, size // 2}
    route = [pair for pair in route if (set(pair) == middle) == across]
    return lax.ppermute(block, "seg", route)


def live(sizes, sector, width):
    rows = lax.broadcasted_iota(jnp.int32, (width, width), 0)
    cols = lax.broadcasted_iota(jnp.int32, (width, width), 1)
    return jnp.maximum(rows, cols) < sizes[sector]


def finish(total, sizes, out):
    num, width, _ = total.shape

    @pl.loop(0, num, step=4)
    def _(start):
        for u in range(4):
            alive = live(sizes, start + u, width)
            out[start + u] = jnp.where(alive, total[start + u].astype(F32), 0.0).astype(BF16)


def rank_blocks(sectors, out, n):
    place = lax.broadcasted_iota(jnp.int32, (n, n), 0)
    block = lax.broadcasted_iota(jnp.int32, (n, n), 1)
    earlier = jnp.where(place < block, 1.0, 0.0).astype(BF16)
    index = lax.broadcasted_iota(jnp.int32, (8, n), 1).astype(F32).astype(BF16)
    for site in range(2):
        for side in range(2):
            mine = sectors[site, side : side + 1, :] == place // PER_SECTOR
            seen = dot(jnp.where(mine, 1.0, 0.0).astype(BF16), earlier, NN)
            wanted = (place % PER_SECTOR).astype(F32)
            chosen = jnp.where(jnp.logical_and(mine, seen == wanted), 1.0, 0.0).astype(BF16)
            row = dot(index, chosen, NT)[:1].astype(jnp.int32)
            out[2 * site + side : 2 * site + side + 1, :n] = row


def group(order, table, sector):
    return [order[table, PER_SECTOR * sector + j] for j in range(PER_SECTOR)]


def stage(first, last, unroll, body):
    @pl.loop(first, last, step=unroll)
    def _(start):
        for u in range(unroll):
            body(start + u)


def keep(out, sizes=None):
    def emit(sector, value):
        if sizes is None:
            out[sector] = value
        else:
            alive = live(sizes, sector, value.shape[0])
            out[sector] = jnp.where(alive, value, 0.0).astype(BF16)

    return emit


def left_outward(env, blocks, half, order, weights, site, unroll):
    num, width, _ = env.shape

    def outward(s):
        members = group(order, 2 * site, s)
        found = dot(env[s], jnp.concatenate([blocks[k] for k in members], axis=1), NN)
        for j, k in enumerate(members):
            piece = found[:, j * width : (j + 1) * width]
            half[k] = (piece * weights[site, 0, k]).astype(BF16)

    stage(0, num, unroll, outward)


def left_inward(blocks, half, emit, order, site, num, unroll, cuts=(0,), done=None):
    def inward(t):
        members = group(order, 2 * site + 1, t)
        a = jnp.concatenate([blocks[k] for k in members], axis=0)
        y = jnp.concatenate([half[k] for k in members], axis=0)
        emit(t, dot(a, y, TN))

    in_parts(inward, num, unroll, cuts, done)


def right_outward(env, blocks, half, order, weights, site, unroll):
    num, width, _ = env.shape

    def outward(t):
        members = group(order, 2 * site + 1, t)
        found = dot(jnp.concatenate([blocks[k] for k in members], axis=0), env[t], NN)
        for j, k in enumerate(members):
            piece = found[j * width : (j + 1) * width]
            half[k] = (piece * weights[site, 0, k]).astype(BF16)

    stage(0, num, unroll, outward)


def right_inward(blocks, half, emit, order, site, num, unroll, cuts=(0,), done=None):
    def inward(s):
        members = group(order, 2 * site, s)
        a = jnp.concatenate([blocks[k] for k in members], axis=1)
        z = jnp.concatenate([half[k] for k in members], axis=1)
        emit(s, dot(z, a, NT))

    in_parts(inward, num, unroll, cuts, done)


def in_parts(body, num, unroll, cuts, done):
    for first, last in zip(cuts, tuple(cuts[1:]) + (num,)):
        stage(first, last, min(unroll, last - first), body)
        if done is not None:
            done(first, last)


def add_left(env, total, blocks, sectors, weights, site, first, count):
    found = []
    for j in range(count):
        k = first + j
        block = blocks[j]
        half = (dot(env[sectors[site, 0, k]], block, NN) * weights[site, 0, k]).astype(BF16)
        found.append((sectors[site, 1, k], dot(block, half, TN)))
    for place, value in found:
        total[place] += value


def add_right(env, total, blocks, sectors, weights, site, first, count):
    found = []
    for j in range(count):
        k = first + j
        block = blocks[j]
        half = (dot(block, env[sectors[site, 1, k]], NN) * weights[site, 0, k]).astype(BF16)
        found.append((sectors[site, 0, k], dot(half, block, NT)))
    for place, value in found:
        total[place] += value


def shard_at(slot):
    dy, dx = STEPS_OF[slot]
    me = lax.axis_index("op")
    return ((me // NX + dy + NY) % NY) * NX + ((me % NX) ^ dx)


def after(token, *arrays):
    def body(token, *refs):
        pass

    return pl.pallas_call(
        body,
        out_shape=[jax.ShapeDtypeStruct(a.shape, a.dtype) for a in arrays],
        in_specs=[SMEM] + [HBM] * len(arrays),
        out_specs=[HBM] * len(arrays),
        input_output_aliases={1 + i: i for i in range(len(arrays))},
    )(token, *arrays)


def call(body, outs, ins, scratch=(), flops=0, vmem=60, aliases={}):
    return pl.pallas_call(
        body,
        out_shape=[shape for _, shape in outs],
        in_specs=[spec for spec, _ in ins],
        out_specs=[spec for spec, _ in outs],
        scratch_shapes=list(scratch),
        input_output_aliases=aliases,
        compiler_params=pltpu.CompilerParams(vmem_limit_bytes=vmem * 1024 * 1024),
        cost_estimate=pl.CostEstimate(flops=flops, bytes_accessed=6000000, transcendentals=0),
    )(*[array for _, array in ins])


def local(left_in, right_in, site_blocks, sectors, site_operator, sector_sizes):
    num, width = left_in.shape[2], left_in.shape[3]
    n = sectors.shape[1]
    share = n // TERMS
    per = num // TERMS
    env = jax.ShapeDtypeStruct((num, width, width), BF16)
    total = jax.ShapeDtypeStruct((num, width, width), F32)
    site_shape = jax.ShapeDtypeStruct((share, width, width), BF16)
    token_shape = jax.ShapeDtypeStruct((1,), jnp.int32)
    env_scratch = pltpu.VMEM(env.shape, BF16)
    total_scratch = pltpu.VMEM(total.shape, F32)
    site_scratch = pltpu.VMEM((n, width, width), BF16)
    sec = jnp.transpose(sectors, (0, 2, 1))
    wts = site_operator

    def move(pairs, sems):
        copies = [
            pltpu.make_async_copy(source, into, sems.at[i])
            for i, (source, into) in enumerate(pairs)
        ]
        for copy in copies:
            copy.start()
        return copies

    def wait(copies):
        for copy in copies:
            copy.wait()

    own = site_blocks
    b_x = hop(own, 0, 1)
    down = hop(own, 1, 0)
    up = hop(own, -1, 0)

    def prepare(sizes, sec_rows, lo_in, ro_in, lo_out, ro_out, order, left, right, ranked, sems):
        coming = move([(lo_in, left), (ro_in, right)], sems.at[pl.ds(0, 2)])
        rank_blocks(sec_rows, ranked, n)
        ranking = move([(ranked, order)], sems.at[pl.ds(2, 1)])
        going = []
        for i, (env_ref, out) in enumerate(((left, lo_out), (right, ro_out))):
            coming[i].wait()
            finish(env_ref, sizes, env_ref)
            going += move([(env_ref, out)], sems.at[pl.ds(3 + i, 1)])
        wait(ranking + going)

    left_own, right_own, order = call(
        prepare,
        [(HBM, env)] * 2 + [(SMEM, jax.ShapeDtypeStruct((4, 128), jnp.int32))],
        [(SMEM, sector_sizes), (VMEM, sec), (HBM, left_in[0, 0]), (HBM, right_in[0, 0])],
        scratch=[env_scratch] * 2
        + [pltpu.VMEM((4, 128), jnp.int32), pltpu.SemaphoreType.DMA((5,))],
    )
    left_arrived = along_segments(left_own, 1, False)
    right_arrived = along_segments(right_own, -1, False)
    x_up = hop(b_x, -1, 0)
    x_down = hop(down, 0, 1)
    opp = hop(down, 1, 0)

    def seg_flags():
        seg, size = lax.axis_index("seg"), lax.axis_size("seg")
        return seg == 0, seg == size - 1

    def choose(pairs, into, sem):
        for flag, source in pairs:

            @pl.when(flag)
            def _():
                pltpu.make_async_copy(source, into, sem).start()

        return pltpu.make_async_copy(pairs[0][1], into, sem)

    pair_scratch = pltpu.VMEM((2, share, width, width), BF16)
    half_scratch = pltpu.VMEM((share, width, width), BF16)

    def near(wts, sec, lo, la, own, down, up, b_x, lt_out, token, left, lt, *rest):
        ins, sems, env_sem = rest[:4], rest[4], rest[5]
        first_seg, _ = seg_flags()
        edges = ((first_seg, lo), (jnp.logical_not(first_seg), la))
        coming_left = choose(edges, left, env_sem)
        coming = move([(a.at[0], b) for a, b in zip((own, down, up, b_x), ins)], sems)
        token[0] = 0

        @pl.loop(0, num, step=4)
        def _(t):
            for u in range(4):
                lt[t + u] = jnp.zeros((width, width), F32)

        coming_left.wait()
        for ref, slot, copy in zip(ins, (OWN, DOWN, UP, X_OWN), coming):
            copy.wait()
            add_left(left, lt, ref, sec, wts, 0, shard_at(slot) * share, share)
        wait(move([(lt, lt_out)], sems))

    lt, token = call(
        near,
        [(HBM, total), (SMEM, token_shape)],
        [(SMEM, wts), (SMEM, sec)]
        + [(HBM, a) for a in (left_own, left_arrived, own, down, up, b_x)],
        scratch=[env_scratch, total_scratch]
        + [half_scratch] * 4
        + [pltpu.SemaphoreType.DMA((4,)), pltpu.SemaphoreType.DMA(())],
        flops=2 * 48 * 2 * 128**3,
    )

    def pick(token, x_down, x_up, lo, ro, out0, out1, lo_out, ro_out, sems):
        wait(move([(x_down.at[0], out0), (x_up.at[1], out1)], sems))

    send0, send1, left_own, right_own = call(
        pick,
        [(VMEM, site_shape), (VMEM, site_shape), (HBM, env), (HBM, env)],
        [(SMEM, token)] + [(HBM, a) for a in (x_down, x_up, left_own, right_own)],
        scratch=[pltpu.SemaphoreType.DMA((2,))],
        vmem=4,
        aliases={3: 2, 4: 3},
    )
    x_opp0 = hop(send0, 1, 0)
    x_opp1 = hop(send1, -1, 0)
    left_across = along_segments(left_own, 1, True)
    right_across = along_segments(right_own, -1, True)

    def further(wts, sec, lo, la, lt_in, opp, x_down, x_up, lt_out, left, lt, *rest):
        ins, sems = rest[:3], rest[3]
        first_seg, _ = seg_flags()
        edges = ((first_seg, lo), (jnp.logical_not(first_seg), la))
        coming = [choose(edges, left, sems.at[0])] + move([(lt_in, lt)], sems.at[pl.ds(1, 1)])
        froms = [a.at[0] for a in (opp, x_down, x_up)]
        blocks = move(list(zip(froms, ins)), sems.at[pl.ds(2, 3)])
        wait(coming)
        for ref, slot, copy in zip(ins, (OPP, X_DOWN, X_UP), blocks):
            copy.wait()
            add_left(left, lt, ref, sec, wts, 0, shard_at(slot) * share, share)
        wait(move([(lt, lt_out)], sems.at[pl.ds(1, 1)]))

    (lt,) = call(
        further,
        [(HBM, total)],
        [(SMEM, wts), (SMEM, sec)] + [(HBM, a) for a in (left_own, left_arrived, lt, opp, x_down, x_up)],
        scratch=[env_scratch, total_scratch]
        + [half_scratch] * 3
        + [pltpu.SemaphoreType.DMA((5,))],
        flops=2 * 36 * 2 * 128**3,
    )

    slots = (OWN, X_OWN, DOWN, UP, OPP, X_DOWN, X_UP)
    pairs = (own, b_x, down, up, opp, x_down, x_up)

    def last(wts, sizes, sec, order, lo, la, lx, ro, ra, rx, lt_in, late0, late1, *rest):
        pairs, rest = rest[: TERMS - 1], rest[TERMS - 1 :]
        left_out, right_out, both, left, right, lt, done_left, done_right = rest[:8]
        blocks0, blocks1, half, sems, late_sems, out_sems = rest[8:]
        seg, middle = lax.axis_index("seg"), lax.axis_size("seg") // 2
        first_seg, last_seg = seg_flags()
        left_mid, right_mid = seg == middle, seg == middle - 1

        def places(site, blocks):
            refs = [pair.at[site] for pair in pairs]
            firsts = [pl.multiple_of(shard_at(slot) * share, share) for slot in slots]
            return [(ref, blocks.at[pl.ds(f, share)]) for ref, f in zip(refs, firsts)]

        first = shard_at(X_OPP) * share
        late = pl.ds(pl.multiple_of(first, share), share)
        for_left = move([(late0, blocks0.at[late]), (lt_in, lt)], late_sems)
        plain = jnp.logical_not(jnp.logical_or(first_seg, left_mid))
        edges = ((first_seg, lo), (left_mid, lx), (plain, la))
        for_left.append(choose(edges, left, late_sems.at[2]))
        copies1 = move([(late1, blocks1.at[late])], late_sems.at[pl.ds(3, 1)])
        plain = jnp.logical_not(jnp.logical_or(last_seg, right_mid))
        edges = ((last_seg, ro), (right_mid, rx), (plain, ra))
        copies1.append(choose(edges, right, late_sems.at[4]))
        copies1 += move(places(1, blocks1), sems.at[pl.ds(0, TERMS - 1)])
        wait(for_left)

        @pl.when(jnp.logical_not(left_mid))
        def _():
            add_left(left, lt, blocks0.at[late], sec, wts, 0, first, share)
            finish(lt, sizes, left)

        wait(copies1)
        copies0 = move(places(0, blocks0), sems.at[pl.ds(TERMS - 1, TERMS - 1)])

        right_outward(right, blocks1, half, order, wts, 1, UNROLL)
        right_inward(blocks1, half, keep(right, sizes), order, 1, num, UNROLL)
        wait(copies0)

        @pl.when(left_mid)
        def _():
            left_outward(left, blocks0, half, order, wts, 0, UNROLL)
            left_inward(blocks0, half, keep(left, sizes), order, 0, num, UNROLL)

        sent = []

        def sender(done, out, at):
            def send(begin, end):
                count = (end - begin) // per
                to = both.at[pl.ds(begin // per, count), pl.ds(at * per, per)]
                rows = pl.ds(begin, end - begin)
                packed = done.at[rows].reshape(count, per, width, width)
                going = [(done.at[rows], out.at[rows]), (packed, to)]
                sent.extend(move(going, out_sems.at[pl.ds(len(sent), 2)]))

            return send

        cuts = (0, num // 2)
        left_outward(left, blocks1, half, order, wts, 1, UNROLL)
        left_inward(
            blocks1, half, keep(done_left, sizes), order, 1, num, UNROLL,
            cuts, sender(done_left, left_out, 0),
        )
        right_outward(right, blocks0, half, order, wts, 0, UNROLL)
        right_inward(
            blocks0, half, keep(done_right, sizes), order, 0, num, UNROLL,
            cuts, sender(done_right, right_out, 1),
        )
        wait(sent)

    packed = jax.ShapeDtypeStruct((TERMS, 2 * per, width, width), BF16)
    left_state, right_state, both = call(
        last,
        [(HBM, env), (HBM, env), (HBM, packed)],
        [(SMEM, wts), (SMEM, sector_sizes), (SMEM, sec), (SMEM, order)]
        + [(HBM, a) for a in (left_own, left_arrived, left_across, right_own, right_arrived, right_across)]
        + [(HBM, a) for a in (lt, x_opp0, x_opp1)]
        + [(HBM, a) for a in pairs],
        scratch=[env_scratch] * 2
        + [total_scratch]
        + [env_scratch] * 2
        + [site_scratch] * 3
        + [pltpu.SemaphoreType.DMA((2 * TERMS - 2,))]
        + [pltpu.SemaphoreType.DMA((5,)), pltpu.SemaphoreType.DMA((8,))],
        flops=2 * 300 * 2 * 128**3,
    )
    parts = lax.all_to_all(both, "op", 0, 0, tiled=True)

    def sum_terms(parts, left_sum, right_sum):
        for t in range(per):
            for out, at in ((left_sum, t), (right_sum, per + t)):
                value = parts[0, at].astype(F32)
                for term in range(1, TERMS):
                    value += parts[term, at].astype(F32)
                out[t] = value

    part = jax.ShapeDtypeStruct((per, width, width), F32)
    left_sum, right_sum = call(sum_terms, [(VMEM, part), (VMEM, part)], [(VMEM, parts)], vmem=16)
    return left_state[None, None], right_state[None, None], left_sum[None], right_sum[None]


def solution(mesh):
    placed = (
        P("seg", "op", None, None, None),
        P("seg", "op", None, None, None),
        P("seg", "op", None, None),
        P("seg", None, None),
        P("seg", "op", None),
        P(),
    )
    return jax.shard_map(
        local,
        mesh=mesh,
        in_specs=placed,
        out_specs=(
            P("seg", "op", None, None, None),
            P("seg", "op", None, None, None),
            P("seg", "op", None, None),
            P("seg", "op", None, None),
        ),
        check_vma=False,
    )
```

time: 111 us -> 109 us (0.982)
  the two profiles are of different devices: /device:TPU:484 before, /device:TPU:4 now
where the time goes in v2:
time: 109 us; the launch traced here: 108 us
  starting transfers between devices  41.4 us (38%)
  Pallas kernels  30.6 us (28%)
  blocking collectives  18.1 us (17%)
  waiting for transfers between devices  15.1 us (14%)
  local copies, waits for them, and re-layouts  1.79 us (2%)
    pallas_call x6, Pallas kernels, call(): pl.pallas_call(body, out_shape=[shape for _, shape in outs], in_specs=[sp...  30.6 us
    ppermute x8, starting transfers between devices, hop(): return lax.ppermute(block, 'op', op_route(dy, dx))  28.5 us
    all_to_all x1, blocking collectives, local(): parts = lax.all_to_all(both, 'op', 0, 0, tiled=True)  18.1 us
    ppermute x4, starting transfers between devices, along_segments(): return lax.ppermute(block, 'seg', route)  12.9 us
    ppermute x8, waiting for transfers between devices, hop(): return lax.ppermute(block, 'op', op_route(dy, dx))  11.9 us
    ppermute x4, waiting for transfers between devices, along_segments(): return lax.ppermute(block, 'seg', route)  3.28 us
  transfers between devices with their start and end apart: 12, of which 5 were waited for; matrix products, arithmetic and copies ran while one was open for 0% of the time, Pallas kernels for 15%

profile of v2, /device:TPU:4, one launch (start us, length us, event | category | flops | bytes accessed | tf_op | source)
XLA Modules:
  0.0 107.9 jit_solution(9941640558414702615)
XLA Ops:
  0.6 3.1 %collective-permute-start.3 = (bf16[2,12,128,128]{3,2,1,0:T(8,128)(2,1)}, bf16[2,12,128,128]{3,2,1,0:T(8,128)(2,1)}, u32[]{:S(2)}, u32[]{:S(2)}) collective-permute-start(bf16[2,12,128,128]{3,2,1,0:T(8,128)(2,1)} %rest_0_.1), channel_id=1, source_target_pairs={{0,1},{1,0},{2,3},{3,2},{4,5},{5,4},{6,7},{7,6},{8,9},{9,8},{10,11... | collective-permute-start | bytes 2359304 | tf_op jit(solution)/shard_map/ppermute | solution.py:33
  3.7 3.5 %collective-permute-start.1 = (bf16[2,12,128,128]{3,2,1,0:T(8,128)(2,1)}, bf16[2,12,128,128]{3,2,1,0:T(8,128)(2,1)}, u32[]{:S(2)}, u32[]{:S(2)}) collective-permute-start(bf16[2,12,128,128]{3,2,1,0:T(8,128)(2,1)} %rest_0_.1), channel_id=1, source_target_pairs={{0,2},{1,3},{2,4},{3,5},{4,6},{5,7},{6,0},{7,1},{8,10},{9,11},{10,... | collective-permute-start | bytes 2359304 | tf_op jit(solution)/shard_map/ppermute | solution.py:33
  7.2 3.6 %collective-permute-start.2 = (bf16[2,12,128,128]{3,2,1,0:T(8,128)(2,1)}, bf16[2,12,128,128]{3,2,1,0:T(8,128)(2,1)}, u32[]{:S(2)}, u32[]{:S(2)}) collective-permute-start(bf16[2,12,128,128]{3,2,1,0:T(8,128)(2,1)} %rest_0_.1), channel_id=1, source_target_pairs={{0,6},{1,7},{2,0},{3,1},{4,2},{5,3},{6,4},{7,5},{8,14},{9,15},{10,... | collective-permute-start | bytes 2359304 | tf_op jit(solution)/shard_map/ppermute | solution.py:33
  10.8 3.8 %shard_map.93 = (bf16[24,128,128]{2,1,0:T(8,128)(2,1)}, bf16[24,128,128]{2,1,0:T(8,128)(2,1)}, s32[4,128]{1,0:T(4,128)}) custom-call(s32[24]{0:T(128)} %sizes.3, s32[2,2,96]{2,1,0:T(2,128)} %bitcast.9, bf16[24,128,128]{2,1,0:T(8,128)(2,1)} %bitcast.7, bf16[24,128,128]{2,1,0:T(8,128)(2,1)} %bitcast.8), custom_call_target="tpu_custom_call" | custom-call | bytes 6000000 | tf_op jit(solution)/shard_map/pallas_call | solution.py:192
  14.6 1.3 %collective-permute-start = (bf16[24,128,128]{2,1,0:T(8,128)(2,1)}, bf16[24,128,128]{2,1,0:T(8,128)(2,1)S(1)}, u32[]{:S(2)}, u32[]{:S(2)}) collective-permute-start(bf16[24,128,128]{2,1,0:T(8,128)(2,1)} %get-tuple-element.19.lo), channel_id=1, source_target_pairs={{0,8},{8,16},{16,24},{24,32},{32,40},{40,48},{48,56},{56,64},{64,7... | collective-permute-start | bytes 2359304 | tf_op jit(solution)/shard_map/ppermute | solution.py:41
  16.0 0.0 copy-start
  16.0 0.0 copy-start.4
  16.0 1.4 %collective-permute-start.7 = (bf16[24,128,128]{2,1,0:T(8,128)(2,1)}, bf16[24,128,128]{2,1,0:T(8,128)(2,1)}, u32[]{:S(2)}, u32[]{:S(2)}) collective-permute-start(bf16[24,128,128]{2,1,0:T(8,128)(2,1)} %get-tuple-element.21.ro), channel_id=1, source_target_pairs={{8,0},{16,8},{24,16},{32,24},{40,32},{48,40},{56,48},{64,56},{72,6... | collective-permute-start | bytes 2359304 | tf_op jit(solution)/shard_map/ppermute | solution.py:41
  17.5 4.7 %collective-permute-done.3.b_x.rest_1_ = bf16[2,12,128,128]{3,2,1,0:T(8,128)(2,1)} collective-permute-done((bf16[2,12,128,128]{3,2,1,0:T(8,128)(2,1)}, bf16[2,12,128,128]{3,2,1,0:T(8,128)(2,1)}, u32[]{:S(2)}, u32[]{:S(2)}) %collective-permute-start.3) | collective-permute-done | bytes 786464 | tf_op jit(solution)/shard_map/ppermute | solution.py:33
  22.1 4.9 %collective-permute-start.5 = (bf16[2,12,128,128]{3,2,1,0:T(8,128)(2,1)}, bf16[2,12,128,128]{3,2,1,0:T(8,128)(2,1)S(1)}, u32[]{:S(2)}, u32[]{:S(2)}) collective-permute-start(bf16[2,12,128,128]{3,2,1,0:T(8,128)(2,1)} %collective-permute-done.3.b_x.rest_1_), channel_id=1, source_target_pairs={{0,6},{1,7},{2,0},{3,1},{4,2},{5,3},{6,4},{7,5},{8,14},{9,15},{10,... | collective-permute-start | bytes 2359304 | tf_op jit(solution)/shard_map/ppermute | solution.py:33
  27.0 0.0 collective-permute-done.1.down.rest_2_
  27.1 3.1 %collective-permute-start.4 = (bf16[2,12,128,128]{3,2,1,0:T(8,128)(2,1)}, bf16[2,12,128,128]{3,2,1,0:T(8,128)(2,1)S(1)}, u32[]{:S(2)}, u32[]{:S(2)}) collective-permute-start(bf16[2,12,128,128]{3,2,1,0:T(8,128)(2,1)} %collective-permute-done.1.down.rest_2_), channel_id=1, source_target_pairs={{0,1},{1,0},{2,3},{3,2},{4,5},{5,4},{6,7},{7,6},{8,9},{9,8},{10,11... | collective-permute-start | bytes 2359304 | tf_op jit(solution)/shard_map/ppermute | solution.py:33
  30.2 0.0 collective-permute-done.2.up.rest_3_
  30.2 3.2 %collective-permute-start.9 = (bf16[2,12,128,128]{3,2,1,0:T(8,128)(2,1)}, bf16[2,12,128,128]{3,2,1,0:T(8,128)(2,1)}, u32[]{:S(2)}, u32[]{:S(2)}) collective-permute-start(bf16[2,12,128,128]{3,2,1,0:T(8,128)(2,1)} %collective-permute-done.1.down.rest_2_), channel_id=1, source_target_pairs={{0,2},{1,3},{2,4},{3,5},{4,6},{5,7},{6,0},{7,1},{8,10},{9,11},{10,... | collective-permute-start | bytes 2359304 | tf_op jit(solution)/shard_map/ppermute | solution.py:33
  33.4 0.0 collective-permute-done.la
  33.4 0.0 copy-start.6
  33.4 0.9 copy-done.6
  34.3 5.9 %shard_map.94 = (f32[24,128,128]{2,1,0:T(8,128)}, s32[1]{0:T(128)}) custom-call(f32[2,1,96]{2,1,0:T(1,128)} %wts.5, s32[2,2,96]{2,1,0:T(2,128)} %bitcast.10, bf16[24,128,128]{2,1,0:T(8,128)(2,1)} %get-tuple-element.19.lo, bf16[24,128,128]{2,1,0:T(8,128)(2,1)} %copy-done.6, bf16[2,12,128,128]{3,2,1,0:T(8,128)(2,1)} %rest_0_.1, ...), custom_call_target="tpu_custom_call" | custom-call | flops 402653184 | bytes 6000000 | tf_op jit(solution)/shard_map/pallas_call | solution.py:192
  40.3 0.0 collective-permute-done.7.ra
  40.3 4.7 %collective-permute-done.5.x_up.rest_6_ = bf16[2,12,128,128]{3,2,1,0:T(8,128)(2,1)S(1)} collective-permute-done((bf16[2,12,128,128]{3,2,1,0:T(8,128)(2,1)}, bf16[2,12,128,128]{3,2,1,0:T(8,128)(2,1)S(1)}, u32[]{:S(2)}, u32[]{:S(2)}) %collective-permute-start.5) | collective-permute-done | bytes 786464 | tf_op jit(solution)/shard_map/ppermute | solution.py:33
  44.9 0.0 copy-start.2
  44.9 2.4 %collective-permute-done.4.x_down.rest_5_ = bf16[2,12,128,128]{3,2,1,0:T(8,128)(2,1)S(1)} collective-permute-done((bf16[2,12,128,128]{3,2,1,0:T(8,128)(2,1)}, bf16[2,12,128,128]{3,2,1,0:T(8,128)(2,1)S(1)}, u32[]{:S(2)}, u32[]{:S(2)}) %collective-permute-start.4) | collective-permute-done | bytes 786464 | tf_op jit(solution)/shard_map/ppermute | solution.py:33
  47.3 0.0 copy-start.3
  47.3 0.0 copy-done
  47.3 0.0 copy-done.4
  47.3 1.1 shard_map.95
  48.4 0.0 copy-done.2
  48.4 0.0 copy-done.3
  48.4 0.0 copy-start.1
  48.4 0.0 copy-start.5
  48.4 8.9 %collective-permute-start.8 = (bf16[24,128,128]{2,1,0:T(8,128)(2,1)S(1)}, bf16[24,128,128]{2,1,0:T(8,128)(2,1)S(1)}, u32[]{:S(2)}, u32[]{:S(2)}) collective-permute-start(bf16[24,128,128]{2,1,0:T(8,128)(2,1)S(1)} %get-tuple-element.23.ro), channel_id=1, source_target_pairs={{256,248},{257,249},{258,250},{259,251},{260,252},{261,253},{262,2... | collective-permute-start | bytes 2359304 | tf_op jit(solution)/shard_map/ppermute | solution.py:41
  57.3 1.3 %collective-permute-start.6 = (bf16[24,128,128]{2,1,0:T(8,128)(2,1)S(1)}, bf16[24,128,128]{2,1,0:T(8,128)(2,1)S(1)}, u32[]{:S(2)}, u32[]{:S(2)}) collective-permute-start(bf16[24,128,128]{2,1,0:T(8,128)(2,1)S(1)} %get-tuple-element.22.lo), channel_id=1, source_target_pairs={{248,256},{249,257},{250,258},{251,259},{252,260},{253,261},{254,2... | collective-permute-start | bytes 2359304 | tf_op jit(solution)/shard_map/ppermute | solution.py:41
  58.6 2.0 %collective-permute-start.10 = (bf16[12,128,128]{2,1,0:T(8,128)(2,1)S(1)}, bf16[12,128,128]{2,1,0:T(8,128)(2,1)}, u32[]{:S(2)}, u32[]{:S(2)}) collective-permute-start(bf16[12,128,128]{2,1,0:T(8,128)(2,1)S(1)} %get-tuple-element.25), channel_id=1, source_target_pairs={{0,2},{1,3},{2,4},{3,5},{4,6},{5,7},{6,0},{7,1},{8,10},{9,11},{10,... | collective-permute-start | bytes 1179656 | tf_op jit(solution)/shard_map/ppermute | solution.py:33
  60.6 5.0 %collective-permute-start.11 = (bf16[12,128,128]{2,1,0:T(8,128)(2,1)S(1)}, bf16[12,128,128]{2,1,0:T(8,128)(2,1)}, u32[]{:S(2)}, u32[]{:S(2)}) collective-permute-start(bf16[12,128,128]{2,1,0:T(8,128)(2,1)S(1)} %get-tuple-element.26), channel_id=1, source_target_pairs={{0,6},{1,7},{2,0},{3,1},{4,2},{5,3},{6,4},{7,5},{8,14},{9,15},{10,... | collective-permute-start | bytes 1179656 | tf_op jit(solution)/shard_map/ppermute | solution.py:33
  65.6 0.0 collective-permute-done.9.opp.rest_4_
  65.7 0.0 copy-done.1
  65.7 5.1 %shard_map.96.lt_in = f32[24,128,128]{2,1,0:T(8,128)} custom-call(f32[2,1,96]{2,1,0:T(1,128)} %wts.5, s32[2,2,96]{2,1,0:T(2,128)} %bitcast.11, bf16[24,128,128]{2,1,0:T(8,128)(2,1)} %copy-done.1, bf16[24,128,128]{2,1,0:T(8,128)(2,1)} %copy-done.6, f32[24,128,128]{2,1,0:T(8,128)} %get-tuple-element.24.lt_in, ...), custom_call_target="tpu_custom_call" | custom-call | flops 301989888 | bytes 6000000 | tf_op jit(solution)/shard_map/pallas_call | solution.py:192
  70.7 0.0 copy-done.5
  70.7 0.0 collective-permute-done.10.late0
  70.8 0.2 collective-permute-done.11.late1
  70.9 0.0 collective-permute-done.8.rx
  70.9 0.0 copy-start.7
  70.9 3.3 %collective-permute-done.6.lx = bf16[24,128,128]{2,1,0:T(8,128)(2,1)S(1)} collective-permute-done((bf16[24,128,128]{2,1,0:T(8,128)(2,1)S(1)}, bf16[24,128,128]{2,1,0:T(8,128)(2,1)S(1)}, u32[]{:S(2)}, u32[]{:S(2)}) %collective-permute-start.6) | collective-permute-done | bytes 786464 | tf_op jit(solution)/shard_map/ppermute | solution.py:41
  74.2 0.0 copy-done.7
  74.2 0.9 copy-done.8
  75.1 13.8 %shard_map.97 = (bf16[24,128,128]{2,1,0:T(8,128)(2,1)}, bf16[24,128,128]{2,1,0:T(8,128)(2,1)}, bf16[8,6,128,128]{3,2,1,0:T(8,128)(2,1)}) custom-call(f32[2,1,96]{2,1,0:T(1,128)} %wts.5, s32[24]{0:T(128)} %sizes.3, s32[2,2,96]{2,1,0:T(2,128)} %bitcast.12, s32[4,128]{1,0:T(4,128)} %get-tuple-element.18.order, bf16[24,128,128]{2,1,0:T(8,128)(2,1)} %copy-done.1, ...), custom_call_target="tpu_custom_call" | custom-call | flops 2516582400 | bytes 6000000 | tf_op jit(solution)/shard_map/pallas_call | solution.py:192
  88.9 18.1 %all_to_all.5.parts = bf16[8,6,128,128]{3,2,1,0:T(8,128)(2,1)S(1)} all-to-all(bf16[8,6,128,128]{3,2,1,0:T(8,128)(2,1)} %get-tuple-element.29), channel_id=1, replica_groups=mesh['seg'=64,'op'=8] {'op'}, dimensions={0} | all-to-all | bytes 3145728 | tf_op jit(solution)/shard_map/all_to_all | solution.py:434
  107.0 0.9 shard_map.98
  (1 shorter events, 0.0 us)
Async XLA Ops:
  0.6 21.5 %collective-permute-start.3 = (bf16[2,12,128,128]{3,2,1,0:T(8,128)(2,1)}, bf16[2,12,128,128]{3,2,1,0:T(8,128)(2,1)}, u32[]{:S(2)}, u32[]{:S(2)}) collective-permute-start(bf16[2,12,128,128]{3,2,1,0:T(8,128)(2,1)} %rest_0_.1), channel_id=1, source_target_pairs={{0,1},{1,0},{2,3},{3,2},{4,5},{5,4},{6,7},{7,6},{8,9},{9,8},{10,11... | collective-permute-start | bytes 2359304 | tf_op jit(solution)/shard_map/ppermute | solution.py:33
  3.7 23.3 %collective-permute-start.1 = (bf16[2,12,128,128]{3,2,1,0:T(8,128)(2,1)}, bf16[2,12,128,128]{3,2,1,0:T(8,128)(2,1)}, u32[]{:S(2)}, u32[]{:S(2)}) collective-permute-start(bf16[2,12,128,128]{3,2,1,0:T(8,128)(2,1)} %rest_0_.1), channel_id=1, source_target_pairs={{0,2},{1,3},{2,4},{3,5},{4,6},{5,7},{6,0},{7,1},{8,10},{9,11},{10,... | collective-permute-start | bytes 2359304 | tf_op jit(solution)/shard_map/ppermute | solution.py:33
  7.2 22.9 %collective-permute-start.2 = (bf16[2,12,128,128]{3,2,1,0:T(8,128)(2,1)}, bf16[2,12,128,128]{3,2,1,0:T(8,128)(2,1)}, u32[]{:S(2)}, u32[]{:S(2)}) collective-permute-start(bf16[2,12,128,128]{3,2,1,0:T(8,128)(2,1)} %rest_0_.1), channel_id=1, source_target_pairs={{0,6},{1,7},{2,0},{3,1},{4,2},{5,3},{6,4},{7,5},{8,14},{9,15},{10,... | collective-permute-start | bytes 2359304 | tf_op jit(solution)/shard_map/ppermute | solution.py:33
  14.6 18.8 %collective-permute-start = (bf16[24,128,128]{2,1,0:T(8,128)(2,1)}, bf16[24,128,128]{2,1,0:T(8,128)(2,1)S(1)}, u32[]{:S(2)}, u32[]{:S(2)}) collective-permute-start(bf16[24,128,128]{2,1,0:T(8,128)(2,1)} %get-tuple-element.19.lo), channel_id=1, source_target_pairs={{0,8},{8,16},{16,24},{24,32},{32,40},{40,48},{48,56},{56,64},{64,7... | collective-permute-start | bytes 2359304 | tf_op jit(solution)/shard_map/ppermute | solution.py:41
  16.0 31.3 %copy-start = (bf16[24,128,128]{2,1,0:T(8,128)(2,1)S(1)}, bf16[24,128,128]{2,1,0:T(8,128)(2,1)}, u32[]{:S(2)}) copy-start(bf16[24,128,128]{2,1,0:T(8,128)(2,1)} %get-tuple-element.19.lo) | copy-start | bytes 2359300
  16.0 31.3 %copy-start.4 = (bf16[24,128,128]{2,1,0:T(8,128)(2,1)S(1)}, bf16[24,128,128]{2,1,0:T(8,128)(2,1)}, u32[]{:S(2)}) copy-start(bf16[24,128,128]{2,1,0:T(8,128)(2,1)} %get-tuple-element.21.ro) | copy-start | bytes 2359300
  16.0 24.2 %collective-permute-start.7 = (bf16[24,128,128]{2,1,0:T(8,128)(2,1)}, bf16[24,128,128]{2,1,0:T(8,128)(2,1)}, u32[]{:S(2)}, u32[]{:S(2)}) collective-permute-start(bf16[24,128,128]{2,1,0:T(8,128)(2,1)} %get-tuple-element.21.ro), channel_id=1, source_target_pairs={{8,0},{16,8},{24,16},{32,24},{40,32},{48,40},{56,48},{64,56},{72,6... | collective-permute-start | bytes 2359304 | tf_op jit(solution)/shard_map/ppermute | solution.py:41
  22.1 22.8 %collective-permute-start.5 = (bf16[2,12,128,128]{3,2,1,0:T(8,128)(2,1)}, bf16[2,12,128,128]{3,2,1,0:T(8,128)(2,1)S(1)}, u32[]{:S(2)}, u32[]{:S(2)}) collective-permute-start(bf16[2,12,128,128]{3,2,1,0:T(8,128)(2,1)} %collective-permute-done.3.b_x.rest_1_), channel_id=1, source_target_pairs={{0,6},{1,7},{2,0},{3,1},{4,2},{5,3},{6,4},{7,5},{8,14},{9,15},{10,... | collective-permute-start | bytes 2359304 | tf_op jit(solution)/shard_map/ppermute | solution.py:33
  27.1 20.2 %collective-permute-start.4 = (bf16[2,12,128,128]{3,2,1,0:T(8,128)(2,1)}, bf16[2,12,128,128]{3,2,1,0:T(8,128)(2,1)S(1)}, u32[]{:S(2)}, u32[]{:S(2)}) collective-permute-start(bf16[2,12,128,128]{3,2,1,0:T(8,128)(2,1)} %collective-permute-done.1.down.rest_2_), channel_id=1, source_target_pairs={{0,1},{1,0},{2,3},{3,2},{4,5},{5,4},{6,7},{7,6},{8,9},{9,8},{10,11... | collective-permute-start | bytes 2359304 | tf_op jit(solution)/shard_map/ppermute | solution.py:33
  30.2 35.5 %collective-permute-start.9 = (bf16[2,12,128,128]{3,2,1,0:T(8,128)(2,1)}, bf16[2,12,128,128]{3,2,1,0:T(8,128)(2,1)}, u32[]{:S(2)}, u32[]{:S(2)}) collective-permute-start(bf16[2,12,128,128]{3,2,1,0:T(8,128)(2,1)} %collective-permute-done.1.down.rest_2_), channel_id=1, source_target_pairs={{0,2},{1,3},{2,4},{3,5},{4,6},{5,7},{6,0},{7,1},{8,10},{9,11},{10,... | collective-permute-start | bytes 2359304 | tf_op jit(solution)/shard_map/ppermute | solution.py:33
  33.4 0.9 copy-start.6
  44.9 3.4 %copy-start.2 = (bf16[2,12,128,128]{3,2,1,0:T(8,128)(2,1)}, bf16[2,12,128,128]{3,2,1,0:T(8,128)(2,1)S(1)}, u32[]{:S(2)}) copy-start(bf16[2,12,128,128]{3,2,1,0:T(8,128)(2,1)S(1)} %collective-permute-done.5.x_up.rest_6_) | copy-start | bytes 2359300
  47.3 1.1 %copy-start.3 = (bf16[2,12,128,128]{3,2,1,0:T(8,128)(2,1)}, bf16[2,12,128,128]{3,2,1,0:T(8,128)(2,1)S(1)}, u32[]{:S(2)}) copy-start(bf16[2,12,128,128]{3,2,1,0:T(8,128)(2,1)S(1)} %collective-permute-done.4.x_down.rest_5_) | copy-start | bytes 2359300
  48.4 17.3 %copy-start.1 = (bf16[24,128,128]{2,1,0:T(8,128)(2,1)}, bf16[24,128,128]{2,1,0:T(8,128)(2,1)S(1)}, u32[]{:S(2)}) copy-start(bf16[24,128,128]{2,1,0:T(8,128)(2,1)S(1)} %get-tuple-element.22.lo) | copy-start | bytes 2359300
  48.4 22.3 %copy-start.5 = (bf16[24,128,128]{2,1,0:T(8,128)(2,1)}, bf16[24,128,128]{2,1,0:T(8,128)(2,1)S(1)}, u32[]{:S(2)}) copy-start(bf16[24,128,128]{2,1,0:T(8,128)(2,1)S(1)} %get-tuple-element.23.ro) | copy-start | bytes 2359300
  48.4 22.5 %collective-permute-start.8 = (bf16[24,128,128]{2,1,0:T(8,128)(2,1)S(1)}, bf16[24,128,128]{2,1,0:T(8,128)(2,1)S(1)}, u32[]{:S(2)}, u32[]{:S(2)}) collective-permute-start(bf16[24,128,128]{2,1,0:T(8,128)(2,1)S(1)} %get-tuple-element.23.ro), channel_id=1, source_target_pairs={{256,248},{257,249},{258,250},{259,251},{260,252},{261,253},{262,2... | collective-permute-start | bytes 2359304 | tf_op jit(solution)/shard_map/ppermute | solution.py:41
  57.3 16.9 %collective-permute-start.6 = (bf16[24,128,128]{2,1,0:T(8,128)(2,1)S(1)}, bf16[24,128,128]{2,1,0:T(8,128)(2,1)S(1)}, u32[]{:S(2)}, u32[]{:S(2)}) collective-permute-start(bf16[24,128,128]{2,1,0:T(8,128)(2,1)S(1)} %get-tuple-element.22.lo), channel_id=1, source_target_pairs={{248,256},{249,257},{250,258},{251,259},{252,260},{253,261},{254,2... | collective-permute-start | bytes 2359304 | tf_op jit(solution)/shard_map/ppermute | solution.py:41
  58.6 12.2 %collective-permute-start.10 = (bf16[12,128,128]{2,1,0:T(8,128)(2,1)S(1)}, bf16[12,128,128]{2,1,0:T(8,128)(2,1)}, u32[]{:S(2)}, u32[]{:S(2)}) collective-permute-start(bf16[12,128,128]{2,1,0:T(8,128)(2,1)S(1)} %get-tuple-element.25), channel_id=1, source_target_pairs={{0,2},{1,3},{2,4},{3,5},{4,6},{5,7},{6,0},{7,1},{8,10},{9,11},{10,... | collective-permute-start | bytes 1179656 | tf_op jit(solution)/shard_map/ppermute | solution.py:33
  60.6 10.3 %collective-permute-start.11 = (bf16[12,128,128]{2,1,0:T(8,128)(2,1)S(1)}, bf16[12,128,128]{2,1,0:T(8,128)(2,1)}, u32[]{:S(2)}, u32[]{:S(2)}) collective-permute-start(bf16[12,128,128]{2,1,0:T(8,128)(2,1)S(1)} %get-tuple-element.26), channel_id=1, source_target_pairs={{0,6},{1,7},{2,0},{3,1},{4,2},{5,3},{6,4},{7,5},{8,14},{9,15},{10,... | collective-permute-start | bytes 1179656 | tf_op jit(solution)/shard_map/ppermute | solution.py:33
  70.9 3.3 %copy-start.7 = (bf16[24,128,128]{2,1,0:T(8,128)(2,1)}, bf16[24,128,128]{2,1,0:T(8,128)(2,1)S(1)}, u32[]{:S(2)}) copy-start(bf16[24,128,128]{2,1,0:T(8,128)(2,1)S(1)} %collective-permute-done.8.rx) | copy-start | bytes 2359300
  74.2 0.9 copy-start.8

commit v3 on v2

--- a/solution.py
+++ b/solution.py
@@ -14,6 +14,7 @@
 TERMS = NY * NX
 PER_SECTOR = 4
 UNROLL = 12
+K_VMEM = 52
 NN = (((1,), (0,)), ((), ()))
 TN = (((0,), (0,)), ((), ()))
 NT = (((1,), (1,)), ((), ()))
@@ -33,11 +34,9 @@
     return lax.ppermute(block, "op", op_route(dy, dx))
 
 
-def along_segments(block, distance, across):
-    size = lax.axis_size("seg")
-    route = [(i - distance, i) for i in range(size) if i - distance in range(size)]
-    middle = {size // 2 - 1, size // 2}
-    route = [pair for pair in route if (set(pair) == middle) == across]
+def along_segments(block, distance):
+    devices = range(lax.axis_size("seg"))
+    route = [(i - distance, i) for i in devices if i - distance in devices]
     return lax.ppermute(block, "seg", route)
 
 
@@ -188,14 +187,13 @@
     )(token, *arrays)
 
 
-def call(body, outs, ins, scratch=(), flops=0, vmem=60, aliases={}):
+def call(body, outs, ins, scratch=(), flops=0, vmem=52):
     return pl.pallas_call(
         body,
         out_shape=[shape for _, shape in outs],
         in_specs=[spec for spec, _ in ins],
         out_specs=[spec for spec, _ in outs],
         scratch_shapes=list(scratch),
-        input_output_aliases=aliases,
         compiler_params=pltpu.CompilerParams(vmem_limit_bytes=vmem * 1024 * 1024),
         cost_estimate=pl.CostEstimate(flops=flops, bytes_accessed=6000000, transcendentals=0),
     )(*[array for _, array in ins])
@@ -252,8 +250,8 @@
         scratch=[env_scratch] * 2
         + [pltpu.VMEM((4, 128), jnp.int32), pltpu.SemaphoreType.DMA((5,))],
     )
-    left_arrived = along_segments(left_own, 1, False)
-    right_arrived = along_segments(right_own, -1, False)
+    left_arrived = along_segments(left_own, 1)
+    right_arrived = along_segments(right_own, -1)
     x_up = hop(b_x, -1, 0)
     x_down = hop(down, 0, 1)
     opp = hop(down, 1, 0)
@@ -274,7 +272,7 @@
     pair_scratch = pltpu.VMEM((2, share, width, width), BF16)
     half_scratch = pltpu.VMEM((share, width, width), BF16)
 
-    def near(wts, sec, lo, la, own, down, up, b_x, lt_out, token, left, lt, *rest):
+    def near(wts, sec, lo, la, ra, own, down, up, b_x, lt_out, token, left, lt, *rest):
         ins, sems, env_sem = rest[:4], rest[4], rest[5]
         first_seg, _ = seg_flags()
         edges = ((first_seg, lo), (jnp.logical_not(first_seg), la))
@@ -297,28 +295,25 @@
         near,
         [(HBM, total), (SMEM, token_shape)],
         [(SMEM, wts), (SMEM, sec)]
-        + [(HBM, a) for a in (left_own, left_arrived, own, down, up, b_x)],
+        + [(HBM, a) for a in (left_own, left_arrived, right_arrived, own, down, up, b_x)],
         scratch=[env_scratch, total_scratch]
         + [half_scratch] * 4
         + [pltpu.SemaphoreType.DMA((4,)), pltpu.SemaphoreType.DMA(())],
         flops=2 * 48 * 2 * 128**3,
     )
 
-    def pick(token, x_down, x_up, lo, ro, out0, out1, lo_out, ro_out, sems):
+    def pick(token, x_down, x_up, out0, out1, sems):
         wait(move([(x_down.at[0], out0), (x_up.at[1], out1)], sems))
 
-    send0, send1, left_own, right_own = call(
+    send0, send1 = call(
         pick,
-        [(VMEM, site_shape), (VMEM, site_shape), (HBM, env), (HBM, env)],
-        [(SMEM, token)] + [(HBM, a) for a in (x_down, x_up, left_own, right_own)],
+        [(VMEM, site_shape), (VMEM, site_shape)],
+        [(SMEM, token), (HBM, x_down), (HBM, x_up)],
         scratch=[pltpu.SemaphoreType.DMA((2,))],
         vmem=4,
-        aliases={3: 2, 4: 3},
     )
     x_opp0 = hop(send0, 1, 0)
     x_opp1 = hop(send1, -1, 0)
-    left_across = along_segments(left_own, 1, True)
-    right_across = along_segments(right_own, -1, True)
 
     def further(wts, sec, lo, la, lt_in, opp, x_down, x_up, lt_out, left, lt, *rest):
         ins, sems = rest[:3], rest[3]
@@ -346,13 +341,11 @@
     slots = (OWN, X_OWN, DOWN, UP, OPP, X_DOWN, X_UP)
     pairs = (own, b_x, down, up, opp, x_down, x_up)
 
-    def last(wts, sizes, sec, order, lo, la, lx, ro, ra, rx, lt_in, late0, late1, *rest):
+    def last(wts, sizes, sec, order, lo, la, ro, ra, lt_in, late0, late1, *rest):
         pairs, rest = rest[: TERMS - 1], rest[TERMS - 1 :]
         left_out, right_out, both, left, right, lt, done_left, done_right = rest[:8]
         blocks0, blocks1, half, sems, late_sems, out_sems = rest[8:]
-        seg, middle = lax.axis_index("seg"), lax.axis_size("seg") // 2
         first_seg, last_seg = seg_flags()
-        left_mid, right_mid = seg == middle, seg == middle - 1
 
         def places(site, blocks):
             refs = [pair.at[site] for pair in pairs]
@@ -361,34 +354,18 @@
 
         first = shard_at(X_OPP) * share
         late = pl.ds(pl.multiple_of(first, share), share)
-        for_left = move([(late0, blocks0.at[late]), (lt_in, lt)], late_sems)
-        plain = jnp.logical_not(jnp.logical_or(first_seg, left_mid))
-        edges = ((first_seg, lo), (left_mid, lx), (plain, la))
-        for_left.append(choose(edges, left, late_sems.at[2]))
-        copies1 = move([(late1, blocks1.at[late])], late_sems.at[pl.ds(3, 1)])
-        plain = jnp.logical_not(jnp.logical_or(last_seg, right_mid))
-        edges = ((last_seg, ro), (right_mid, rx), (plain, ra))
-        copies1.append(choose(edges, right, late_sems.at[4]))
+        edges = ((first_seg, lo), (jnp.logical_not(first_seg), la))
+        for_left = [choose(edges, left, late_sems.at[0])]
+        for_left += move([(late0, blocks0.at[late]), (lt_in, lt)], late_sems.at[pl.ds(1, 2)])
+        edges = ((last_seg, ro), (jnp.logical_not(last_seg), ra))
+        copies1 = [choose(edges, right, late_sems.at[3])]
+        copies1 += move([(late1, blocks1.at[late])], late_sems.at[pl.ds(4, 1)])
         copies1 += move(places(1, blocks1), sems.at[pl.ds(0, TERMS - 1)])
         wait(for_left)
-
-        @pl.when(jnp.logical_not(left_mid))
-        def _():
-            add_left(left, lt, blocks0.at[late], sec, wts, 0, first, share)
-            finish(lt, sizes, left)
-
+        add_left(left, lt, blocks0.at[late], sec, wts, 0, first, share)
+        finish(lt, sizes, left)
         wait(copies1)
         copies0 = move(places(0, blocks0), sems.at[pl.ds(TERMS - 1, TERMS - 1)])
-
-        right_outward(right, blocks1, half, order, wts, 1, UNROLL)
-        right_inward(blocks1, half, keep(right, sizes), order, 1, num, UNROLL)
-        wait(copies0)
-
-        @pl.when(left_mid)
-        def _():
-            left_outward(left, blocks0, half, order, wts, 0, UNROLL)
-            left_inward(blocks0, half, keep(left, sizes), order, 0, num, UNROLL)
-
         sent = []
 
         def sender(done, out, at):
@@ -408,6 +385,9 @@
             blocks1, half, keep(done_left, sizes), order, 1, num, UNROLL,
             cuts, sender(done_left, left_out, 0),
         )
+        right_outward(right, blocks1, half, order, wts, 1, UNROLL)
+        right_inward(blocks1, half, keep(right, sizes), order, 1, num, UNROLL)
+        wait(copies0)
         right_outward(right, blocks0, half, order, wts, 0, UNROLL)
         right_inward(
             blocks0, half, keep(done_right, sizes), order, 0, num, UNROLL,
@@ -420,7 +400,7 @@
         last,
         [(HBM, env), (HBM, env), (HBM, packed)],
         [(SMEM, wts), (SMEM, sector_sizes), (SMEM, sec), (SMEM, order)]
-        + [(HBM, a) for a in (left_own, left_arrived, left_across, right_own, right_arrived, right_across)]
+        + [(HBM, a) for a in (left_own, left_arrived, right_own, right_arrived)]
         + [(HBM, a) for a in (lt, x_opp0, x_opp1)]
         + [(HBM, a) for a in pairs],
         scratch=[env_scratch] * 2
@@ -430,6 +410,7 @@
         + [pltpu.SemaphoreType.DMA((2 * TERMS - 2,))]
         + [pltpu.SemaphoreType.DMA((5,)), pltpu.SemaphoreType.DMA((8,))],
         flops=2 * 300 * 2 * 128**3,
+        vmem=K_VMEM,
     )
     parts = lax.all_to_all(both, "op", 0, 0, tiled=True)
 

time: 109 us -> 108 us (level)
  the two profiles are of different devices: /device:TPU:4 before, /device:TPU:2 now
where the time goes in v3:
time: 108 us; the launch traced here: 107 us
  starting transfers between devices  34.2 us (32%)
  Pallas kernels  26.1 us (24%)
  blocking collectives  22.6 us (21%)
  waiting for transfers between devices  19.9 us (18%)
  local copies, waits for them, and re-layouts  3.13 us (3%)
    ppermute x8, starting transfers between devices, hop(): return lax.ppermute(block, 'op', op_route(dy, dx))  29.9 us
    pallas_call x6, Pallas kernels, call(): pl.pallas_call(body, out_shape=[shape for _, shape in outs], in_specs=[sp...  26.1 us
    all_to_all x1, blocking collectives, local(): parts = lax.all_to_all(both, 'op', 0, 0, tiled=True)  22.6 us
    ppermute x8, waiting for transfers between devices, hop(): return lax.ppermute(block, 'op', op_route(dy, dx))  19.9 us
    ppermute x2, starting transfers between devices, along_segments(): return lax.ppermute(block, 'seg', route)  4.37 us
    unnamed x26, local copies, waits for them, and re-layouts  3.13 us
  transfers between devices with their start and end apart: 10, of which 3 were waited for; matrix products, arithmetic and copies ran while one was open for 0% of the time, Pallas kernels for 13%

profile of v3, /device:TPU:2, one launch (start us, length us, event | category | flops | bytes accessed | tf_op | source)
XLA Modules:
  0.0 106.9 jit_solution(17427597134966513595)
XLA Ops:
  0.6 0.0 copy-start.5
  0.6 0.0 copy-start.6
  0.7 8.0 %collective-permute-start.4 = (bf16[2,12,128,128]{3,2,1,0:T(8,128)(2,1)}, bf16[2,12,128,128]{3,2,1,0:T(8,128)(2,1)S(1)}, u32[]{:S(2)}, u32[]{:S(2)}) collective-permute-start(bf16[2,12,128,128]{3,2,1,0:T(8,128)(2,1)} %rest_0_.1), channel_id=1, source_target_pairs={{0,1},{1,0},{2,3},{3,2},{4,5},{5,4},{6,7},{7,6},{8,9},{9,8},{10,11... | collective-permute-start | bytes 2359304 | tf_op jit(solution)/shard_map/ppermute | solution.py:34
  8.6 1.9 %collective-permute-start.2 = (bf16[2,12,128,128]{3,2,1,0:T(8,128)(2,1)}, bf16[2,12,128,128]{3,2,1,0:T(8,128)(2,1)S(1)}, u32[]{:S(2)}, u32[]{:S(2)}) collective-permute-start(bf16[2,12,128,128]{3,2,1,0:T(8,128)(2,1)} %rest_0_.1), channel_id=1, source_target_pairs={{0,2},{1,3},{2,4},{3,5},{4,6},{5,7},{6,0},{7,1},{8,10},{9,11},{10,... | collective-permute-start | bytes 2359304 | tf_op jit(solution)/shard_map/ppermute | solution.py:34
  10.5 5.1 %collective-permute-start.3 = (bf16[2,12,128,128]{3,2,1,0:T(8,128)(2,1)}, bf16[2,12,128,128]{3,2,1,0:T(8,128)(2,1)S(1)}, u32[]{:S(2)}, u32[]{:S(2)}) collective-permute-start(bf16[2,12,128,128]{3,2,1,0:T(8,128)(2,1)} %rest_0_.1), channel_id=1, source_target_pairs={{0,6},{1,7},{2,0},{3,1},{4,2},{5,3},{6,4},{7,5},{8,14},{9,15},{10,... | collective-permute-start | bytes 2359304 | tf_op jit(solution)/shard_map/ppermute | solution.py:34
  15.7 0.0 copy-start.4
  15.7 0.7 copy-done.4
  16.4 0.7 copy-done.7
  17.0 3.0 %shard_map.93 = (bf16[24,128,128]{2,1,0:T(8,128)(2,1)S(1)}, bf16[24,128,128]{2,1,0:T(8,128)(2,1)S(1)}, s32[4,128]{1,0:T(4,128)S(1)}) custom-call(s32[24]{0:T(128)S(1)} %copy-done.7, s32[2,2,96]{2,1,0:T(2,128)S(1)} %bitcast.7, bf16[24,128,128]{2,1,0:T(8,128)(2,1)} %bitcast.11, bf16[24,128,128]{2,1,0:T(8,128)(2,1)} %bitcast.12), custom_call_target="tpu_custom_call" | custom-call | bytes 6000000 | tf_op jit(solution)/shard_map/pallas_call | solution.py:191
  20.1 0.0 copy-start.3
  20.1 1.3 %collective-permute-start.1 = (bf16[24,128,128]{2,1,0:T(8,128)(2,1)S(1)}, bf16[24,128,128]{2,1,0:T(8,128)(2,1)S(1)}, u32[]{:S(2)}, u32[]{:S(2)}) collective-permute-start(bf16[24,128,128]{2,1,0:T(8,128)(2,1)S(1)} %get-tuple-element.18.ro), channel_id=1, source_target_pairs={{8,0},{16,8},{24,16},{32,24},{40,32},{48,40},{56,48},{64,56},{72,6... | collective-permute-start | bytes 2359304 | tf_op jit(solution)/shard_map/ppermute | solution.py:40
  21.4 3.1 %collective-permute-start = (bf16[24,128,128]{2,1,0:T(8,128)(2,1)S(1)}, bf16[24,128,128]{2,1,0:T(8,128)(2,1)S(1)}, u32[]{:S(2)}, u32[]{:S(2)}) collective-permute-start(bf16[24,128,128]{2,1,0:T(8,128)(2,1)S(1)} %get-tuple-element.17.lo), channel_id=1, source_target_pairs={{0,8},{8,16},{16,24},{24,32},{32,40},{40,48},{48,56},{56,64},{64,7... | collective-permute-start | bytes 2359304 | tf_op jit(solution)/shard_map/ppermute | solution.py:40
  24.5 0.0 collective-permute-done.4.b_x.rest_1_
  24.5 0.0 copy-start.8
  24.5 2.6 %collective-permute-start.7 = (bf16[2,12,128,128]{3,2,1,0:T(8,128)(2,1)S(1)}, bf16[2,12,128,128]{3,2,1,0:T(8,128)(2,1)S(1)}, u32[]{:S(2)}, u32[]{:S(2)}) collective-permute-start(bf16[2,12,128,128]{3,2,1,0:T(8,128)(2,1)S(1)} %collective-permute-done.4.b_x.rest_1_), channel_id=1, source_target_pairs={{0,6},{1,7},{2,0},{3,1},{4,2},{5,3},{6,4},{7,5},{8,14},{9,15},{10,... | collective-permute-start | bytes 2359304 | tf_op jit(solution)/shard_map/ppermute | solution.py:34
  27.1 0.0 collective-permute-done.2.down.rest_2_
  27.1 0.0 copy-start.9
  27.1 2.4 %collective-permute-start.6 = (bf16[2,12,128,128]{3,2,1,0:T(8,128)(2,1)S(1)}, bf16[2,12,128,128]{3,2,1,0:T(8,128)(2,1)S(1)}, u32[]{:S(2)}, u32[]{:S(2)}) collective-permute-start(bf16[2,12,128,128]{3,2,1,0:T(8,128)(2,1)S(1)} %collective-permute-done.2.down.rest_2_), channel_id=1, source_target_pairs={{0,1},{1,0},{2,3},{3,2},{4,5},{5,4},{6,7},{7,6},{8,9},{9,8},{10,11... | collective-permute-start | bytes 2359304 | tf_op jit(solution)/shard_map/ppermute | solution.py:34
  29.6 0.0 collective-permute-done.3.up.rest_3_
  29.6 0.0 copy-start.10
  29.6 2.8 %collective-permute-start.5 = (bf16[2,12,128,128]{3,2,1,0:T(8,128)(2,1)S(1)}, bf16[2,12,128,128]{3,2,1,0:T(8,128)(2,1)S(1)}, u32[]{:S(2)}, u32[]{:S(2)}) collective-permute-start(bf16[2,12,128,128]{3,2,1,0:T(8,128)(2,1)S(1)} %collective-permute-done.2.down.rest_2_), channel_id=1, source_target_pairs={{0,2},{1,3},{2,4},{3,5},{4,6},{5,7},{6,0},{7,1},{8,10},{9,11},{10,... | collective-permute-start | bytes 2359304 | tf_op jit(solution)/shard_map/ppermute | solution.py:34
  32.4 0.0 collective-permute-done.1.ra
  32.4 0.0 copy-start.11
  32.4 0.0 collective-permute-done.la
  32.4 0.0 copy-done.8
  32.4 0.0 copy-done.9
  32.4 0.0 copy-done.10
  32.4 0.9 copy-done.11
  33.3 0.0 copy-done.5
  33.3 0.0 copy-done.6
  33.3 5.3 %shard_map.94 = (f32[24,128,128]{2,1,0:T(8,128)}, s32[1]{0:T(128)}) custom-call(f32[2,1,96]{2,1,0:T(1,128)S(1)} %copy-done.6, s32[2,2,96]{2,1,0:T(2,128)S(1)} %bitcast.8, bf16[24,128,128]{2,1,0:T(8,128)(2,1)S(1)} %get-tuple-element.17.lo, bf16[24,128,128]{2,1,0:T(8,128)(2,1)S(1)} %collective-permute-done.la, bf16[24,128,128]{2,1,0:T(8,128)(2,1)} %copy-done.11, ...), custom_call_target="tpu_custom_call" | custom-call | flops 402653184 | bytes 6000000 | tf_op jit(solution)/shard_map/pallas_call | solution.py:191
  38.6 7.2 %collective-permute-done.7.x_up.rest_6_ = bf16[2,12,128,128]{3,2,1,0:T(8,128)(2,1)S(1)} collective-permute-done((bf16[2,12,128,128]{3,2,1,0:T(8,128)(2,1)S(1)}, bf16[2,12,128,128]{3,2,1,0:T(8,128)(2,1)S(1)}, u32[]{:S(2)}, u32[]{:S(2)}) %collective-permute-start.7) | collective-permute-done | bytes 786464 | tf_op jit(solution)/shard_map/ppermute | solution.py:34
  45.8 10.4 %collective-permute-done.6.x_down.rest_5_ = bf16[2,12,128,128]{3,2,1,0:T(8,128)(2,1)S(1)} collective-permute-done((bf16[2,12,128,128]{3,2,1,0:T(8,128)(2,1)S(1)}, bf16[2,12,128,128]{3,2,1,0:T(8,128)(2,1)S(1)}, u32[]{:S(2)}, u32[]{:S(2)}) %collective-permute-start.6) | collective-permute-done | bytes 786464 | tf_op jit(solution)/shard_map/ppermute | solution.py:34
  56.2 1.0 shard_map.96
  57.2 3.6 %collective-permute-start.8 = (bf16[12,128,128]{2,1,0:T(8,128)(2,1)S(1)}, bf16[12,128,128]{2,1,0:T(8,128)(2,1)S(1)}, u32[]{:S(2)}, u32[]{:S(2)}) collective-permute-start(bf16[12,128,128]{2,1,0:T(8,128)(2,1)S(1)} %get-tuple-element.21), channel_id=1, source_target_pairs={{0,2},{1,3},{2,4},{3,5},{4,6},{5,7},{6,0},{7,1},{8,10},{9,11},{10,... | collective-permute-start | bytes 1179656 | tf_op jit(solution)/shard_map/ppermute | solution.py:34
  60.9 3.4 %collective-permute-start.9 = (bf16[12,128,128]{2,1,0:T(8,128)(2,1)S(1)}, bf16[12,128,128]{2,1,0:T(8,128)(2,1)S(1)}, u32[]{:S(2)}, u32[]{:S(2)}) collective-permute-start(bf16[12,128,128]{2,1,0:T(8,128)(2,1)S(1)} %get-tuple-element.22), channel_id=1, source_target_pairs={{0,6},{1,7},{2,0},{3,1},{4,2},{5,3},{6,4},{7,5},{8,14},{9,15},{10,... | collective-permute-start | bytes 1179656 | tf_op jit(solution)/shard_map/ppermute | solution.py:34
  64.3 0.0 collective-permute-done.5.opp.rest_4_
  64.3 0.0 copy-start.12
  64.3 0.0 copy-done.2
  64.3 0.0 copy-done
  64.3 0.0 copy-done.1
  64.3 0.9 copy-done.12
  65.3 4.8 %shard_map.95.lt_in = f32[24,128,128]{2,1,0:T(8,128)} custom-call(f32[2,1,96]{2,1,0:T(1,128)S(1)} %copy-done.6, s32[2,2,96]{2,1,0:T(2,128)S(1)} %bitcast.9, bf16[24,128,128]{2,1,0:T(8,128)(2,1)S(1)} %get-tuple-element.17.lo, bf16[24,128,128]{2,1,0:T(8,128)(2,1)S(1)} %collective-permute-done.la, f32[24,128,128]{2,1,0:T(8,128)} %get-tuple-element.19.lt_in, ...), custom_call_target="tpu_custom_call" | custom-call | flops 301989888 | bytes 6000000 | tf_op jit(solution)/shard_map/pallas_call | solution.py:191
  70.0 0.0 collective-permute-done.8.late0
  70.0 2.3 %collective-permute-done.9.late1 = bf16[12,128,128]{2,1,0:T(8,128)(2,1)S(1)} collective-permute-done((bf16[12,128,128]{2,1,0:T(8,128)(2,1)S(1)}, bf16[12,128,128]{2,1,0:T(8,128)(2,1)S(1)}, u32[]{:S(2)}, u32[]{:S(2)}) %collective-permute-start.9) | collective-permute-done | bytes 393248 | tf_op jit(solution)/shard_map/ppermute | solution.py:34
  72.3 11.1 %shard_map.97 = (bf16[24,128,128]{2,1,0:T(8,128)(2,1)}, bf16[24,128,128]{2,1,0:T(8,128)(2,1)}, bf16[8,6,128,128]{3,2,1,0:T(8,128)(2,1)}) custom-call(f32[2,1,96]{2,1,0:T(1,128)S(1)} %copy-done.6, s32[24]{0:T(128)S(1)} %copy-done.7, s32[2,2,96]{2,1,0:T(2,128)S(1)} %bitcast.10, s32[4,128]{1,0:T(4,128)S(1)} %get-tuple-element.16.order, ...), custom_call_target="tpu_custom_call" | custom-call | flops 2516582400 | bytes 6000000 | tf_op jit(solution)/shard_map/pallas_call | solution.py:191
  83.4 22.6 %all_to_all.5.parts = bf16[8,6,128,128]{3,2,1,0:T(8,128)(2,1)S(1)} all-to-all(bf16[8,6,128,128]{3,2,1,0:T(8,128)(2,1)} %get-tuple-element.25), channel_id=1, replica_groups=mesh['seg'=64,'op'=8] {'op'}, dimensions={0} | all-to-all | bytes 3145728 | tf_op jit(solution)/shard_map/all_to_all | solution.py:415
  106.0 0.9 shard_map.98
  (5 shorter events, 0.0 us)
Async XLA Ops:
  0.6 32.6 %copy-start.5 = (s32[2,96,2]{1,2,0:T(2,128)S(1)}, s32[2,96,2]{1,2,0:T(2,128)}, u32[]{:S(2)}) copy-start(s32[2,96,2]{1,2,0:T(2,128)} %param.9) | copy-start | bytes 4612
  0.6 32.6 %copy-start.6 = (f32[2,1,96]{2,1,0:T(1,128)S(1)}, f32[2,1,96]{2,1,0:T(1,128)}, u32[]{:S(2)}) copy-start(f32[2,1,96]{2,1,0:T(1,128)} %wts.5) | copy-start | bytes 2308
  0.7 23.8 %collective-permute-start.4 = (bf16[2,12,128,128]{3,2,1,0:T(8,128)(2,1)}, bf16[2,12,128,128]{3,2,1,0:T(8,128)(2,1)S(1)}, u32[]{:S(2)}, u32[]{:S(2)}) collective-permute-start(bf16[2,12,128,128]{3,2,1,0:T(8,128)(2,1)} %rest_0_.1), channel_id=1, source_target_pairs={{0,1},{1,0},{2,3},{3,2},{4,5},{5,4},{6,7},{7,6},{8,9},{9,8},{10,11... | collective-permute-start | bytes 2359304 | tf_op jit(solution)/shard_map/ppermute | solution.py:34
  8.6 18.5 %collective-permute-start.2 = (bf16[2,12,128,128]{3,2,1,0:T(8,128)(2,1)}, bf16[2,12,128,128]{3,2,1,0:T(8,128)(2,1)S(1)}, u32[]{:S(2)}, u32[]{:S(2)}) collective-permute-start(bf16[2,12,128,128]{3,2,1,0:T(8,128)(2,1)} %rest_0_.1), channel_id=1, source_target_pairs={{0,2},{1,3},{2,4},{3,5},{4,6},{5,7},{6,0},{7,1},{8,10},{9,11},{10,... | collective-permute-start | bytes 2359304 | tf_op jit(solution)/shard_map/ppermute | solution.py:34
  10.5 19.0 %collective-permute-start.3 = (bf16[2,12,128,128]{3,2,1,0:T(8,128)(2,1)}, bf16[2,12,128,128]{3,2,1,0:T(8,128)(2,1)S(1)}, u32[]{:S(2)}, u32[]{:S(2)}) collective-permute-start(bf16[2,12,128,128]{3,2,1,0:T(8,128)(2,1)} %rest_0_.1), channel_id=1, source_target_pairs={{0,6},{1,7},{2,0},{3,1},{4,2},{5,3},{6,4},{7,5},{8,14},{9,15},{10,... | collective-permute-start | bytes 2359304 | tf_op jit(solution)/shard_map/ppermute | solution.py:34
  15.7 0.7 copy-start.4
  16.4 0.7 copy-start.7
  20.1 18.5 %copy-start.3 = (bf16[24,128,128]{2,1,0:T(8,128)(2,1)}, bf16[24,128,128]{2,1,0:T(8,128)(2,1)S(1)}, u32[]{:S(2)}) copy-start(bf16[24,128,128]{2,1,0:T(8,128)(2,1)S(1)} %get-tuple-element.18.ro) | copy-start | bytes 2359300
  20.1 12.3 %collective-permute-start.1 = (bf16[24,128,128]{2,1,0:T(8,128)(2,1)S(1)}, bf16[24,128,128]{2,1,0:T(8,128)(2,1)S(1)}, u32[]{:S(2)}, u32[]{:S(2)}) collective-permute-start(bf16[24,128,128]{2,1,0:T(8,128)(2,1)S(1)} %get-tuple-element.18.ro), channel_id=1, source_target_pairs={{8,0},{16,8},{24,16},{32,24},{40,32},{48,40},{56,48},{64,56},{72,6... | collective-permute-start | bytes 2359304 | tf_op jit(solution)/shard_map/ppermute | solution.py:40
  21.4 11.0 %collective-permute-start = (bf16[24,128,128]{2,1,0:T(8,128)(2,1)S(1)}, bf16[24,128,128]{2,1,0:T(8,128)(2,1)S(1)}, u32[]{:S(2)}, u32[]{:S(2)}) collective-permute-start(bf16[24,128,128]{2,1,0:T(8,128)(2,1)S(1)} %get-tuple-element.17.lo), channel_id=1, source_target_pairs={{0,8},{8,16},{16,24},{24,32},{32,40},{40,48},{48,56},{56,64},{64,7... | collective-permute-start | bytes 2359304 | tf_op jit(solution)/shard_map/ppermute | solution.py:40
  24.5 7.9 %copy-start.8 = (bf16[2,12,128,128]{3,2,1,0:T(8,128)(2,1)}, bf16[2,12,128,128]{3,2,1,0:T(8,128)(2,1)S(1)}, u32[]{:S(2)}) copy-start(bf16[2,12,128,128]{3,2,1,0:T(8,128)(2,1)S(1)} %collective-permute-done.4.b_x.rest_1_) | copy-start | bytes 2359300
  24.5 21.3 %collective-permute-start.7 = (bf16[2,12,128,128]{3,2,1,0:T(8,128)(2,1)S(1)}, bf16[2,12,128,128]{3,2,1,0:T(8,128)(2,1)S(1)}, u32[]{:S(2)}, u32[]{:S(2)}) collective-permute-start(bf16[2,12,128,128]{3,2,1,0:T(8,128)(2,1)S(1)} %collective-permute-done.4.b_x.rest_1_), channel_id=1, source_target_pairs={{0,6},{1,7},{2,0},{3,1},{4,2},{5,3},{6,4},{7,5},{8,14},{9,15},{10,... | collective-permute-start | bytes 2359304 | tf_op jit(solution)/shard_map/ppermute | solution.py:34
  27.1 5.3 %copy-start.9 = (bf16[2,12,128,128]{3,2,1,0:T(8,128)(2,1)}, bf16[2,12,128,128]{3,2,1,0:T(8,128)(2,1)S(1)}, u32[]{:S(2)}) copy-start(bf16[2,12,128,128]{3,2,1,0:T(8,128)(2,1)S(1)} %collective-permute-done.2.down.rest_2_) | copy-start | bytes 2359300
  27.1 29.1 %collective-permute-start.6 = (bf16[2,12,128,128]{3,2,1,0:T(8,128)(2,1)S(1)}, bf16[2,12,128,128]{3,2,1,0:T(8,128)(2,1)S(1)}, u32[]{:S(2)}, u32[]{:S(2)}) collective-permute-start(bf16[2,12,128,128]{3,2,1,0:T(8,128)(2,1)S(1)} %collective-permute-done.2.down.rest_2_), channel_id=1, source_target_pairs={{0,1},{1,0},{2,3},{3,2},{4,5},{5,4},{6,7},{7,6},{8,9},{9,8},{10,11... | collective-permute-start | bytes 2359304 | tf_op jit(solution)/shard_map/ppermute | solution.py:34
  29.6 2.8 %copy-start.10 = (bf16[2,12,128,128]{3,2,1,0:T(8,128)(2,1)}, bf16[2,12,128,128]{3,2,1,0:T(8,128)(2,1)S(1)}, u32[]{:S(2)}) copy-start(bf16[2,12,128,128]{3,2,1,0:T(8,128)(2,1)S(1)} %collective-permute-done.3.up.rest_3_) | copy-start | bytes 2359300
  29.6 34.7 %collective-permute-start.5 = (bf16[2,12,128,128]{3,2,1,0:T(8,128)(2,1)S(1)}, bf16[2,12,128,128]{3,2,1,0:T(8,128)(2,1)S(1)}, u32[]{:S(2)}, u32[]{:S(2)}) collective-permute-start(bf16[2,12,128,128]{3,2,1,0:T(8,128)(2,1)S(1)} %collective-permute-done.2.down.rest_2_), channel_id=1, source_target_pairs={{0,2},{1,3},{2,4},{3,5},{4,6},{5,7},{6,0},{7,1},{8,10},{9,11},{10,... | collective-permute-start | bytes 2359304 | tf_op jit(solution)/shard_map/ppermute | solution.py:34
  32.4 0.9 copy-start.11
  33.3 31.0 %copy-start.2 = (bf16[24,128,128]{2,1,0:T(8,128)(2,1)}, bf16[24,128,128]{2,1,0:T(8,128)(2,1)S(1)}, u32[]{:S(2)}) copy-start(bf16[24,128,128]{2,1,0:T(8,128)(2,1)S(1)} %collective-permute-done.la) | copy-start | bytes 2359300
  45.8 18.5 %copy-start = (bf16[2,12,128,128]{3,2,1,0:T(8,128)(2,1)}, bf16[2,12,128,128]{3,2,1,0:T(8,128)(2,1)S(1)}, u32[]{:S(2)}) copy-start(bf16[2,12,128,128]{3,2,1,0:T(8,128)(2,1)S(1)} %collective-permute-done.7.x_up.rest_6_) | copy-start | bytes 2359300
  56.2 8.2 %copy-start.1 = (bf16[2,12,128,128]{3,2,1,0:T(8,128)(2,1)}, bf16[2,12,128,128]{3,2,1,0:T(8,128)(2,1)S(1)}, u32[]{:S(2)}) copy-start(bf16[2,12,128,128]{3,2,1,0:T(8,128)(2,1)S(1)} %collective-permute-done.6.x_down.rest_5_) | copy-start | bytes 2359300
  57.2 12.8 %collective-permute-start.8 = (bf16[12,128,128]{2,1,0:T(8,128)(2,1)S(1)}, bf16[12,128,128]{2,1,0:T(8,128)(2,1)S(1)}, u32[]{:S(2)}, u32[]{:S(2)}) collective-permute-start(bf16[12,128,128]{2,1,0:T(8,128)(2,1)S(1)} %get-tuple-element.21), channel_id=1, source_target_pairs={{0,2},{1,3},{2,4},{3,5},{4,6},{5,7},{6,0},{7,1},{8,10},{9,11},{10,... | collective-permute-start | bytes 1179656 | tf_op jit(solution)/shard_map/ppermute | solution.py:34
  60.9 11.4 %collective-permute-start.9 = (bf16[12,128,128]{2,1,0:T(8,128)(2,1)S(1)}, bf16[12,128,128]{2,1,0:T(8,128)(2,1)S(1)}, u32[]{:S(2)}, u32[]{:S(2)}) collective-permute-start(bf16[12,128,128]{2,1,0:T(8,128)(2,1)S(1)} %get-tuple-element.22), channel_id=1, source_target_pairs={{0,6},{1,7},{2,0},{3,1},{4,2},{5,3},{6,4},{7,5},{8,14},{9,15},{10,... | collective-permute-start | bytes 1179656 | tf_op jit(solution)/shard_map/ppermute | solution.py:34
  64.3 0.9 copy-start.12

commit v4 on v3

--- a/solution.py
+++ b/solution.py
@@ -34,9 +34,16 @@
     return lax.ppermute(block, "op", op_route(dy, dx))
 
 
-def along_segments(block, distance):
-    devices = range(lax.axis_size("seg"))
-    route = [(i - distance, i) for i in devices if i - distance in devices]
+def along_segments(block, step):
+    size = lax.axis_size("seg")
+    middle, end = (size // 2 - 1, 0) if step > 0 else (size // 2, size - 1)
+    route = [(i, i + step) for i in range(size) if i != middle and 0 <= i + step < size]
+    return lax.ppermute(block, "seg", route + [(middle, end)])
+
+
+def from_end(block, step):
+    size = lax.axis_size("seg")
+    route = [(0, size // 2)] if step > 0 else [(size - 1, size // 2 - 1)]
     return lax.ppermute(block, "seg", route)
 
 
@@ -187,13 +194,14 @@
     )(token, *arrays)
 
 
-def call(body, outs, ins, scratch=(), flops=0, vmem=52):
+def call(body, outs, ins, scratch=(), flops=0, vmem=52, aliases={}):
     return pl.pallas_call(
         body,
         out_shape=[shape for _, shape in outs],
         in_specs=[spec for spec, _ in ins],
         out_specs=[spec for spec, _ in outs],
         scratch_shapes=list(scratch),
+        input_output_aliases=aliases,
         compiler_params=pltpu.CompilerParams(vmem_limit_bytes=vmem * 1024 * 1024),
         cost_estimate=pl.CostEstimate(flops=flops, bytes_accessed=6000000, transcendentals=0),
     )(*[array for _, array in ins])
@@ -302,16 +310,19 @@
         flops=2 * 48 * 2 * 128**3,
     )
 
-    def pick(token, x_down, x_up, out0, out1, sems):
+    def pick(token, x_down, x_up, la, ra, out0, out1, la_out, ra_out, sems):
         wait(move([(x_down.at[0], out0), (x_up.at[1], out1)], sems))
 
-    send0, send1 = call(
+    send0, send1, left_arrived, right_arrived = call(
         pick,
-        [(VMEM, site_shape), (VMEM, site_shape)],
-        [(SMEM, token), (HBM, x_down), (HBM, x_up)],
+        [(VMEM, site_shape), (VMEM, site_shape), (HBM, env), (HBM, env)],
+        [(SMEM, token)] + [(HBM, a) for a in (x_down, x_up, left_arrived, right_arrived)],
         scratch=[pltpu.SemaphoreType.DMA((2,))],
         vmem=4,
-    )
+        aliases={3: 2, 4: 3},
+    )
+    left_middle = from_end(left_arrived, 1)
+    right_middle = from_end(right_arrived, -1)
     x_opp0 = hop(send0, 1, 0)
     x_opp1 = hop(send1, -1, 0)
 
@@ -341,7 +352,7 @@
     slots = (OWN, X_OWN, DOWN, UP, OPP, X_DOWN, X_UP)
     pairs = (own, b_x, down, up, opp, x_down, x_up)
 
-    def last(wts, sizes, sec, order, lo, la, ro, ra, lt_in, late0, late1, *rest):
+    def last(wts, sizes, sec, order, lo, la, lm, ro, ra, rm, lt_in, late0, late1, *rest):
         pairs, rest = rest[: TERMS - 1], rest[TERMS - 1 :]
         left_out, right_out, both, left, right, lt, done_left, done_right = rest[:8]
         blocks0, blocks1, half, sems, late_sems, out_sems = rest[8:]
@@ -354,18 +365,33 @@
 
         first = shard_at(X_OPP) * share
         late = pl.ds(pl.multiple_of(first, share), share)
-        edges = ((first_seg, lo), (jnp.logical_not(first_seg), la))
+        left_mid = lax.axis_index("seg") == lax.axis_size("seg") // 2
+        plain = jnp.logical_not(jnp.logical_or(first_seg, left_mid))
+        edges = ((first_seg, lo), (left_mid, lm), (plain, la))
         for_left = [choose(edges, left, late_sems.at[0])]
         for_left += move([(late0, blocks0.at[late]), (lt_in, lt)], late_sems.at[pl.ds(1, 2)])
-        edges = ((last_seg, ro), (jnp.logical_not(last_seg), ra))
+        middle = lax.axis_index("seg") == lax.axis_size("seg") // 2 - 1
+        plain = jnp.logical_not(jnp.logical_or(last_seg, middle))
+        edges = ((last_seg, ro), (middle, rm), (plain, ra))
         copies1 = [choose(edges, right, late_sems.at[3])]
         copies1 += move([(late1, blocks1.at[late])], late_sems.at[pl.ds(4, 1)])
         copies1 += move(places(1, blocks1), sems.at[pl.ds(0, TERMS - 1)])
         wait(for_left)
-        add_left(left, lt, blocks0.at[late], sec, wts, 0, first, share)
-        finish(lt, sizes, left)
+        copies0 = move(places(0, blocks0), sems.at[pl.ds(TERMS - 1, TERMS - 1)])
+
+        @pl.when(jnp.logical_not(left_mid))
+        def _():
+            add_left(left, lt, blocks0.at[late], sec, wts, 0, first, share)
+            finish(lt, sizes, left)
+
+        wait(copies0)
+
+        @pl.when(left_mid)
+        def _():
+            left_outward(left, blocks0, half, order, wts, 0, UNROLL)
+            left_inward(blocks0, half, keep(left, sizes), order, 0, num, UNROLL)
+
         wait(copies1)
-        copies0 = move(places(0, blocks0), sems.at[pl.ds(TERMS - 1, TERMS - 1)])
         sent = []
 
         def sender(done, out, at):
@@ -387,7 +413,6 @@
         )
         right_outward(right, blocks1, half, order, wts, 1, UNROLL)
         right_inward(blocks1, half, keep(right, sizes), order, 1, num, UNROLL)
-        wait(copies0)
         right_outward(right, blocks0, half, order, wts, 0, UNROLL)
         right_inward(
             blocks0, half, keep(done_right, sizes), order, 0, num, UNROLL,
@@ -400,7 +425,7 @@
         last,
         [(HBM, env), (HBM, env), (HBM, packed)],
         [(SMEM, wts), (SMEM, sector_sizes), (SMEM, sec), (SMEM, order)]
-        + [(HBM, a) for a in (left_own, left_arrived, right_own, right_arrived)]
+        + [(HBM, a) for a in (left_own, left_arrived, left_middle, right_own, right_arrived, right_middle)]
         + [(HBM, a) for a in (lt, x_opp0, x_opp1)]
         + [(HBM, a) for a in pairs],
         scratch=[env_scratch] * 2

time: 108 us -> 106 us (0.981)
  the two profiles are of different devices: /device:TPU:2 before, /device:TPU:484 now
where the time goes in v4:
time: 106 us; the launch traced here: 105 us
  starting transfers between devices  34.2 us (32%)
  Pallas kernels  27.1 us (26%)
  blocking collectives  27 us (25%)
  waiting for transfers between devices  12.6 us (12%)
  local copies, waits for them, and re-layouts  3.39 us (3%)
    ppermute x8, starting transfers between devices, hop(): return lax.ppermute(block, 'op', op_route(dy, dx))  28.4 us
    pallas_call x6, Pallas kernels, call(): pl.pallas_call(body, out_shape=[shape for _, shape in outs], in_specs=[sp...  27.1 us
    all_to_all x1, blocking collectives, local(): parts = lax.all_to_all(both, 'op', 0, 0, tiled=True)  27 us
    ppermute x8, waiting for transfers between devices, hop(): return lax.ppermute(block, 'op', op_route(dy, dx))  12.6 us
    ppermute x2, starting transfers between devices, along_segments(): return lax.ppermute(block, 'seg', route + [(middle, end)])  4.33 us
    unnamed x26, local copies, waits for them, and re-layouts  3.39 us
  transfers between devices with their start and end apart: 12, of which 5 were waited for; matrix products, arithmetic and copies ran while one was open for 0% of the time, Pallas kernels for 13%

profile of v4, /device:TPU:484, one launch (start us, length us, event | category | flops | bytes accessed | tf_op | source)
XLA Modules:
  0.0 105.1 jit_solution(9060471485413022094)
XLA Ops:
  0.6 0.0 copy-start.5
  0.6 3.1 %collective-permute-start.4 = (bf16[2,12,128,128]{3,2,1,0:T(8,128)(2,1)}, bf16[2,12,128,128]{3,2,1,0:T(8,128)(2,1)S(1)}, u32[]{:S(2)}, u32[]{:S(2)}) collective-permute-start(bf16[2,12,128,128]{3,2,1,0:T(8,128)(2,1)} %rest_0_.1), channel_id=1, source_target_pairs={{0,1},{1,0},{2,3},{3,2},{4,5},{5,4},{6,7},{7,6},{8,9},{9,8},{10,11... | collective-permute-start | bytes 2359304 | tf_op jit(solution)/shard_map/ppermute | solution.py:34
  3.8 3.5 %collective-permute-start.2 = (bf16[2,12,128,128]{3,2,1,0:T(8,128)(2,1)}, bf16[2,12,128,128]{3,2,1,0:T(8,128)(2,1)S(1)}, u32[]{:S(2)}, u32[]{:S(2)}) collective-permute-start(bf16[2,12,128,128]{3,2,1,0:T(8,128)(2,1)} %rest_0_.1), channel_id=1, source_target_pairs={{0,2},{1,3},{2,4},{3,5},{4,6},{5,7},{6,0},{7,1},{8,10},{9,11},{10,... | collective-permute-start | bytes 2359304 | tf_op jit(solution)/shard_map/ppermute | solution.py:34
  7.3 3.6 %collective-permute-start.3 = (bf16[2,12,128,128]{3,2,1,0:T(8,128)(2,1)}, bf16[2,12,128,128]{3,2,1,0:T(8,128)(2,1)S(1)}, u32[]{:S(2)}, u32[]{:S(2)}) collective-permute-start(bf16[2,12,128,128]{3,2,1,0:T(8,128)(2,1)} %rest_0_.1), channel_id=1, source_target_pairs={{0,6},{1,7},{2,0},{3,1},{4,2},{5,3},{6,4},{7,5},{8,14},{9,15},{10,... | collective-permute-start | bytes 2359304 | tf_op jit(solution)/shard_map/ppermute | solution.py:34
  10.8 0.0 copy-start.4
  10.8 0.7 copy-done.4
  11.5 0.7 copy-done.6
  12.2 3.0 %shard_map.93 = (bf16[24,128,128]{2,1,0:T(8,128)(2,1)S(1)}, bf16[24,128,128]{2,1,0:T(8,128)(2,1)S(1)}, s32[4,128]{1,0:T(4,128)S(1)}) custom-call(s32[24]{0:T(128)S(1)} %copy-done.6, s32[2,2,96]{2,1,0:T(2,128)S(1)} %bitcast.7, bf16[24,128,128]{2,1,0:T(8,128)(2,1)} %bitcast.11, bf16[24,128,128]{2,1,0:T(8,128)(2,1)} %bitcast.12), custom_call_target="tpu_custom_call" | custom-call | bytes 6000000 | tf_op jit(solution)/shard_map/pallas_call | solution.py:198
  15.2 0.0 copy-start.3
  15.2 1.9 %collective-permute-start.1 = (bf16[24,128,128]{2,1,0:T(8,128)(2,1)S(1)}, bf16[24,128,128]{2,1,0:T(8,128)(2,1)}, u32[]{:S(2)}, u32[]{:S(2)}) collective-permute-start(bf16[24,128,128]{2,1,0:T(8,128)(2,1)S(1)} %get-tuple-element.20.ro), channel_id=1, source_target_pairs={{8,0},{16,8},{24,16},{32,24},{40,32},{48,40},{56,48},{64,56},{72,6... | collective-permute-start | bytes 2359304 | tf_op jit(solution)/shard_map/ppermute | solution.py:41
  17.2 2.4 %collective-permute-start = (bf16[24,128,128]{2,1,0:T(8,128)(2,1)S(1)}, bf16[24,128,128]{2,1,0:T(8,128)(2,1)S(1)}, u32[]{:S(2)}, u32[]{:S(2)}) collective-permute-start(bf16[24,128,128]{2,1,0:T(8,128)(2,1)S(1)} %get-tuple-element.19.lo), channel_id=1, source_target_pairs={{0,8},{8,16},{16,24},{24,32},{32,40},{40,48},{48,56},{56,64},{64,7... | collective-permute-start | bytes 2359304 | tf_op jit(solution)/shard_map/ppermute | solution.py:41
  19.6 2.4 %collective-permute-done.4.b_x.rest_1_ = bf16[2,12,128,128]{3,2,1,0:T(8,128)(2,1)S(1)} collective-permute-done((bf16[2,12,128,128]{3,2,1,0:T(8,128)(2,1)}, bf16[2,12,128,128]{3,2,1,0:T(8,128)(2,1)S(1)}, u32[]{:S(2)}, u32[]{:S(2)}) %collective-permute-start.4) | collective-permute-done | bytes 786464 | tf_op jit(solution)/shard_map/ppermute | solution.py:34
  22.0 4.9 %collective-permute-start.6 = (bf16[2,12,128,128]{3,2,1,0:T(8,128)(2,1)S(1)}, bf16[2,12,128,128]{3,2,1,0:T(8,128)(2,1)S(1)}, u32[]{:S(2)}, u32[]{:S(2)}) collective-permute-start(bf16[2,12,128,128]{3,2,1,0:T(8,128)(2,1)S(1)} %collective-permute-done.4.b_x.rest_1_), channel_id=1, source_target_pairs={{0,6},{1,7},{2,0},{3,1},{4,2},{5,3},{6,4},{7,5},{8,14},{9,15},{10,... | collective-permute-start | bytes 2359304 | tf_op jit(solution)/shard_map/ppermute | solution.py:34
  27.0 0.0 collective-permute-done.2.down.rest_2_
  27.0 0.0 copy-start.8
  27.0 3.1 %collective-permute-start.5 = (bf16[2,12,128,128]{3,2,1,0:T(8,128)(2,1)S(1)}, bf16[2,12,128,128]{3,2,1,0:T(8,128)(2,1)S(1)}, u32[]{:S(2)}, u32[]{:S(2)}) collective-permute-start(bf16[2,12,128,128]{3,2,1,0:T(8,128)(2,1)S(1)} %collective-permute-done.2.down.rest_2_), channel_id=1, source_target_pairs={{0,1},{1,0},{2,3},{3,2},{4,5},{5,4},{6,7},{7,6},{8,9},{9,8},{10,11... | collective-permute-start | bytes 2359304 | tf_op jit(solution)/shard_map/ppermute | solution.py:34
  30.1 0.0 collective-permute-done.3.up.rest_3_
  30.1 0.0 copy-start.9
  30.1 3.2 %collective-permute-start.9 = (bf16[2,12,128,128]{3,2,1,0:T(8,128)(2,1)S(1)}, bf16[2,12,128,128]{3,2,1,0:T(8,128)(2,1)S(1)}, u32[]{:S(2)}, u32[]{:S(2)}) collective-permute-start(bf16[2,12,128,128]{3,2,1,0:T(8,128)(2,1)S(1)} %collective-permute-done.2.down.rest_2_), channel_id=1, source_target_pairs={{0,2},{1,3},{2,4},{3,5},{4,6},{5,7},{6,0},{7,1},{8,10},{9,11},{10,... | collective-permute-start | bytes 2359304 | tf_op jit(solution)/shard_map/ppermute | solution.py:34
  33.3 0.0 collective-permute-done.1.ra
  33.3 0.0 collective-permute-done.la
  33.3 0.0 copy-done.7
  33.4 0.0 copy-done.8
  33.4 0.0 copy-done.9
  33.4 0.0 copy-done.5
  33.4 5.2 %shard_map.94 = (f32[24,128,128]{2,1,0:T(8,128)}, s32[1]{0:T(128)}) custom-call(f32[2,1,96]{2,1,0:T(1,128)S(1)} %copy-done.5, s32[2,2,96]{2,1,0:T(2,128)S(1)} %bitcast.8, bf16[24,128,128]{2,1,0:T(8,128)(2,1)S(1)} %get-tuple-element.19.lo, bf16[24,128,128]{2,1,0:T(8,128)(2,1)S(1)} %collective-permute-done.la, ...), custom_call_target="tpu_custom_call" | custom-call | flops 402653184 | bytes 6000000 | tf_op jit(solution)/shard_map/pallas_call | solution.py:198
  38.6 0.0 copy-done.3
  38.6 6.3 %collective-permute-done.6.x_up.rest_6_ = bf16[2,12,128,128]{3,2,1,0:T(8,128)(2,1)S(1)} collective-permute-done((bf16[2,12,128,128]{3,2,1,0:T(8,128)(2,1)S(1)}, bf16[2,12,128,128]{3,2,1,0:T(8,128)(2,1)S(1)}, u32[]{:S(2)}, u32[]{:S(2)}) %collective-permute-start.6) | collective-permute-done | bytes 786464 | tf_op jit(solution)/shard_map/ppermute | solution.py:34
  44.9 2.1 %collective-permute-done.5.x_down.rest_5_ = bf16[2,12,128,128]{3,2,1,0:T(8,128)(2,1)S(1)} collective-permute-done((bf16[2,12,128,128]{3,2,1,0:T(8,128)(2,1)S(1)}, bf16[2,12,128,128]{3,2,1,0:T(8,128)(2,1)S(1)}, u32[]{:S(2)}, u32[]{:S(2)}) %collective-permute-start.5) | collective-permute-done | bytes 786464 | tf_op jit(solution)/shard_map/ppermute | solution.py:34
  47.0 1.0 shard_map.95
  48.0 0.0 copy-done.1
  48.1 0.7 collective-permute-start.8
  48.8 0.7 collective-permute-start.7
  49.5 1.9 %collective-permute-start.10 = (bf16[12,128,128]{2,1,0:T(8,128)(2,1)S(1)}, bf16[12,128,128]{2,1,0:T(8,128)(2,1)S(1)}, u32[]{:S(2)}, u32[]{:S(2)}) collective-permute-start(bf16[12,128,128]{2,1,0:T(8,128)(2,1)S(1)} %get-tuple-element.25), channel_id=1, source_target_pairs={{0,2},{1,3},{2,4},{3,5},{4,6},{5,7},{6,0},{7,1},{8,10},{9,11},{10,... | collective-permute-start | bytes 1179656 | tf_op jit(solution)/shard_map/ppermute | solution.py:34
  51.4 5.1 %collective-permute-start.11 = (bf16[12,128,128]{2,1,0:T(8,128)(2,1)S(1)}, bf16[12,128,128]{2,1,0:T(8,128)(2,1)S(1)}, u32[]{:S(2)}, u32[]{:S(2)}) collective-permute-start(bf16[12,128,128]{2,1,0:T(8,128)(2,1)S(1)} %get-tuple-element.26), channel_id=1, source_target_pairs={{0,6},{1,7},{2,0},{3,1},{4,2},{5,3},{6,4},{7,5},{8,14},{9,15},{10,... | collective-permute-start | bytes 1179656 | tf_op jit(solution)/shard_map/ppermute | solution.py:34
  56.6 0.0 collective-permute-done.9.opp.rest_4_
  56.6 0.0 copy-start.10
  56.6 0.9 copy-done.10
  57.5 4.8 %shard_map.96.lt_in = f32[24,128,128]{2,1,0:T(8,128)} custom-call(f32[2,1,96]{2,1,0:T(1,128)S(1)} %copy-done.5, s32[2,2,96]{2,1,0:T(2,128)S(1)} %bitcast.9, bf16[24,128,128]{2,1,0:T(8,128)(2,1)S(1)} %get-tuple-element.19.lo, bf16[24,128,128]{2,1,0:T(8,128)(2,1)S(1)} %get-tuple-element.22.la, f32[24,128,128]{2,1,0:T(8,128)} %get-tuple-element.24.lt_in, ...), custom_call_target="tpu_custom_call" | custom-call | flops 301989888 | bytes 6000000 | tf_op jit(solution)/shard_map/pallas_call | solution.py:198
  62.3 0.6 collective-permute-done.10.late0
  62.9 1.2 %collective-permute-done.11.late1 = bf16[12,128,128]{2,1,0:T(8,128)(2,1)S(1)} collective-permute-done((bf16[12,128,128]{2,1,0:T(8,128)(2,1)S(1)}, bf16[12,128,128]{2,1,0:T(8,128)(2,1)S(1)}, u32[]{:S(2)}, u32[]{:S(2)}) %collective-permute-start.11) | collective-permute-done | bytes 393248 | tf_op jit(solution)/shard_map/ppermute | solution.py:34
  64.0 0.0 collective-permute-done.8.rm
  64.1 0.0 collective-permute-done.7.lm
  64.1 0.9 copy-done.11
  65.0 0.2 copy-done.12
  65.2 12.1 %shard_map.97 = (bf16[24,128,128]{2,1,0:T(8,128)(2,1)}, bf16[24,128,128]{2,1,0:T(8,128)(2,1)}, bf16[8,6,128,128]{3,2,1,0:T(8,128)(2,1)}) custom-call(f32[2,1,96]{2,1,0:T(1,128)S(1)} %copy-done.5, s32[24]{0:T(128)S(1)} %copy-done.6, s32[2,2,96]{2,1,0:T(2,128)S(1)} %bitcast.10, s32[4,128]{1,0:T(4,128)S(1)} %get-tuple-element.18.order, ...), custom_call_target="tpu_custom_call" | custom-call | flops 2516582400 | bytes 6000000 | tf_op jit(solution)/shard_map/pallas_call | solution.py:198
  77.3 27.0 %all_to_all.5.parts = bf16[8,6,128,128]{3,2,1,0:T(8,128)(2,1)S(1)} all-to-all(bf16[8,6,128,128]{3,2,1,0:T(8,128)(2,1)} %get-tuple-element.29), channel_id=1, replica_groups=mesh['seg'=64,'op'=8] {'op'}, dimensions={0} | all-to-all | bytes 3145728 | tf_op jit(solution)/shard_map/all_to_all | solution.py:440
  104.2 0.9 shard_map.98
  (9 shorter events, 0.0 us)
Async XLA Ops:
  0.6 32.7 %copy-start.5 = (f32[2,1,96]{2,1,0:T(1,128)S(1)}, f32[2,1,96]{2,1,0:T(1,128)}, u32[]{:S(2)}) copy-start(f32[2,1,96]{2,1,0:T(1,128)} %wts.5) | copy-start | bytes 2308
  0.6 21.4 %collective-permute-start.4 = (bf16[2,12,128,128]{3,2,1,0:T(8,128)(2,1)}, bf16[2,12,128,128]{3,2,1,0:T(8,128)(2,1)S(1)}, u32[]{:S(2)}, u32[]{:S(2)}) collective-permute-start(bf16[2,12,128,128]{3,2,1,0:T(8,128)(2,1)} %rest_0_.1), channel_id=1, source_target_pairs={{0,1},{1,0},{2,3},{3,2},{4,5},{5,4},{6,7},{7,6},{8,9},{9,8},{10,11... | collective-permute-start | bytes 2359304 | tf_op jit(solution)/shard_map/ppermute | solution.py:34
  3.8 23.2 %collective-permute-start.2 = (bf16[2,12,128,128]{3,2,1,0:T(8,128)(2,1)}, bf16[2,12,128,128]{3,2,1,0:T(8,128)(2,1)S(1)}, u32[]{:S(2)}, u32[]{:S(2)}) collective-permute-start(bf16[2,12,128,128]{3,2,1,0:T(8,128)(2,1)} %rest_0_.1), channel_id=1, source_target_pairs={{0,2},{1,3},{2,4},{3,5},{4,6},{5,7},{6,0},{7,1},{8,10},{9,11},{10,... | collective-permute-start | bytes 2359304 | tf_op jit(solution)/shard_map/ppermute | solution.py:34
  7.3 22.8 %collective-permute-start.3 = (bf16[2,12,128,128]{3,2,1,0:T(8,128)(2,1)}, bf16[2,12,128,128]{3,2,1,0:T(8,128)(2,1)S(1)}, u32[]{:S(2)}, u32[]{:S(2)}) collective-permute-start(bf16[2,12,128,128]{3,2,1,0:T(8,128)(2,1)} %rest_0_.1), channel_id=1, source_target_pairs={{0,6},{1,7},{2,0},{3,1},{4,2},{5,3},{6,4},{7,5},{8,14},{9,15},{10,... | collective-permute-start | bytes 2359304 | tf_op jit(solution)/shard_map/ppermute | solution.py:34
  10.8 0.7 copy-start.4
  11.5 0.7 copy-start.6
  15.2 23.4 %copy-start.3 = (bf16[24,128,128]{2,1,0:T(8,128)(2,1)}, bf16[24,128,128]{2,1,0:T(8,128)(2,1)S(1)}, u32[]{:S(2)}) copy-start(bf16[24,128,128]{2,1,0:T(8,128)(2,1)S(1)} %get-tuple-element.20.ro) | copy-start | bytes 2359300
  15.2 18.1 %collective-permute-start.1 = (bf16[24,128,128]{2,1,0:T(8,128)(2,1)S(1)}, bf16[24,128,128]{2,1,0:T(8,128)(2,1)}, u32[]{:S(2)}, u32[]{:S(2)}) collective-permute-start(bf16[24,128,128]{2,1,0:T(8,128)(2,1)S(1)} %get-tuple-element.20.ro), channel_id=1, source_target_pairs={{8,0},{16,8},{24,16},{32,24},{40,32},{48,40},{56,48},{64,56},{72,6... | collective-permute-start | bytes 2359304 | tf_op jit(solution)/shard_map/ppermute | solution.py:41
  17.2 16.2 %collective-permute-start = (bf16[24,128,128]{2,1,0:T(8,128)(2,1)S(1)}, bf16[24,128,128]{2,1,0:T(8,128)(2,1)S(1)}, u32[]{:S(2)}, u32[]{:S(2)}) collective-permute-start(bf16[24,128,128]{2,1,0:T(8,128)(2,1)S(1)} %get-tuple-element.19.lo), channel_id=1, source_target_pairs={{0,8},{8,16},{16,24},{24,32},{32,40},{40,48},{48,56},{56,64},{64,7... | collective-permute-start | bytes 2359304 | tf_op jit(solution)/shard_map/ppermute | solution.py:41
  22.0 11.3 %copy-start.7 = (bf16[2,12,128,128]{3,2,1,0:T(8,128)(2,1)}, bf16[2,12,128,128]{3,2,1,0:T(8,128)(2,1)S(1)}, u32[]{:S(2)}) copy-start(bf16[2,12,128,128]{3,2,1,0:T(8,128)(2,1)S(1)} %collective-permute-done.4.b_x.rest_1_) | copy-start | bytes 2359300
  22.0 22.9 %collective-permute-start.6 = (bf16[2,12,128,128]{3,2,1,0:T(8,128)(2,1)S(1)}, bf16[2,12,128,128]{3,2,1,0:T(8,128)(2,1)S(1)}, u32[]{:S(2)}, u32[]{:S(2)}) collective-permute-start(bf16[2,12,128,128]{3,2,1,0:T(8,128)(2,1)S(1)} %collective-permute-done.4.b_x.rest_1_), channel_id=1, source_target_pairs={{0,6},{1,7},{2,0},{3,1},{4,2},{5,3},{6,4},{7,5},{8,14},{9,15},{10,... | collective-permute-start | bytes 2359304 | tf_op jit(solution)/shard_map/ppermute | solution.py:34
  27.0 6.4 %copy-start.8 = (bf16[2,12,128,128]{3,2,1,0:T(8,128)(2,1)}, bf16[2,12,128,128]{3,2,1,0:T(8,128)(2,1)S(1)}, u32[]{:S(2)}) copy-start(bf16[2,12,128,128]{3,2,1,0:T(8,128)(2,1)S(1)} %collective-permute-done.2.down.rest_2_) | copy-start | bytes 2359300
  27.0 20.0 %collective-permute-start.5 = (bf16[2,12,128,128]{3,2,1,0:T(8,128)(2,1)S(1)}, bf16[2,12,128,128]{3,2,1,0:T(8,128)(2,1)S(1)}, u32[]{:S(2)}, u32[]{:S(2)}) collective-permute-start(bf16[2,12,128,128]{3,2,1,0:T(8,128)(2,1)S(1)} %collective-permute-done.2.down.rest_2_), channel_id=1, source_target_pairs={{0,1},{1,0},{2,3},{3,2},{4,5},{5,4},{6,7},{7,6},{8,9},{9,8},{10,11... | collective-permute-start | bytes 2359304 | tf_op jit(solution)/shard_map/ppermute | solution.py:34
  30.1 3.3 %copy-start.9 = (bf16[2,12,128,128]{3,2,1,0:T(8,128)(2,1)}, bf16[2,12,128,128]{3,2,1,0:T(8,128)(2,1)S(1)}, u32[]{:S(2)}) copy-start(bf16[2,12,128,128]{3,2,1,0:T(8,128)(2,1)S(1)} %collective-permute-done.3.up.rest_3_) | copy-start | bytes 2359300
  30.1 26.5 %collective-permute-start.9 = (bf16[2,12,128,128]{3,2,1,0:T(8,128)(2,1)S(1)}, bf16[2,12,128,128]{3,2,1,0:T(8,128)(2,1)S(1)}, u32[]{:S(2)}, u32[]{:S(2)}) collective-permute-start(bf16[2,12,128,128]{3,2,1,0:T(8,128)(2,1)S(1)} %collective-permute-done.2.down.rest_2_), channel_id=1, source_target_pairs={{0,2},{1,3},{2,4},{3,5},{4,6},{5,7},{6,0},{7,1},{8,10},{9,11},{10,... | collective-permute-start | bytes 2359304 | tf_op jit(solution)/shard_map/ppermute | solution.py:34
  44.9 3.1 %copy-start.1 = (bf16[2,12,128,128]{3,2,1,0:T(8,128)(2,1)}, bf16[2,12,128,128]{3,2,1,0:T(8,128)(2,1)S(1)}, u32[]{:S(2)}) copy-start(bf16[2,12,128,128]{3,2,1,0:T(8,128)(2,1)S(1)} %collective-permute-done.6.x_up.rest_6_) | copy-start | bytes 2359300
  47.0 1.1 %copy-start.2 = (bf16[2,12,128,128]{3,2,1,0:T(8,128)(2,1)}, bf16[2,12,128,128]{3,2,1,0:T(8,128)(2,1)S(1)}, u32[]{:S(2)}) copy-start(bf16[2,12,128,128]{3,2,1,0:T(8,128)(2,1)S(1)} %collective-permute-done.5.x_down.rest_5_) | copy-start | bytes 2359300
  48.1 14.2 %copy-start = (bf16[24,128,128]{2,1,0:T(8,128)(2,1)}, bf16[24,128,128]{2,1,0:T(8,128)(2,1)S(1)}, u32[]{:S(2)}) copy-start(bf16[24,128,128]{2,1,0:T(8,128)(2,1)S(1)} %get-tuple-element.22.la) | copy-start | bytes 2359300
  48.1 16.0 %collective-permute-start.8 = (bf16[24,128,128]{2,1,0:T(8,128)(2,1)}, bf16[24,128,128]{2,1,0:T(8,128)(2,1)S(1)}, u32[]{:S(2)}, u32[]{:S(2)}) collective-permute-start(bf16[24,128,128]{2,1,0:T(8,128)(2,1)} %get-tuple-element.23.ra), channel_id=1, source_target_pairs={{504,248},{505,249},{506,250},{507,251},{508,252},{509,253},{510,2... | collective-permute-start | bytes 2359304 | tf_op jit(solution)/shard_map/ppermute | solution.py:47
  48.8 15.3 %collective-permute-start.7 = (bf16[24,128,128]{2,1,0:T(8,128)(2,1)S(1)}, bf16[24,128,128]{2,1,0:T(8,128)(2,1)S(1)}, u32[]{:S(2)}, u32[]{:S(2)}) collective-permute-start(bf16[24,128,128]{2,1,0:T(8,128)(2,1)S(1)} %get-tuple-element.22.la), channel_id=1, source_target_pairs={{0,256},{1,257},{2,258},{3,259},{4,260},{5,261},{6,262},{7,263}} | collective-permute-start | bytes 2359304 | tf_op jit(solution)/shard_map/ppermute | solution.py:47
  49.5 13.4 %collective-permute-start.10 = (bf16[12,128,128]{2,1,0:T(8,128)(2,1)S(1)}, bf16[12,128,128]{2,1,0:T(8,128)(2,1)S(1)}, u32[]{:S(2)}, u32[]{:S(2)}) collective-permute-start(bf16[12,128,128]{2,1,0:T(8,128)(2,1)S(1)} %get-tuple-element.25), channel_id=1, source_target_pairs={{0,2},{1,3},{2,4},{3,5},{4,6},{5,7},{6,0},{7,1},{8,10},{9,11},{10,... | collective-permute-start | bytes 1179656 | tf_op jit(solution)/shard_map/ppermute | solution.py:34
  51.4 12.6 %collective-permute-start.11 = (bf16[12,128,128]{2,1,0:T(8,128)(2,1)S(1)}, bf16[12,128,128]{2,1,0:T(8,128)(2,1)S(1)}, u32[]{:S(2)}, u32[]{:S(2)}) collective-permute-start(bf16[12,128,128]{2,1,0:T(8,128)(2,1)S(1)} %get-tuple-element.26), channel_id=1, source_target_pairs={{0,6},{1,7},{2,0},{3,1},{4,2},{5,3},{6,4},{7,5},{8,14},{9,15},{10,... | collective-permute-start | bytes 1179656 | tf_op jit(solution)/shard_map/ppermute | solution.py:34
  56.6 0.9 copy-start.10
  64.1 0.9 copy-start.11
  64.1 1.1 %copy-start.12 = (bf16[24,128,128]{2,1,0:T(8,128)(2,1)}, bf16[24,128,128]{2,1,0:T(8,128)(2,1)S(1)}, u32[]{:S(2)}) copy-start(bf16[24,128,128]{2,1,0:T(8,128)(2,1)S(1)} %collective-permute-done.7.lm) | copy-start | bytes 2359300

commit v5 on v4

--- a/solution.py
+++ b/solution.py
@@ -14,7 +14,7 @@
 TERMS = NY * NX
 PER_SECTOR = 4
 UNROLL = 12
-K_VMEM = 52
+K_VMEM = 48
 NN = (((1,), (0,)), ((), ()))
 TN = (((0,), (0,)), ((), ()))
 NT = (((1,), (1,)), ((), ()))
@@ -41,10 +41,9 @@
     return lax.ppermute(block, "seg", route + [(middle, end)])
 
 
-def from_end(block, step):
+def from_ends(block):
     size = lax.axis_size("seg")
-    route = [(0, size // 2)] if step > 0 else [(size - 1, size // 2 - 1)]
-    return lax.ppermute(block, "seg", route)
+    return lax.ppermute(block, "seg", [(0, size // 2), (size - 1, size // 2 - 1)])
 
 
 def live(sizes, sector, width):
@@ -194,14 +193,13 @@
     )(token, *arrays)
 
 
-def call(body, outs, ins, scratch=(), flops=0, vmem=52, aliases={}):
+def call(body, outs, ins, scratch=(), flops=0, vmem=48):
     return pl.pallas_call(
         body,
         out_shape=[shape for _, shape in outs],
         in_specs=[spec for spec, _ in ins],
         out_specs=[spec for spec, _ in outs],
         scratch_shapes=list(scratch),
-        input_output_aliases=aliases,
         compiler_params=pltpu.CompilerParams(vmem_limit_bytes=vmem * 1024 * 1024),
         cost_estimate=pl.CostEstimate(flops=flops, bytes_accessed=6000000, transcendentals=0),
     )(*[array for _, array in ins])
@@ -310,19 +308,25 @@
         flops=2 * 48 * 2 * 128**3,
     )
 
-    def pick(token, x_down, x_up, la, ra, out0, out1, la_out, ra_out, sems):
-        wait(move([(x_down.at[0], out0), (x_up.at[1], out1)], sems))
-
-    send0, send1, left_arrived, right_arrived = call(
+    def pick(token, x_down, x_up, la, ra, out0, out1, passing, sems):
+        first_seg, last_seg = seg_flags()
+        coming = move([(x_down.at[0], out0), (x_up.at[1], out1)], sems.at[pl.ds(0, 2)])
+        for flag, source in ((first_seg, la), (last_seg, ra)):
+
+            @pl.when(flag)
+            def _():
+                wait(move([(source, passing)], sems.at[pl.ds(2, 1)]))
+
+        wait(coming)
+
+    send0, send1, passing = call(
         pick,
-        [(VMEM, site_shape), (VMEM, site_shape), (HBM, env), (HBM, env)],
+        [(VMEM, site_shape), (VMEM, site_shape), (VMEM, env)],
         [(SMEM, token)] + [(HBM, a) for a in (x_down, x_up, left_arrived, right_arrived)],
-        scratch=[pltpu.SemaphoreType.DMA((2,))],
+        scratch=[pltpu.SemaphoreType.DMA((3,))],
         vmem=4,
-        aliases={3: 2, 4: 3},
-    )
-    left_middle = from_end(left_arrived, 1)
-    right_middle = from_end(right_arrived, -1)
+    )
+    env_middle = from_ends(passing)
     x_opp0 = hop(send0, 1, 0)
     x_opp1 = hop(send1, -1, 0)
 
@@ -352,7 +356,7 @@
     slots = (OWN, X_OWN, DOWN, UP, OPP, X_DOWN, X_UP)
     pairs = (own, b_x, down, up, opp, x_down, x_up)
 
-    def last(wts, sizes, sec, order, lo, la, lm, ro, ra, rm, lt_in, late0, late1, *rest):
+    def last(wts, sizes, sec, order, lo, la, ro, ra, mid, lt_in, late0, late1, *rest):
         pairs, rest = rest[: TERMS - 1], rest[TERMS - 1 :]
         left_out, right_out, both, left, right, lt, done_left, done_right = rest[:8]
         blocks0, blocks1, half, sems, late_sems, out_sems = rest[8:]
@@ -367,31 +371,31 @@
         late = pl.ds(pl.multiple_of(first, share), share)
         left_mid = lax.axis_index("seg") == lax.axis_size("seg") // 2
         plain = jnp.logical_not(jnp.logical_or(first_seg, left_mid))
-        edges = ((first_seg, lo), (left_mid, lm), (plain, la))
+        edges = ((first_seg, lo), (left_mid, mid), (plain, la))
         for_left = [choose(edges, left, late_sems.at[0])]
         for_left += move([(late0, blocks0.at[late]), (lt_in, lt)], late_sems.at[pl.ds(1, 2)])
         middle = lax.axis_index("seg") == lax.axis_size("seg") // 2 - 1
         plain = jnp.logical_not(jnp.logical_or(last_seg, middle))
-        edges = ((last_seg, ro), (middle, rm), (plain, ra))
+        edges = ((last_seg, ro), (middle, mid), (plain, ra))
         copies1 = [choose(edges, right, late_sems.at[3])]
         copies1 += move([(late1, blocks1.at[late])], late_sems.at[pl.ds(4, 1)])
         copies1 += move(places(1, blocks1), sems.at[pl.ds(0, TERMS - 1)])
         wait(for_left)
-        copies0 = move(places(0, blocks0), sems.at[pl.ds(TERMS - 1, TERMS - 1)])
 
         @pl.when(jnp.logical_not(left_mid))
         def _():
             add_left(left, lt, blocks0.at[late], sec, wts, 0, first, share)
             finish(lt, sizes, left)
 
-        wait(copies0)
+        wait(copies1)
+        copies0 = move(places(0, blocks0), sems.at[pl.ds(TERMS - 1, TERMS - 1)])
 
         @pl.when(left_mid)
         def _():
+            wait(copies0)
             left_outward(left, blocks0, half, order, wts, 0, UNROLL)
             left_inward(blocks0, half, keep(left, sizes), order, 0, num, UNROLL)
 
-        wait(copies1)
         sent = []
 
         def sender(done, out, at):
@@ -413,6 +417,11 @@
         )
         right_outward(right, blocks1, half, order, wts, 1, UNROLL)
         right_inward(blocks1, half, keep(right, sizes), order, 1, num, UNROLL)
+
+        @pl.when(jnp.logical_not(left_mid))
+        def _():
+            wait(copies0)
+
         right_outward(right, blocks0, half, order, wts, 0, UNROLL)
         right_inward(
             blocks0, half, keep(done_right, sizes), order, 0, num, UNROLL,
@@ -425,7 +434,7 @@
         last,
         [(HBM, env), (HBM, env), (HBM, packed)],
         [(SMEM, wts), (SMEM, sector_sizes), (SMEM, sec), (SMEM, order)]
-        + [(HBM, a) for a in (left_own, left_arrived, left_middle, right_own, right_arrived, right_middle)]
+        + [(HBM, a) for a in (left_own, left_arrived, right_own, right_arrived, env_middle)]
         + [(HBM, a) for a in (lt, x_opp0, x_opp1)]
         + [(HBM, a) for a in pairs],
         scratch=[env_scratch] * 2

time: 106 us -> 104 us (0.981)
  the two profiles are of different devices: /device:TPU:484 before, /device:TPU:96 now
where the time goes in v5:
time: 104 us; the launch traced here: 103 us
  starting transfers between devices  33.3 us (32%)
  blocking collectives  25.2 us (24%)
  Pallas kernels  24.1 us (23%)
  waiting for transfers between devices  14.8 us (14%)
  local copies, waits for them, and re-layouts  4.79 us (5%)
    ppermute x8, starting transfers between devices, hop(): return lax.ppermute(block, 'op', op_route(dy, dx))  28.3 us
    all_to_all x1, blocking collectives, local(): parts = lax.all_to_all(both, 'op', 0, 0, tiled=True)  25.2 us
    pallas_call x6, Pallas kernels, call(): pl.pallas_call(body, out_shape=[shape for _, shape in outs], in_specs=[sp...  24.1 us
    ppermute x8, waiting for transfers between devices, hop(): return lax.ppermute(block, 'op', op_route(dy, dx))  14.8 us
    unnamed x26, local copies, waits for them, and re-layouts  4.79 us
    ppermute x2, starting transfers between devices, along_segments(): return lax.ppermute(block, 'seg', route + [(middle, end)])  4.33 us
  transfers between devices with their start and end apart: 11, of which 5 were waited for; matrix products, arithmetic and copies ran while one was open for 0% of the time, Pallas kernels for 12%

profile of v5, /device:TPU:96, one launch (start us, length us, event | category | flops | bytes accessed | tf_op | source)
XLA Modules:
  0.0 103.1 jit_solution(7428332567367307166)
XLA Ops:
  0.6 0.0 copy-start.3
  0.6 3.5 %collective-permute-start.4 = (bf16[2,12,128,128]{3,2,1,0:T(8,128)(2,1)}, bf16[2,12,128,128]{3,2,1,0:T(8,128)(2,1)S(1)}, u32[]{:S(2)}, u32[]{:S(2)}) collective-permute-start(bf16[2,12,128,128]{3,2,1,0:T(8,128)(2,1)} %rest_0_.1), channel_id=1, source_target_pairs={{0,1},{1,0},{2,3},{3,2},{4,5},{5,4},{6,7},{7,6},{8,9},{9,8},{10,11... | collective-permute-start | bytes 2359304 | tf_op jit(solution)/shard_map/ppermute | solution.py:34
  4.2 3.5 %collective-permute-start.2 = (bf16[2,12,128,128]{3,2,1,0:T(8,128)(2,1)}, bf16[2,12,128,128]{3,2,1,0:T(8,128)(2,1)S(1)}, u32[]{:S(2)}, u32[]{:S(2)}) collective-permute-start(bf16[2,12,128,128]{3,2,1,0:T(8,128)(2,1)} %rest_0_.1), channel_id=1, source_target_pairs={{0,2},{1,3},{2,4},{3,5},{4,6},{5,7},{6,0},{7,1},{8,10},{9,11},{10,... | collective-permute-start | bytes 2359304 | tf_op jit(solution)/shard_map/ppermute | solution.py:34
  7.7 3.6 %collective-permute-start.3 = (bf16[2,12,128,128]{3,2,1,0:T(8,128)(2,1)}, bf16[2,12,128,128]{3,2,1,0:T(8,128)(2,1)S(1)}, u32[]{:S(2)}, u32[]{:S(2)}) collective-permute-start(bf16[2,12,128,128]{3,2,1,0:T(8,128)(2,1)} %rest_0_.1), channel_id=1, source_target_pairs={{0,6},{1,7},{2,0},{3,1},{4,2},{5,3},{6,4},{7,5},{8,14},{9,15},{10,... | collective-permute-start | bytes 2359304 | tf_op jit(solution)/shard_map/ppermute | solution.py:34
  11.2 0.0 copy-start.8
  11.3 1.1 %copy-done.8 = bf16[1,1,24,128,128]{4,3,2,1,0:T(8,128)(2,1)S(1)} copy-done((bf16[1,1,24,128,128]{4,3,2,1,0:T(8,128)(2,1)S(1)}, bf16[1,1,24,128,128]{4,3,2,1,0:T(8,128)(2,1)}, u32[]{:S(2)}) %copy-start.8) | copy-done | bytes 786456
  12.4 1.1 %copy-done.9 = bf16[1,1,24,128,128]{4,3,2,1,0:T(8,128)(2,1)S(1)} copy-done((bf16[1,1,24,128,128]{4,3,2,1,0:T(8,128)(2,1)S(1)}, bf16[1,1,24,128,128]{4,3,2,1,0:T(8,128)(2,1)}, u32[]{:S(2)}) %copy-start.9) | copy-done | bytes 786456
  13.5 0.7 copy-done.10
  14.2 0.7 copy-done.12
  14.9 2.3 %shard_map.93 = (bf16[24,128,128]{2,1,0:T(8,128)(2,1)S(1)}, bf16[24,128,128]{2,1,0:T(8,128)(2,1)S(1)}, s32[4,128]{1,0:T(4,128)S(1)}) custom-call(s32[24]{0:T(128)S(1)} %copy-done.12, s32[2,2,96]{2,1,0:T(2,128)S(1)} %bitcast.9, bf16[24,128,128]{2,1,0:T(8,128)(2,1)S(1)} %bitcast.7, bf16[24,128,128]{2,1,0:T(8,128)(2,1)S(1)} %bitcast.8), custom_call_target="tpu_custom_call" | custom-call | bytes 6000000 | tf_op jit(solution)/shard_map/pallas_call | solution.py:197
  17.2 1.9 %collective-permute-start.1 = (bf16[24,128,128]{2,1,0:T(8,128)(2,1)S(1)}, bf16[24,128,128]{2,1,0:T(8,128)(2,1)S(1)}, u32[]{:S(2)}, u32[]{:S(2)}) collective-permute-start(bf16[24,128,128]{2,1,0:T(8,128)(2,1)S(1)} %get-tuple-element.19.ro), channel_id=1, source_target_pairs={{8,0},{16,8},{24,16},{32,24},{40,32},{48,40},{56,48},{64,56},{72,6... | collective-permute-start | bytes 2359304 | tf_op jit(solution)/shard_map/ppermute | solution.py:41
  19.1 2.4 %collective-permute-start = (bf16[24,128,128]{2,1,0:T(8,128)(2,1)S(1)}, bf16[24,128,128]{2,1,0:T(8,128)(2,1)S(1)}, u32[]{:S(2)}, u32[]{:S(2)}) collective-permute-start(bf16[24,128,128]{2,1,0:T(8,128)(2,1)S(1)} %get-tuple-element.18.lo), channel_id=1, source_target_pairs={{0,8},{8,16},{16,24},{24,32},{32,40},{40,48},{48,56},{56,64},{64,7... | collective-permute-start | bytes 2359304 | tf_op jit(solution)/shard_map/ppermute | solution.py:41
  21.5 0.6 collective-permute-done.4.b_x.rest_1_
  22.2 4.9 %collective-permute-start.6 = (bf16[2,12,128,128]{3,2,1,0:T(8,128)(2,1)S(1)}, bf16[2,12,128,128]{3,2,1,0:T(8,128)(2,1)S(1)}, u32[]{:S(2)}, u32[]{:S(2)}) collective-permute-start(bf16[2,12,128,128]{3,2,1,0:T(8,128)(2,1)S(1)} %collective-permute-done.4.b_x.rest_1_), channel_id=1, source_target_pairs={{0,6},{1,7},{2,0},{3,1},{4,2},{5,3},{6,4},{7,5},{8,14},{9,15},{10,... | collective-permute-start | bytes 2359304 | tf_op jit(solution)/shard_map/ppermute | solution.py:34
  27.1 0.0 collective-permute-done.2.down.rest_2_
  27.1 0.0 copy-start.5
  27.1 3.4 %collective-permute-start.5 = (bf16[2,12,128,128]{3,2,1,0:T(8,128)(2,1)S(1)}, bf16[2,12,128,128]{3,2,1,0:T(8,128)(2,1)S(1)}, u32[]{:S(2)}, u32[]{:S(2)}) collective-permute-start(bf16[2,12,128,128]{3,2,1,0:T(8,128)(2,1)S(1)} %collective-permute-done.2.down.rest_2_), channel_id=1, source_target_pairs={{0,1},{1,0},{2,3},{3,2},{4,5},{5,4},{6,7},{7,6},{8,9},{9,8},{10,11... | collective-permute-start | bytes 2359304 | tf_op jit(solution)/shard_map/ppermute | solution.py:34
  30.5 0.0 collective-permute-done.3.up.rest_3_
  30.5 0.0 copy-start.6
  30.5 2.3 %collective-permute-start.8 = (bf16[2,12,128,128]{3,2,1,0:T(8,128)(2,1)S(1)}, bf16[2,12,128,128]{3,2,1,0:T(8,128)(2,1)S(1)}, u32[]{:S(2)}, u32[]{:S(2)}) collective-permute-start(bf16[2,12,128,128]{3,2,1,0:T(8,128)(2,1)S(1)} %collective-permute-done.2.down.rest_2_), channel_id=1, source_target_pairs={{0,2},{1,3},{2,4},{3,5},{4,6},{5,7},{6,0},{7,1},{8,10},{9,11},{10,... | collective-permute-start | bytes 2359304 | tf_op jit(solution)/shard_map/ppermute | solution.py:34
  32.8 0.0 collective-permute-done.1.ra
  32.9 0.0 collective-permute-done.la
  32.9 0.0 copy-done.3
  32.9 0.0 copy-done.11
  32.9 5.1 %shard_map.94 = (f32[24,128,128]{2,1,0:T(8,128)}, s32[1]{0:T(128)}) custom-call(f32[2,1,96]{2,1,0:T(1,128)S(1)} %copy-done.11, s32[2,2,96]{2,1,0:T(2,128)S(1)} %bitcast.10, bf16[24,128,128]{2,1,0:T(8,128)(2,1)S(1)} %get-tuple-element.18.lo, bf16[24,128,128]{2,1,0:T(8,128)(2,1)S(1)} %collective-permute-done.la, ...), custom_call_target="tpu_custom_call" | custom-call | flops 402653184 | bytes 6000000 | tf_op jit(solution)/shard_map/pallas_call | solution.py:197
  38.0 0.0 copy-done.4
  38.0 0.0 copy-done.5
  38.1 0.0 copy-done.6
  38.1 6.9 %collective-permute-done.6.x_up.rest_6_ = bf16[2,12,128,128]{3,2,1,0:T(8,128)(2,1)S(1)} collective-permute-done((bf16[2,12,128,128]{3,2,1,0:T(8,128)(2,1)S(1)}, bf16[2,12,128,128]{3,2,1,0:T(8,128)(2,1)S(1)}, u32[]{:S(2)}, u32[]{:S(2)}) %collective-permute-start.6) | collective-permute-done | bytes 786464 | tf_op jit(solution)/shard_map/ppermute | solution.py:34
  45.0 4.1 %collective-permute-done.5.x_down.rest_5_ = bf16[2,12,128,128]{3,2,1,0:T(8,128)(2,1)S(1)} collective-permute-done((bf16[2,12,128,128]{3,2,1,0:T(8,128)(2,1)S(1)}, bf16[2,12,128,128]{3,2,1,0:T(8,128)(2,1)S(1)}, u32[]{:S(2)}, u32[]{:S(2)}) %collective-permute-start.5) | collective-permute-done | bytes 786464 | tf_op jit(solution)/shard_map/ppermute | solution.py:34
  49.1 1.1 %shard_map.95 = (bf16[12,128,128]{2,1,0:T(8,128)(2,1)S(1)}, bf16[12,128,128]{2,1,0:T(8,128)(2,1)S(1)}, bf16[24,128,128]{2,1,0:T(8,128)(2,1)S(1)}) custom-call(s32[1]{0:T(128)} %get-tuple-element.20.token, bf16[2,12,128,128]{3,2,1,0:T(8,128)(2,1)S(1)} %collective-permute-done.5.x_down.rest_5_, ...), custom_call_target="tpu_custom_call" | custom-call | bytes 6000000 | tf_op jit(solution)/shard_map/pallas_call | solution.py:197
  50.2 0.7 collective-permute-start.7
  50.9 1.9 %collective-permute-start.9 = (bf16[12,128,128]{2,1,0:T(8,128)(2,1)S(1)}, bf16[12,128,128]{2,1,0:T(8,128)(2,1)S(1)}, u32[]{:S(2)}, u32[]{:S(2)}) collective-permute-start(bf16[12,128,128]{2,1,0:T(8,128)(2,1)S(1)} %get-tuple-element.23), channel_id=1, source_target_pairs={{0,2},{1,3},{2,4},{3,5},{4,6},{5,7},{6,0},{7,1},{8,10},{9,11},{10,... | collective-permute-start | bytes 1179656 | tf_op jit(solution)/shard_map/ppermute | solution.py:34
  52.8 5.1 %collective-permute-start.10 = (bf16[12,128,128]{2,1,0:T(8,128)(2,1)S(1)}, bf16[12,128,128]{2,1,0:T(8,128)(2,1)S(1)}, u32[]{:S(2)}, u32[]{:S(2)}) collective-permute-start(bf16[12,128,128]{2,1,0:T(8,128)(2,1)S(1)} %get-tuple-element.24), channel_id=1, source_target_pairs={{0,6},{1,7},{2,0},{3,1},{4,2},{5,3},{6,4},{7,5},{8,14},{9,15},{10,... | collective-permute-start | bytes 1179656 | tf_op jit(solution)/shard_map/ppermute | solution.py:34
  58.0 0.0 collective-permute-done.8.opp.rest_4_
  58.0 0.0 copy-start.7
  58.0 0.0 copy-done
  58.0 0.0 copy-done.1
  58.0 3.6 %shard_map.96.lt_in = f32[24,128,128]{2,1,0:T(8,128)S(1)} custom-call(f32[2,1,96]{2,1,0:T(1,128)S(1)} %copy-done.11, s32[2,2,96]{2,1,0:T(2,128)S(1)} %bitcast.11, bf16[24,128,128]{2,1,0:T(8,128)(2,1)S(1)} %get-tuple-element.18.lo, bf16[24,128,128]{2,1,0:T(8,128)(2,1)S(1)} %collective-permute-done.la, f32[24,128,128]{2,1,0:T(8,128)} %get-tuple-element.22.lt_in, ...), custom_call_target="tpu_custom_call" | custom-call | flops 301989888 | bytes 6000000 | tf_op jit(solution)/shard_map/pallas_call | solution.py:197
  61.6 0.0 copy-done.7
  61.7 0.0 copy-start.2
  61.7 1.2 %copy-done.2 = f32[24,128,128]{2,1,0:T(8,128)} copy-done((f32[24,128,128]{2,1,0:T(8,128)}, f32[24,128,128]{2,1,0:T(8,128)S(1)}, u32[]{:S(2)}) %copy-start.2) | copy-done | bytes 1572888
  62.8 2.0 %collective-permute-done.9.late0 = bf16[12,128,128]{2,1,0:T(8,128)(2,1)S(1)} collective-permute-done((bf16[12,128,128]{2,1,0:T(8,128)(2,1)S(1)}, bf16[12,128,128]{2,1,0:T(8,128)(2,1)S(1)}, u32[]{:S(2)}, u32[]{:S(2)}) %collective-permute-start.9) | collective-permute-done | bytes 393248 | tf_op jit(solution)/shard_map/ppermute | solution.py:34
  64.8 1.2 %collective-permute-done.10.late1 = bf16[12,128,128]{2,1,0:T(8,128)(2,1)S(1)} collective-permute-done((bf16[12,128,128]{2,1,0:T(8,128)(2,1)S(1)}, bf16[12,128,128]{2,1,0:T(8,128)(2,1)S(1)}, u32[]{:S(2)}, u32[]{:S(2)}) %collective-permute-start.10) | collective-permute-done | bytes 393248 | tf_op jit(solution)/shard_map/ppermute | solution.py:34
  66.0 0.0 collective-permute-done.7.mid
  66.0 11.0 %shard_map.97 = (bf16[24,128,128]{2,1,0:T(8,128)(2,1)}, bf16[24,128,128]{2,1,0:T(8,128)(2,1)}, bf16[8,6,128,128]{3,2,1,0:T(8,128)(2,1)}) custom-call(f32[2,1,96]{2,1,0:T(1,128)S(1)} %copy-done.11, s32[24]{0:T(128)S(1)} %copy-done.12, s32[2,2,96]{2,1,0:T(2,128)S(1)} %bitcast.12, s32[4,128]{1,0:T(4,128)S(1)} %get-tuple-element.17.order, ...), custom_call_target="tpu_custom_call" | custom-call | flops 2516582400 | bytes 6000000 | tf_op jit(solution)/shard_map/pallas_call | solution.py:197
  77.0 25.2 %all_to_all.5.parts = bf16[8,6,128,128]{3,2,1,0:T(8,128)(2,1)S(1)} all-to-all(bf16[8,6,128,128]{3,2,1,0:T(8,128)(2,1)} %get-tuple-element.27), channel_id=1, replica_groups=mesh['seg'=64,'op'=8] {'op'}, dimensions={0} | all-to-all | bytes 3145728 | tf_op jit(solution)/shard_map/all_to_all | solution.py:449
  102.2 0.9 shard_map.98
  (7 shorter events, 0.0 us)
Async XLA Ops:
  0.6 32.2 %copy-start.3 = (bf16[2,12,128,128]{3,2,1,0:T(8,128)(2,1)S(1)}, bf16[2,12,128,128]{3,2,1,0:T(8,128)(2,1)}, u32[]{:S(2)}) copy-start(bf16[2,12,128,128]{3,2,1,0:T(8,128)(2,1)} %rest_0_.1) | copy-start | bytes 2359300
  0.6 21.5 %collective-permute-start.4 = (bf16[2,12,128,128]{3,2,1,0:T(8,128)(2,1)}, bf16[2,12,128,128]{3,2,1,0:T(8,128)(2,1)S(1)}, u32[]{:S(2)}, u32[]{:S(2)}) collective-permute-start(bf16[2,12,128,128]{3,2,1,0:T(8,128)(2,1)} %rest_0_.1), channel_id=1, source_target_pairs={{0,1},{1,0},{2,3},{3,2},{4,5},{5,4},{6,7},{7,6},{8,9},{9,8},{10,11... | collective-permute-start | bytes 2359304 | tf_op jit(solution)/shard_map/ppermute | solution.py:34
  4.2 22.9 %collective-permute-start.2 = (bf16[2,12,128,128]{3,2,1,0:T(8,128)(2,1)}, bf16[2,12,128,128]{3,2,1,0:T(8,128)(2,1)S(1)}, u32[]{:S(2)}, u32[]{:S(2)}) collective-permute-start(bf16[2,12,128,128]{3,2,1,0:T(8,128)(2,1)} %rest_0_.1), channel_id=1, source_target_pairs={{0,2},{1,3},{2,4},{3,5},{4,6},{5,7},{6,0},{7,1},{8,10},{9,11},{10,... | collective-permute-start | bytes 2359304 | tf_op jit(solution)/shard_map/ppermute | solution.py:34
  7.7 22.8 %collective-permute-start.3 = (bf16[2,12,128,128]{3,2,1,0:T(8,128)(2,1)}, bf16[2,12,128,128]{3,2,1,0:T(8,128)(2,1)S(1)}, u32[]{:S(2)}, u32[]{:S(2)}) collective-permute-start(bf16[2,12,128,128]{3,2,1,0:T(8,128)(2,1)} %rest_0_.1), channel_id=1, source_target_pairs={{0,6},{1,7},{2,0},{3,1},{4,2},{5,3},{6,4},{7,5},{8,14},{9,15},{10,... | collective-permute-start | bytes 2359304 | tf_op jit(solution)/shard_map/ppermute | solution.py:34
  11.2 1.1 %copy-start.8 = (bf16[1,1,24,128,128]{4,3,2,1,0:T(8,128)(2,1)S(1)}, bf16[1,1,24,128,128]{4,3,2,1,0:T(8,128)(2,1)}, u32[]{:S(2)}) copy-start(bf16[1,1,24,128,128]{4,3,2,1,0:T(8,128)(2,1)} %param.6) | copy-start | bytes 2359300
  12.4 1.1 %copy-start.9 = (bf16[1,1,24,128,128]{4,3,2,1,0:T(8,128)(2,1)S(1)}, bf16[1,1,24,128,128]{4,3,2,1,0:T(8,128)(2,1)}, u32[]{:S(2)}) copy-start(bf16[1,1,24,128,128]{4,3,2,1,0:T(8,128)(2,1)} %param.7) | copy-start | bytes 2359300
  13.5 0.7 copy-start.10
  14.2 0.7 copy-start.12
  14.9 18.0 %copy-start.11 = (f32[2,1,96]{2,1,0:T(1,128)S(1)}, f32[2,1,96]{2,1,0:T(1,128)}, u32[]{:S(2)}) copy-start(f32[2,1,96]{2,1,0:T(1,128)} %wts.5) | copy-start | bytes 2308
  17.2 15.7 %collective-permute-start.1 = (bf16[24,128,128]{2,1,0:T(8,128)(2,1)S(1)}, bf16[24,128,128]{2,1,0:T(8,128)(2,1)S(1)}, u32[]{:S(2)}, u32[]{:S(2)}) collective-permute-start(bf16[24,128,128]{2,1,0:T(8,128)(2,1)S(1)} %get-tuple-element.19.ro), channel_id=1, source_target_pairs={{8,0},{16,8},{24,16},{32,24},{40,32},{48,40},{56,48},{64,56},{72,6... | collective-permute-start | bytes 2359304 | tf_op jit(solution)/shard_map/ppermute | solution.py:41
  19.1 13.8 %collective-permute-start = (bf16[24,128,128]{2,1,0:T(8,128)(2,1)S(1)}, bf16[24,128,128]{2,1,0:T(8,128)(2,1)S(1)}, u32[]{:S(2)}, u32[]{:S(2)}) collective-permute-start(bf16[24,128,128]{2,1,0:T(8,128)(2,1)S(1)} %get-tuple-element.18.lo), channel_id=1, source_target_pairs={{0,8},{8,16},{16,24},{24,32},{32,40},{40,48},{48,56},{56,64},{64,7... | collective-permute-start | bytes 2359304 | tf_op jit(solution)/shard_map/ppermute | solution.py:41
  22.2 15.9 %copy-start.4 = (bf16[2,12,128,128]{3,2,1,0:T(8,128)(2,1)}, bf16[2,12,128,128]{3,2,1,0:T(8,128)(2,1)S(1)}, u32[]{:S(2)}) copy-start(bf16[2,12,128,128]{3,2,1,0:T(8,128)(2,1)S(1)} %collective-permute-done.4.b_x.rest_1_) | copy-start | bytes 2359300
  22.2 22.8 %collective-permute-start.6 = (bf16[2,12,128,128]{3,2,1,0:T(8,128)(2,1)S(1)}, bf16[2,12,128,128]{3,2,1,0:T(8,128)(2,1)S(1)}, u32[]{:S(2)}, u32[]{:S(2)}) collective-permute-start(bf16[2,12,128,128]{3,2,1,0:T(8,128)(2,1)S(1)} %collective-permute-done.4.b_x.rest_1_), channel_id=1, source_target_pairs={{0,6},{1,7},{2,0},{3,1},{4,2},{5,3},{6,4},{7,5},{8,14},{9,15},{10,... | collective-permute-start | bytes 2359304 | tf_op jit(solution)/shard_map/ppermute | solution.py:34
  27.1 11.0 %copy-start.5 = (bf16[2,12,128,128]{3,2,1,0:T(8,128)(2,1)}, bf16[2,12,128,128]{3,2,1,0:T(8,128)(2,1)S(1)}, u32[]{:S(2)}) copy-start(bf16[2,12,128,128]{3,2,1,0:T(8,128)(2,1)S(1)} %collective-permute-done.2.down.rest_2_) | copy-start | bytes 2359300
  27.1 22.0 %collective-permute-start.5 = (bf16[2,12,128,128]{3,2,1,0:T(8,128)(2,1)S(1)}, bf16[2,12,128,128]{3,2,1,0:T(8,128)(2,1)S(1)}, u32[]{:S(2)}, u32[]{:S(2)}) collective-permute-start(bf16[2,12,128,128]{3,2,1,0:T(8,128)(2,1)S(1)} %collective-permute-done.2.down.rest_2_), channel_id=1, source_target_pairs={{0,1},{1,0},{2,3},{3,2},{4,5},{5,4},{6,7},{7,6},{8,9},{9,8},{10,11... | collective-permute-start | bytes 2359304 | tf_op jit(solution)/shard_map/ppermute | solution.py:34
  30.5 7.5 %copy-start.6 = (bf16[2,12,128,128]{3,2,1,0:T(8,128)(2,1)}, bf16[2,12,128,128]{3,2,1,0:T(8,128)(2,1)S(1)}, u32[]{:S(2)}) copy-start(bf16[2,12,128,128]{3,2,1,0:T(8,128)(2,1)S(1)} %collective-permute-done.3.up.rest_3_) | copy-start | bytes 2359300
  30.5 27.4 %collective-permute-start.8 = (bf16[2,12,128,128]{3,2,1,0:T(8,128)(2,1)S(1)}, bf16[2,12,128,128]{3,2,1,0:T(8,128)(2,1)S(1)}, u32[]{:S(2)}, u32[]{:S(2)}) collective-permute-start(bf16[2,12,128,128]{3,2,1,0:T(8,128)(2,1)S(1)} %collective-permute-done.2.down.rest_2_), channel_id=1, source_target_pairs={{0,2},{1,3},{2,4},{3,5},{4,6},{5,7},{6,0},{7,1},{8,10},{9,11},{10,... | collective-permute-start | bytes 2359304 | tf_op jit(solution)/shard_map/ppermute | solution.py:34
  45.0 13.0 %copy-start = (bf16[2,12,128,128]{3,2,1,0:T(8,128)(2,1)}, bf16[2,12,128,128]{3,2,1,0:T(8,128)(2,1)S(1)}, u32[]{:S(2)}) copy-start(bf16[2,12,128,128]{3,2,1,0:T(8,128)(2,1)S(1)} %collective-permute-done.6.x_up.rest_6_) | copy-start | bytes 2359300
  49.1 8.9 %copy-start.1 = (bf16[2,12,128,128]{3,2,1,0:T(8,128)(2,1)}, bf16[2,12,128,128]{3,2,1,0:T(8,128)(2,1)S(1)}, u32[]{:S(2)}) copy-start(bf16[2,12,128,128]{3,2,1,0:T(8,128)(2,1)S(1)} %collective-permute-done.5.x_down.rest_5_) | copy-start | bytes 2359300
  50.2 15.8 %collective-permute-start.7 = (bf16[24,128,128]{2,1,0:T(8,128)(2,1)S(1)}, bf16[24,128,128]{2,1,0:T(8,128)(2,1)S(1)}, u32[]{:S(2)}, u32[]{:S(2)}) collective-permute-start(bf16[24,128,128]{2,1,0:T(8,128)(2,1)S(1)} %get-tuple-element.21), channel_id=1, source_target_pairs={{0,256},{504,248},{1,257},{505,249},{2,258},{506,250},{3,259},{507... | collective-permute-start | bytes 2359304 | tf_op jit(solution)/shard_map/ppermute | solution.py:46
  50.9 13.9 %collective-permute-start.9 = (bf16[12,128,128]{2,1,0:T(8,128)(2,1)S(1)}, bf16[12,128,128]{2,1,0:T(8,128)(2,1)S(1)}, u32[]{:S(2)}, u32[]{:S(2)}) collective-permute-start(bf16[12,128,128]{2,1,0:T(8,128)(2,1)S(1)} %get-tuple-element.23), channel_id=1, source_target_pairs={{0,2},{1,3},{2,4},{3,5},{4,6},{5,7},{6,0},{7,1},{8,10},{9,11},{10,... | collective-permute-start | bytes 1179656 | tf_op jit(solution)/shard_map/ppermute | solution.py:34
  52.8 13.2 %collective-permute-start.10 = (bf16[12,128,128]{2,1,0:T(8,128)(2,1)S(1)}, bf16[12,128,128]{2,1,0:T(8,128)(2,1)S(1)}, u32[]{:S(2)}, u32[]{:S(2)}) collective-permute-start(bf16[12,128,128]{2,1,0:T(8,128)(2,1)S(1)} %get-tuple-element.24), channel_id=1, source_target_pairs={{0,6},{1,7},{2,0},{3,1},{4,2},{5,3},{6,4},{7,5},{8,14},{9,15},{10,... | collective-permute-start | bytes 1179656 | tf_op jit(solution)/shard_map/ppermute | solution.py:34
  58.0 3.7 %copy-start.7 = (bf16[2,12,128,128]{3,2,1,0:T(8,128)(2,1)}, bf16[2,12,128,128]{3,2,1,0:T(8,128)(2,1)S(1)}, u32[]{:S(2)}) copy-start(bf16[2,12,128,128]{3,2,1,0:T(8,128)(2,1)S(1)} %collective-permute-done.8.opp.rest_4_) | copy-start | bytes 2359300
  61.7 1.2 %copy-start.2 = (f32[24,128,128]{2,1,0:T(8,128)}, f32[24,128,128]{2,1,0:T(8,128)S(1)}, u32[]{:S(2)}) copy-start(f32[24,128,128]{2,1,0:T(8,128)S(1)} %shard_map.96.lt_in) | copy-start | bytes 4718596

commit v6 on v5

--- a/solution.py
+++ b/solution.py
@@ -308,22 +308,33 @@
         flops=2 * 48 * 2 * 128**3,
     )
 
-    def pick(token, x_down, x_up, la, ra, out0, out1, passing, sems):
+    def pick_up(token, x_up, out, sems):
+        wait(move([(x_up.at[1], out)], sems))
+
+    (send1,) = call(
+        pick_up,
+        [(VMEM, site_shape)],
+        [(SMEM, token), (HBM, x_up)],
+        scratch=[pltpu.SemaphoreType.DMA((1,))],
+        vmem=4,
+    )
+
+    def pick_down(token, x_down, la, ra, out, passing, sems):
         first_seg, last_seg = seg_flags()
-        coming = move([(x_down.at[0], out0), (x_up.at[1], out1)], sems.at[pl.ds(0, 2)])
+        coming = move([(x_down.at[0], out)], sems.at[pl.ds(0, 1)])
         for flag, source in ((first_seg, la), (last_seg, ra)):
 
             @pl.when(flag)
             def _():
-                wait(move([(source, passing)], sems.at[pl.ds(2, 1)]))
+                wait(move([(source, passing)], sems.at[pl.ds(1, 1)]))
 
         wait(coming)
 
-    send0, send1, passing = call(
-        pick,
-        [(VMEM, site_shape), (VMEM, site_shape), (VMEM, env)],
-        [(SMEM, token)] + [(HBM, a) for a in (x_down, x_up, left_arrived, right_arrived)],
-        scratch=[pltpu.SemaphoreType.DMA((3,))],
+    send0, passing = call(
+        pick_down,
+        [(VMEM, site_shape), (VMEM, env)],
+        [(SMEM, token)] + [(HBM, a) for a in (x_down, left_arrived, right_arrived)],
+        scratch=[pltpu.SemaphoreType.DMA((2,))],
         vmem=4,
     )
     env_middle = from_ends(passing)

time: 104 us -> 103 us (level)
  the two profiles are of different devices: /device:TPU:96 before, /device:TPU:2 now
where the time goes in v6:
time: 103 us; the launch traced here: 102 us
  starting transfers between devices  34.3 us (33%)
  Pallas kernels  24.8 us (24%)
  blocking collectives  23.5 us (23%)
  waiting for transfers between devices  14 us (14%)
  local copies, waits for them, and re-layouts  4.8 us (5%)
    ppermute x8, starting transfers between devices, hop(): return lax.ppermute(block, 'op', op_route(dy, dx))  28.6 us
    pallas_call x7, Pallas kernels, call(): pl.pallas_call(body, out_shape=[shape for _, shape in outs], in_specs=[sp...  24.8 us
    all_to_all x1, blocking collectives, local(): parts = lax.all_to_all(both, 'op', 0, 0, tiled=True)  23.5 us
    ppermute x8, waiting for transfers between devices, hop(): return lax.ppermute(block, 'op', op_route(dy, dx))  8.41 us
    ppermute x2, waiting for transfers between devices, along_segments(): return lax.ppermute(block, 'seg', route + [(middle, end)])  5.57 us
    unnamed x26, local copies, waits for them, and re-layouts  4.8 us
    ppermute x2, starting transfers between devices, along_segments(): return lax.ppermute(block, 'seg', route + [(middle, end)])  4.33 us
  transfers between devices with their start and end apart: 11, of which 4 were waited for; matrix products, arithmetic and copies ran while one was open for 0% of the time, Pallas kernels for 13%

profile of v6, /device:TPU:2, one launch (start us, length us, event | category | flops | bytes accessed | tf_op | source)
XLA Modules:
  0.0 102.3 jit_solution(6317911258679982011)
XLA Ops:
  0.6 0.0 copy-start.3
  0.6 3.6 %collective-permute-start.2 = (bf16[2,12,128,128]{3,2,1,0:T(8,128)(2,1)}, bf16[2,12,128,128]{3,2,1,0:T(8,128)(2,1)S(1)}, u32[]{:S(2)}, u32[]{:S(2)}) collective-permute-start(bf16[2,12,128,128]{3,2,1,0:T(8,128)(2,1)} %rest_0_.1), channel_id=1, source_target_pairs={{0,2},{1,3},{2,4},{3,5},{4,6},{5,7},{6,0},{7,1},{8,10},{9,11},{10,... | collective-permute-start | bytes 2359304 | tf_op jit(solution)/shard_map/ppermute | solution.py:34
  4.3 6.3 %collective-permute-start.4 = (bf16[2,12,128,128]{3,2,1,0:T(8,128)(2,1)}, bf16[2,12,128,128]{3,2,1,0:T(8,128)(2,1)S(1)}, u32[]{:S(2)}, u32[]{:S(2)}) collective-permute-start(bf16[2,12,128,128]{3,2,1,0:T(8,128)(2,1)} %rest_0_.1), channel_id=1, source_target_pairs={{0,1},{1,0},{2,3},{3,2},{4,5},{5,4},{6,7},{7,6},{8,9},{9,8},{10,11... | collective-permute-start | bytes 2359304 | tf_op jit(solution)/shard_map/ppermute | solution.py:34
  10.5 5.1 %collective-permute-start.3 = (bf16[2,12,128,128]{3,2,1,0:T(8,128)(2,1)}, bf16[2,12,128,128]{3,2,1,0:T(8,128)(2,1)S(1)}, u32[]{:S(2)}, u32[]{:S(2)}) collective-permute-start(bf16[2,12,128,128]{3,2,1,0:T(8,128)(2,1)} %rest_0_.1), channel_id=1, source_target_pairs={{0,6},{1,7},{2,0},{3,1},{4,2},{5,3},{6,4},{7,5},{8,14},{9,15},{10,... | collective-permute-start | bytes 2359304 | tf_op jit(solution)/shard_map/ppermute | solution.py:34
  15.7 0.0 copy-start.8
  15.7 1.1 %copy-done.8 = bf16[1,1,24,128,128]{4,3,2,1,0:T(8,128)(2,1)S(1)} copy-done((bf16[1,1,24,128,128]{4,3,2,1,0:T(8,128)(2,1)S(1)}, bf16[1,1,24,128,128]{4,3,2,1,0:T(8,128)(2,1)}, u32[]{:S(2)}) %copy-start.8) | copy-done | bytes 786456
  16.8 1.1 %copy-done.9 = bf16[1,1,24,128,128]{4,3,2,1,0:T(8,128)(2,1)S(1)} copy-done((bf16[1,1,24,128,128]{4,3,2,1,0:T(8,128)(2,1)S(1)}, bf16[1,1,24,128,128]{4,3,2,1,0:T(8,128)(2,1)}, u32[]{:S(2)}) %copy-start.9) | copy-done | bytes 786456
  17.9 0.7 copy-done.10
  18.6 0.7 copy-done.12
  19.3 2.3 %shard_map.93 = (bf16[24,128,128]{2,1,0:T(8,128)(2,1)S(1)}, bf16[24,128,128]{2,1,0:T(8,128)(2,1)S(1)}, s32[4,128]{1,0:T(4,128)S(1)}) custom-call(s32[24]{0:T(128)S(1)} %copy-done.12, s32[2,2,96]{2,1,0:T(2,128)S(1)} %bitcast.9, bf16[24,128,128]{2,1,0:T(8,128)(2,1)S(1)} %bitcast.7, bf16[24,128,128]{2,1,0:T(8,128)(2,1)S(1)} %bitcast.8), custom_call_target="tpu_custom_call" | custom-call | bytes 6000000 | tf_op jit(solution)/shard_map/pallas_call | solution.py:197
  21.6 1.3 %collective-permute-start.1 = (bf16[24,128,128]{2,1,0:T(8,128)(2,1)S(1)}, bf16[24,128,128]{2,1,0:T(8,128)(2,1)S(1)}, u32[]{:S(2)}, u32[]{:S(2)}) collective-permute-start(bf16[24,128,128]{2,1,0:T(8,128)(2,1)S(1)} %get-tuple-element.18.ro), channel_id=1, source_target_pairs={{8,0},{16,8},{24,16},{32,24},{40,32},{48,40},{56,48},{64,56},{72,6... | collective-permute-start | bytes 2359304 | tf_op jit(solution)/shard_map/ppermute | solution.py:41
  22.9 3.0 %collective-permute-start = (bf16[24,128,128]{2,1,0:T(8,128)(2,1)S(1)}, bf16[24,128,128]{2,1,0:T(8,128)(2,1)S(1)}, u32[]{:S(2)}, u32[]{:S(2)}) collective-permute-start(bf16[24,128,128]{2,1,0:T(8,128)(2,1)S(1)} %get-tuple-element.17.lo), channel_id=1, source_target_pairs={{0,8},{8,16},{16,24},{24,32},{32,40},{40,48},{48,56},{56,64},{64,7... | collective-permute-start | bytes 2359304 | tf_op jit(solution)/shard_map/ppermute | solution.py:41
  25.9 0.0 collective-permute-done.2.down.rest_2_
  25.9 0.0 copy-start.4
  26.0 1.9 %collective-permute-start.5 = (bf16[2,12,128,128]{3,2,1,0:T(8,128)(2,1)S(1)}, bf16[2,12,128,128]{3,2,1,0:T(8,128)(2,1)S(1)}, u32[]{:S(2)}, u32[]{:S(2)}) collective-permute-start(bf16[2,12,128,128]{3,2,1,0:T(8,128)(2,1)S(1)} %collective-permute-done.2.down.rest_2_), channel_id=1, source_target_pairs={{0,1},{1,0},{2,3},{3,2},{4,5},{5,4},{6,7},{7,6},{8,9},{9,8},{10,11... | collective-permute-start | bytes 2359304 | tf_op jit(solution)/shard_map/ppermute | solution.py:34
  27.9 0.0 collective-permute-done.4.b_x.rest_1_
  27.9 0.0 copy-start.5
  27.9 1.9 %collective-permute-start.8 = (bf16[2,12,128,128]{3,2,1,0:T(8,128)(2,1)S(1)}, bf16[2,12,128,128]{3,2,1,0:T(8,128)(2,1)S(1)}, u32[]{:S(2)}, u32[]{:S(2)}) collective-permute-start(bf16[2,12,128,128]{3,2,1,0:T(8,128)(2,1)S(1)} %collective-permute-done.4.b_x.rest_1_), channel_id=1, source_target_pairs={{0,6},{1,7},{2,0},{3,1},{4,2},{5,3},{6,4},{7,5},{8,14},{9,15},{10,... | collective-permute-start | bytes 2359304 | tf_op jit(solution)/shard_map/ppermute | solution.py:34
  29.8 0.0 collective-permute-done.3.up.rest_3_
  29.8 0.0 copy-start.6
  29.9 3.9 %collective-permute-start.7 = (bf16[2,12,128,128]{3,2,1,0:T(8,128)(2,1)S(1)}, bf16[2,12,128,128]{3,2,1,0:T(8,128)(2,1)S(1)}, u32[]{:S(2)}, u32[]{:S(2)}) collective-permute-start(bf16[2,12,128,128]{3,2,1,0:T(8,128)(2,1)S(1)} %collective-permute-done.2.down.rest_2_), channel_id=1, source_target_pairs={{0,2},{1,3},{2,4},{3,5},{4,6},{5,7},{6,0},{7,1},{8,10},{9,11},{10,... | collective-permute-start | bytes 2359304 | tf_op jit(solution)/shard_map/ppermute | solution.py:34
  33.8 0.0 collective-permute-done.1.ra
  33.8 5.6 %collective-permute-done.la = bf16[24,128,128]{2,1,0:T(8,128)(2,1)S(1)} collective-permute-done((bf16[24,128,128]{2,1,0:T(8,128)(2,1)S(1)}, bf16[24,128,128]{2,1,0:T(8,128)(2,1)S(1)}, u32[]{:S(2)}, u32[]{:S(2)}) %collective-permute-start) | collective-permute-done | bytes 786464 | tf_op jit(solution)/shard_map/ppermute | solution.py:41
  39.4 0.0 copy-done.3
  39.4 0.0 copy-done.11
  39.4 5.1 %shard_map.94 = (f32[24,128,128]{2,1,0:T(8,128)}, s32[1]{0:T(128)}) custom-call(f32[2,1,96]{2,1,0:T(1,128)S(1)} %copy-done.11, s32[2,2,96]{2,1,0:T(2,128)S(1)} %bitcast.10, bf16[24,128,128]{2,1,0:T(8,128)(2,1)S(1)} %get-tuple-element.17.lo, bf16[24,128,128]{2,1,0:T(8,128)(2,1)S(1)} %collective-permute-done.la, ...), custom_call_target="tpu_custom_call" | custom-call | flops 402653184 | bytes 6000000 | tf_op jit(solution)/shard_map/pallas_call | solution.py:197
  44.5 0.0 copy-done.4
  44.5 0.0 copy-done.5
  44.5 0.0 copy-done.6
  44.5 2.8 %collective-permute-done.5.x_down.rest_5_ = bf16[2,12,128,128]{3,2,1,0:T(8,128)(2,1)S(1)} collective-permute-done((bf16[2,12,128,128]{3,2,1,0:T(8,128)(2,1)S(1)}, bf16[2,12,128,128]{3,2,1,0:T(8,128)(2,1)S(1)}, u32[]{:S(2)}, u32[]{:S(2)}) %collective-permute-start.5) | collective-permute-done | bytes 786464 | tf_op jit(solution)/shard_map/ppermute | solution.py:34
  47.3 0.9 shard_map.95
  48.2 1.3 %collective-permute-start.6 = (bf16[24,128,128]{2,1,0:T(8,128)(2,1)S(1)}, bf16[24,128,128]{2,1,0:T(8,128)(2,1)S(1)}, u32[]{:S(2)}, u32[]{:S(2)}) collective-permute-start(bf16[24,128,128]{2,1,0:T(8,128)(2,1)S(1)} %get-tuple-element.20), channel_id=1, source_target_pairs={{0,256},{504,248},{1,257},{505,249},{2,258},{506,250},{3,259},{507... | collective-permute-start | bytes 2359304 | tf_op jit(solution)/shard_map/ppermute | solution.py:46
  49.6 0.0 collective-permute-done.8.x_up.rest_6_
  49.6 0.0 copy-start.1
  49.6 0.9 shard_map.97
  50.5 3.0 %collective-permute-start.10 = (bf16[12,128,128]{2,1,0:T(8,128)(2,1)S(1)}, bf16[12,128,128]{2,1,0:T(8,128)(2,1)S(1)}, u32[]{:S(2)}, u32[]{:S(2)}) collective-permute-start(bf16[12,128,128]{2,1,0:T(8,128)(2,1)S(1)} %shard_map.97), channel_id=1, source_target_pairs={{0,6},{1,7},{2,0},{3,1},{4,2},{5,3},{6,4},{7,5},{8,14},{9,15},{10,... | collective-permute-start | bytes 1179656 | tf_op jit(solution)/shard_map/ppermute | solution.py:34
  53.5 2.8 %collective-permute-start.9 = (bf16[12,128,128]{2,1,0:T(8,128)(2,1)S(1)}, bf16[12,128,128]{2,1,0:T(8,128)(2,1)S(1)}, u32[]{:S(2)}, u32[]{:S(2)}) collective-permute-start(bf16[12,128,128]{2,1,0:T(8,128)(2,1)S(1)} %get-tuple-element.22), channel_id=1, source_target_pairs={{0,2},{1,3},{2,4},{3,5},{4,6},{5,7},{6,0},{7,1},{8,10},{9,11},{10,... | collective-permute-start | bytes 1179656 | tf_op jit(solution)/shard_map/ppermute | solution.py:34
  56.3 0.0 collective-permute-done.7.opp.rest_4_
  56.4 0.0 copy-start.7
  56.4 0.0 copy-done
  56.4 3.6 %shard_map.96.lt_in = f32[24,128,128]{2,1,0:T(8,128)S(1)} custom-call(f32[2,1,96]{2,1,0:T(1,128)S(1)} %copy-done.11, s32[2,2,96]{2,1,0:T(2,128)S(1)} %bitcast.11, bf16[24,128,128]{2,1,0:T(8,128)(2,1)S(1)} %get-tuple-element.17.lo, bf16[24,128,128]{2,1,0:T(8,128)(2,1)S(1)} %collective-permute-done.la, f32[24,128,128]{2,1,0:T(8,128)} %get-tuple-element.21.lt_in, ...), custom_call_target="tpu_custom_call" | custom-call | flops 301989888 | bytes 6000000 | tf_op jit(solution)/shard_map/pallas_call | solution.py:197
  60.1 1.2 %copy-done.2 = f32[24,128,128]{2,1,0:T(8,128)} copy-done((f32[24,128,128]{2,1,0:T(8,128)}, f32[24,128,128]{2,1,0:T(8,128)S(1)}, u32[]{:S(2)}) %copy-start.2) | copy-done | bytes 1572888
  61.2 1.0 collective-permute-done.10.late1
  62.2 4.7 %collective-permute-done.9.late0 = bf16[12,128,128]{2,1,0:T(8,128)(2,1)S(1)} collective-permute-done((bf16[12,128,128]{2,1,0:T(8,128)(2,1)S(1)}, bf16[12,128,128]{2,1,0:T(8,128)(2,1)S(1)}, u32[]{:S(2)}, u32[]{:S(2)}) %collective-permute-start.9) | collective-permute-done | bytes 393248 | tf_op jit(solution)/shard_map/ppermute | solution.py:34
  66.9 0.0 collective-permute-done.6.mid
  66.9 11.0 %shard_map.98 = (bf16[24,128,128]{2,1,0:T(8,128)(2,1)}, bf16[24,128,128]{2,1,0:T(8,128)(2,1)}, bf16[8,6,128,128]{3,2,1,0:T(8,128)(2,1)}) custom-call(f32[2,1,96]{2,1,0:T(1,128)S(1)} %copy-done.11, s32[24]{0:T(128)S(1)} %copy-done.12, s32[2,2,96]{2,1,0:T(2,128)S(1)} %bitcast.12, s32[4,128]{1,0:T(4,128)S(1)} %get-tuple-element.16.order, ...), custom_call_target="tpu_custom_call" | custom-call | flops 2516582400 | bytes 6000000 | tf_op jit(solution)/shard_map/pallas_call | solution.py:197
  77.9 23.5 %all_to_all.5.parts = bf16[8,6,128,128]{3,2,1,0:T(8,128)(2,1)S(1)} all-to-all(bf16[8,6,128,128]{3,2,1,0:T(8,128)(2,1)} %get-tuple-element.25), channel_id=1, replica_groups=mesh['seg'=64,'op'=8] {'op'}, dimensions={0} | all-to-all | bytes 3145728 | tf_op jit(solution)/shard_map/all_to_all | solution.py:460
  101.4 0.9 shard_map.99
  (8 shorter events, 0.0 us)
Async XLA Ops:
  0.6 38.7 %copy-start.3 = (bf16[2,12,128,128]{3,2,1,0:T(8,128)(2,1)S(1)}, bf16[2,12,128,128]{3,2,1,0:T(8,128)(2,1)}, u32[]{:S(2)}) copy-start(bf16[2,12,128,128]{3,2,1,0:T(8,128)(2,1)} %rest_0_.1) | copy-start | bytes 2359300
  0.6 25.3 %collective-permute-start.2 = (bf16[2,12,128,128]{3,2,1,0:T(8,128)(2,1)}, bf16[2,12,128,128]{3,2,1,0:T(8,128)(2,1)S(1)}, u32[]{:S(2)}, u32[]{:S(2)}) collective-permute-start(bf16[2,12,128,128]{3,2,1,0:T(8,128)(2,1)} %rest_0_.1), channel_id=1, source_target_pairs={{0,2},{1,3},{2,4},{3,5},{4,6},{5,7},{6,0},{7,1},{8,10},{9,11},{10,... | collective-permute-start | bytes 2359304 | tf_op jit(solution)/shard_map/ppermute | solution.py:34
  4.3 23.6 %collective-permute-start.4 = (bf16[2,12,128,128]{3,2,1,0:T(8,128)(2,1)}, bf16[2,12,128,128]{3,2,1,0:T(8,128)(2,1)S(1)}, u32[]{:S(2)}, u32[]{:S(2)}) collective-permute-start(bf16[2,12,128,128]{3,2,1,0:T(8,128)(2,1)} %rest_0_.1), channel_id=1, source_target_pairs={{0,1},{1,0},{2,3},{3,2},{4,5},{5,4},{6,7},{7,6},{8,9},{9,8},{10,11... | collective-permute-start | bytes 2359304 | tf_op jit(solution)/shard_map/ppermute | solution.py:34
  10.5 19.3 %collective-permute-start.3 = (bf16[2,12,128,128]{3,2,1,0:T(8,128)(2,1)}, bf16[2,12,128,128]{3,2,1,0:T(8,128)(2,1)S(1)}, u32[]{:S(2)}, u32[]{:S(2)}) collective-permute-start(bf16[2,12,128,128]{3,2,1,0:T(8,128)(2,1)} %rest_0_.1), channel_id=1, source_target_pairs={{0,6},{1,7},{2,0},{3,1},{4,2},{5,3},{6,4},{7,5},{8,14},{9,15},{10,... | collective-permute-start | bytes 2359304 | tf_op jit(solution)/shard_map/ppermute | solution.py:34
  15.7 1.1 %copy-start.8 = (bf16[1,1,24,128,128]{4,3,2,1,0:T(8,128)(2,1)S(1)}, bf16[1,1,24,128,128]{4,3,2,1,0:T(8,128)(2,1)}, u32[]{:S(2)}) copy-start(bf16[1,1,24,128,128]{4,3,2,1,0:T(8,128)(2,1)} %param.6) | copy-start | bytes 2359300
  16.8 1.1 %copy-start.9 = (bf16[1,1,24,128,128]{4,3,2,1,0:T(8,128)(2,1)S(1)}, bf16[1,1,24,128,128]{4,3,2,1,0:T(8,128)(2,1)}, u32[]{:S(2)}) copy-start(bf16[1,1,24,128,128]{4,3,2,1,0:T(8,128)(2,1)} %param.7) | copy-start | bytes 2359300
  17.9 0.7 copy-start.10
  18.6 0.7 copy-start.12
  19.3 20.1 %copy-start.11 = (f32[2,1,96]{2,1,0:T(1,128)S(1)}, f32[2,1,96]{2,1,0:T(1,128)}, u32[]{:S(2)}) copy-start(f32[2,1,96]{2,1,0:T(1,128)} %wts.5) | copy-start | bytes 2308
  21.6 12.2 %collective-permute-start.1 = (bf16[24,128,128]{2,1,0:T(8,128)(2,1)S(1)}, bf16[24,128,128]{2,1,0:T(8,128)(2,1)S(1)}, u32[]{:S(2)}, u32[]{:S(2)}) collective-permute-start(bf16[24,128,128]{2,1,0:T(8,128)(2,1)S(1)} %get-tuple-element.18.ro), channel_id=1, source_target_pairs={{8,0},{16,8},{24,16},{32,24},{40,32},{48,40},{56,48},{64,56},{72,6... | collective-permute-start | bytes 2359304 | tf_op jit(solution)/shard_map/ppermute | solution.py:41
  22.9 16.5 %collective-permute-start = (bf16[24,128,128]{2,1,0:T(8,128)(2,1)S(1)}, bf16[24,128,128]{2,1,0:T(8,128)(2,1)S(1)}, u32[]{:S(2)}, u32[]{:S(2)}) collective-permute-start(bf16[24,128,128]{2,1,0:T(8,128)(2,1)S(1)} %get-tuple-element.17.lo), channel_id=1, source_target_pairs={{0,8},{8,16},{16,24},{24,32},{32,40},{40,48},{48,56},{56,64},{64,7... | collective-permute-start | bytes 2359304 | tf_op jit(solution)/shard_map/ppermute | solution.py:41
  25.9 18.6 %copy-start.4 = (bf16[2,12,128,128]{3,2,1,0:T(8,128)(2,1)}, bf16[2,12,128,128]{3,2,1,0:T(8,128)(2,1)S(1)}, u32[]{:S(2)}) copy-start(bf16[2,12,128,128]{3,2,1,0:T(8,128)(2,1)S(1)} %collective-permute-done.2.down.rest_2_) | copy-start | bytes 2359300
  26.0 21.4 %collective-permute-start.5 = (bf16[2,12,128,128]{3,2,1,0:T(8,128)(2,1)S(1)}, bf16[2,12,128,128]{3,2,1,0:T(8,128)(2,1)S(1)}, u32[]{:S(2)}, u32[]{:S(2)}) collective-permute-start(bf16[2,12,128,128]{3,2,1,0:T(8,128)(2,1)S(1)} %collective-permute-done.2.down.rest_2_), channel_id=1, source_target_pairs={{0,1},{1,0},{2,3},{3,2},{4,5},{5,4},{6,7},{7,6},{8,9},{9,8},{10,11... | collective-permute-start | bytes 2359304 | tf_op jit(solution)/shard_map/ppermute | solution.py:34
  27.9 16.6 %copy-start.5 = (bf16[2,12,128,128]{3,2,1,0:T(8,128)(2,1)}, bf16[2,12,128,128]{3,2,1,0:T(8,128)(2,1)S(1)}, u32[]{:S(2)}) copy-start(bf16[2,12,128,128]{3,2,1,0:T(8,128)(2,1)S(1)} %collective-permute-done.4.b_x.rest_1_) | copy-start | bytes 2359300
  27.9 21.7 %collective-permute-start.8 = (bf16[2,12,128,128]{3,2,1,0:T(8,128)(2,1)S(1)}, bf16[2,12,128,128]{3,2,1,0:T(8,128)(2,1)S(1)}, u32[]{:S(2)}, u32[]{:S(2)}) collective-permute-start(bf16[2,12,128,128]{3,2,1,0:T(8,128)(2,1)S(1)} %collective-permute-done.4.b_x.rest_1_), channel_id=1, source_target_pairs={{0,6},{1,7},{2,0},{3,1},{4,2},{5,3},{6,4},{7,5},{8,14},{9,15},{10,... | collective-permute-start | bytes 2359304 | tf_op jit(solution)/shard_map/ppermute | solution.py:34
  29.8 14.7 %copy-start.6 = (bf16[2,12,128,128]{3,2,1,0:T(8,128)(2,1)}, bf16[2,12,128,128]{3,2,1,0:T(8,128)(2,1)S(1)}, u32[]{:S(2)}) copy-start(bf16[2,12,128,128]{3,2,1,0:T(8,128)(2,1)S(1)} %collective-permute-done.3.up.rest_3_) | copy-start | bytes 2359300
  29.9 26.5 %collective-permute-start.7 = (bf16[2,12,128,128]{3,2,1,0:T(8,128)(2,1)S(1)}, bf16[2,12,128,128]{3,2,1,0:T(8,128)(2,1)S(1)}, u32[]{:S(2)}, u32[]{:S(2)}) collective-permute-start(bf16[2,12,128,128]{3,2,1,0:T(8,128)(2,1)S(1)} %collective-permute-done.2.down.rest_2_), channel_id=1, source_target_pairs={{0,2},{1,3},{2,4},{3,5},{4,6},{5,7},{6,0},{7,1},{8,10},{9,11},{10,... | collective-permute-start | bytes 2359304 | tf_op jit(solution)/shard_map/ppermute | solution.py:34
  47.3 9.1 %copy-start = (bf16[2,12,128,128]{3,2,1,0:T(8,128)(2,1)}, bf16[2,12,128,128]{3,2,1,0:T(8,128)(2,1)S(1)}, u32[]{:S(2)}) copy-start(bf16[2,12,128,128]{3,2,1,0:T(8,128)(2,1)S(1)} %collective-permute-done.5.x_down.rest_5_) | copy-start | bytes 2359300
  48.2 18.6 %collective-permute-start.6 = (bf16[24,128,128]{2,1,0:T(8,128)(2,1)S(1)}, bf16[24,128,128]{2,1,0:T(8,128)(2,1)S(1)}, u32[]{:S(2)}, u32[]{:S(2)}) collective-permute-start(bf16[24,128,128]{2,1,0:T(8,128)(2,1)S(1)} %get-tuple-element.20), channel_id=1, source_target_pairs={{0,256},{504,248},{1,257},{505,249},{2,258},{506,250},{3,259},{507... | collective-permute-start | bytes 2359304 | tf_op jit(solution)/shard_map/ppermute | solution.py:46
  49.6 10.4 %copy-start.1 = (bf16[2,12,128,128]{3,2,1,0:T(8,128)(2,1)}, bf16[2,12,128,128]{3,2,1,0:T(8,128)(2,1)S(1)}, u32[]{:S(2)}) copy-start(bf16[2,12,128,128]{3,2,1,0:T(8,128)(2,1)S(1)} %collective-permute-done.8.x_up.rest_6_) | copy-start | bytes 2359300
  50.5 11.7 %collective-permute-start.10 = (bf16[12,128,128]{2,1,0:T(8,128)(2,1)S(1)}, bf16[12,128,128]{2,1,0:T(8,128)(2,1)S(1)}, u32[]{:S(2)}, u32[]{:S(2)}) collective-permute-start(bf16[12,128,128]{2,1,0:T(8,128)(2,1)S(1)} %shard_map.97), channel_id=1, source_target_pairs={{0,6},{1,7},{2,0},{3,1},{4,2},{5,3},{6,4},{7,5},{8,14},{9,15},{10,... | collective-permute-start | bytes 1179656 | tf_op jit(solution)/shard_map/ppermute | solution.py:34
  53.5 13.3 %collective-permute-start.9 = (bf16[12,128,128]{2,1,0:T(8,128)(2,1)S(1)}, bf16[12,128,128]{2,1,0:T(8,128)(2,1)S(1)}, u32[]{:S(2)}, u32[]{:S(2)}) collective-permute-start(bf16[12,128,128]{2,1,0:T(8,128)(2,1)S(1)} %get-tuple-element.22), channel_id=1, source_target_pairs={{0,2},{1,3},{2,4},{3,5},{4,6},{5,7},{6,0},{7,1},{8,10},{9,11},{10,... | collective-permute-start | bytes 1179656 | tf_op jit(solution)/shard_map/ppermute | solution.py:34
  56.4 3.7 %copy-start.7 = (bf16[2,12,128,128]{3,2,1,0:T(8,128)(2,1)}, bf16[2,12,128,128]{3,2,1,0:T(8,128)(2,1)S(1)}, u32[]{:S(2)}) copy-start(bf16[2,12,128,128]{3,2,1,0:T(8,128)(2,1)S(1)} %collective-permute-done.7.opp.rest_4_) | copy-start | bytes 2359300
  60.0 1.2 %copy-start.2 = (f32[24,128,128]{2,1,0:T(8,128)}, f32[24,128,128]{2,1,0:T(8,128)S(1)}, u32[]{:S(2)}) copy-start(f32[24,128,128]{2,1,0:T(8,128)S(1)} %shard_map.96.lt_in) | copy-start | bytes 4718596
